TPU v7x, 512 devices: a whole 4x4x16 slice. The times are simulated.
512 devices in a mesh: section: 16 (over y_lo, x, core), expert: 32 (over z, y_hi).
Axes of the slice: x: 4, y: 4 (y_hi: 2, y_lo: 2; y = y_hi * 2 + y_lo), z: 16, core: 2. Of those that a mesh axis runs over, the one named last changes fastest.
Arguments:
- tokens: bfloat16 [65536, 2048], P(('section', 'expert')), may hold values from -6 to 6
- upstream: bfloat16 [65536, 2048], P(('section', 'expert')), may hold values from -0.75 to 0.75
- expert_ids: int32 [65536, 1], P(('section', 'expert')), may hold values from 0 to 3; in each aligned block of 128 rows (0 to 127, 128 to 255, ...) at most 36 rows name the same one
- combine: bfloat16 [65536, 1], P(('section', 'expert')), may hold values from 0.049804688 to 0.3984375
- w_gate_up: bfloat16 [16, 32, 2048, 256], P('section', 'expert'), may hold values from -0.125 to 0.125
- w_down: bfloat16 [16, 32, 128, 2048], P('section', 'expert'), may hold values from -0.1875 to 0.1875
Outputs:
- input_grad: bfloat16 [65536, 2048], P(('section', 'expert'))
- combine_grad: bfloat16 [65536, 1], P(('section', 'expert'))
- grad_gate_up: bfloat16 [16, 32, 2048, 256], P('section', 'expert')
- grad_down: bfloat16 [16, 32, 128, 2048], P('section', 'expert')
Inputs may be any that keep to these rules, and one draw needn't show every extreme that they name: `expert_ids`: each row names one expert; within the rows of one device no expert is named more than 36 times, a bound that some block reaches.
All inputs are finite; a program needn't handle non-finite values.
Results may differ from a plain program's by a relative error of at most 0.0058.
Values may be sent and summed in bfloat16 or wider, within the bound.
No kernel may reach another device: no remote copies, remote signals or barrier semaphores. Data moves between devices by JAX's collectives and lax.ppermute only.
A program may use at most 128 MiB of HBM per device.

v0:
```python
import jax
import jax.numpy as jnp
from jax import lax
from jax.sharding import PartitionSpec as P

EXPERTS = 4


def shifted(shard, axis, by):
    peers = lax.axis_size(axis)
    return lax.ppermute(shard, axis, [(i, (i + by) % peers) for i in range(peers)])


def slot_within(ids, groups):
    tok, top = ids.shape
    onehot = (ids[:, :, None] == jnp.arange(groups, dtype=jnp.int32)[None, None, :]).astype(
        jnp.int32
    )
    flat = onehot.reshape(tok * top, groups)
    before = jnp.cumsum(flat, axis=0) - flat
    return jnp.sum(before * flat, axis=1).reshape(tok, top)


def gate_up_forward(xs, wgu, hidden):
    gu = jnp.dot(xs, wgu, preferred_element_type=jnp.float32)
    return (gu[:, :hidden], gu[:, hidden:])


def expert_rest(xs, gs, ps, gate, upper, wgu, wdown):
    sig = jax.nn.sigmoid(gate)
    act = gate * sig
    hid = act * upper
    raw = lax.dot_general(gs, wdown, (((1,), (1,)), ((), ())), preferred_element_type=jnp.float32)
    part_dp = jnp.sum(hid * raw, axis=1).astype(jnp.bfloat16)
    pcol = ps.astype(jnp.float32)[:, None]
    scaled = (pcol * gs.astype(jnp.float32)).astype(jnp.bfloat16)
    grad_down = lax.dot_general(
        hid.astype(jnp.bfloat16),
        scaled,
        (((0,), (0,)), ((), ())),
        preferred_element_type=jnp.float32,
    ).astype(jnp.bfloat16)
    dhid = pcol * raw
    dgate = dhid * upper * sig * (1.0 + gate * (1.0 - sig))
    dupper = dhid * act
    dgu = jnp.concatenate([dgate, dupper], axis=1).astype(jnp.bfloat16)
    grad_gu = lax.dot_general(
        xs, dgu, (((0,), (0,)), ((), ())), preferred_element_type=jnp.float32
    ).astype(jnp.bfloat16)
    part_dx = lax.dot_general(
        dgu, wgu, (((1,), (1,)), ((), ())), preferred_element_type=jnp.float32
    ).astype(jnp.bfloat16)
    return (part_dx, part_dp, grad_gu, grad_down)


def per_device(tokens, upstream, expert_ids, combine, w_gate_up, w_down):
    tok, width = tokens.shape
    top = expert_ids.shape[1]
    devices = lax.axis_size("expert")
    split = devices // EXPERTS
    capacity = tok * top * 9 // (8 * EXPERTS)
    rows = devices * capacity
    wgu = w_gate_up[0, 0]
    wdown = w_down[0, 0]
    hidden = wdown.shape[0]
    out_grad = shifted(upstream, "section", -1)
    slot = slot_within(expert_ids, EXPERTS)
    row_ids = jnp.arange(rows, dtype=jnp.int32)
    row_owner = row_ids // (split * capacity)
    row_slot = row_ids % capacity
    match = (expert_ids[None, :, :] == row_owner[:, None, None]) & (
        slot[None, :, :] == row_slot[:, None, None]
    )
    place = jnp.any(match, axis=2).astype(jnp.bfloat16)
    send_p = jnp.sum(
        jnp.where(match, combine.astype(jnp.float32)[None, :, :], 0.0), axis=(1, 2)
    ).astype(jnp.bfloat16)
    send_x = jnp.dot(place, tokens, preferred_element_type=jnp.float32).astype(jnp.bfloat16)
    send_g = jnp.dot(place, out_grad, preferred_element_type=jnp.float32).astype(jnp.bfloat16)
    recv_x, recv_g, recv_p = (
        lax.all_to_all(send_x, "expert", split_axis=0, concat_axis=0, tiled=True),
        lax.all_to_all(send_g, "expert", split_axis=0, concat_axis=0, tiled=True),
        lax.all_to_all(send_p, "expert", split_axis=0, concat_axis=0, tiled=True),
    )
    gate, upper = gate_up_forward(recv_x, wgu, hidden)
    part_dx, part_dp, grad_gu, grad_down = expert_rest(
        recv_x, recv_g, recv_p, gate, upper, wgu, wdown
    )
    back_x, back_p = (
        lax.all_to_all(part_dx, "expert", split_axis=0, concat_axis=0, tiled=True),
        lax.all_to_all(part_dp, "expert", split_axis=0, concat_axis=0, tiled=True),
    )
    moe = lax.dot_general(
        place, back_x, (((0,), (0,)), ((), ())), preferred_element_type=jnp.float32
    )
    picked = jnp.where(match, back_p.astype(jnp.float32)[:, None, None], 0.0)
    combine_grad = jnp.sum(picked, axis=0).astype(jnp.bfloat16)
    input_grad = (out_grad.astype(jnp.float32) + moe).astype(jnp.bfloat16)
    return (input_grad, combine_grad, grad_gu[None, None], grad_down[None, None])


def solution(mesh):
    in_specs = (
        P(("section", "expert"), None),
        P(("section", "expert"), None),
        P(("section", "expert"), None),
        P(("section", "expert"), None),
        P("section", "expert", None, None),
        P("section", "expert", None, None),
    )
    out_specs = (
        P(("section", "expert"), None),
        P(("section", "expert"), None),
        P("section", "expert", None, None),
        P("section", "expert", None, None),
    )
    return jax.shard_map(
        per_device, mesh=mesh, in_specs=in_specs, out_specs=out_specs, check_vma=False
    )
```

profile of v0, /device:TPU:6, one launch (start us, length us, event | category | flops | bytes accessed | tf_op | source)
XLA Modules:
  0.0 821.5 jit_solution(13868581937322455507)
XLA Ops:
  0.7 0.8 fusion.31
  1.5 0.2 reduce_window_sum.11
  1.7 0.8 select_reduce_fusion.2
  2.5 4.3 convolution_convert_fusion.1
  6.8 7.2 all_to_all.36
  14.0 18.4 %all-to-all-start.2 = ((bf16[32,36,2048]{2,1,0:T(8,128)(2,1)}), bf16[32,36,2048]{2,1,0:T(8,128)(2,1)}, u32[]{:S(2)}, u32[]{:S(2)}) async-start(bf16[32,36,2048]{2,1,0:T(8,128)(2,1)} %all_to_all.36), calls=%async_computation.2 | async-start | bytes 10485760 | tf_op jit(solution)/shard_map/all_to_all | solution.py:81
  32.4 1.9 collective-permute-start
  34.4 6.7 collective-permute-done
  41.0 3.3 convolution_convert_fusion.2
  44.3 7.2 all_to_all.33
  51.5 212.3 %all-to-all-done.2 = bf16[32,36,2048]{2,1,0:T(8,128)(2,1)} async-done(((bf16[32,36,2048]{2,1,0:T(8,128)(2,1)}), bf16[32,36,2048]{2,1,0:T(8,128)(2,1)}, u32[]{:S(2)}, u32[]{:S(2)}) %all-to-all-start.2) | async-done | bytes 4718624 | tf_op jit(solution)/shard_map/all_to_all | solution.py:81
  263.8 10.3 %all-to-all-start.1 = ((bf16[32,36,2048]{2,1,0:T(8,128)(2,1)}), bf16[32,36,2048]{2,1,0:T(8,128)(2,1)}, u32[]{:S(2)}, u32[]{:S(2)}) async-start(bf16[32,36,2048]{2,1,0:T(8,128)(2,1)} %all_to_all.33), calls=%async_computation.1 | async-start | bytes 10485760 | tf_op jit(solution)/shard_map/all_to_all | solution.py:82
  274.1 7.2 all_to_all.38
  281.4 3.9 fusion.6
  285.3 218.4 %all-to-all-done.1 = bf16[32,36,2048]{2,1,0:T(8,128)(2,1)} async-done(((bf16[32,36,2048]{2,1,0:T(8,128)(2,1)}), bf16[32,36,2048]{2,1,0:T(8,128)(2,1)}, u32[]{:S(2)}, u32[]{:S(2)}) %all-to-all-start.1) | async-done | bytes 4718624 | tf_op jit(solution)/shard_map/all_to_all | solution.py:82
  503.7 7.3 all_to_all.35
  511.0 4.8 multiply_reduce_fusion
  515.8 0.7 convert_element_type.130
  516.5 9.3 %all-to-all-start.4 = ((bf16[32,36,1]{1,2,0:T(2,128)(2,1)}), bf16[32,36,1]{1,2,0:T(2,128)(2,1)S(1)}, u32[]{:S(2)}, u32[]{:S(2)}) async-start(bf16[32,36,1]{1,2,0:T(2,128)(2,1)} %convert_element_type.130), calls=%async_computation.4 | async-start | bytes 32768 | tf_op jit(solution)/shard_map/all_to_all | solution.py:91
  525.9 14.6 %all-to-all-done.4 = bf16[32,36,1]{1,2,0:T(2,128)(2,1)S(1)} async-done(((bf16[32,36,1]{1,2,0:T(2,128)(2,1)}), bf16[32,36,1]{1,2,0:T(2,128)(2,1)S(1)}, u32[]{:S(2)}, u32[]{:S(2)}) %all-to-all-start.4) | async-done | bytes 2336 | tf_op jit(solution)/shard_map/all_to_all | solution.py:91
  540.6 1.1 select_reduce_fusion
  541.7 0.1 convert_element_type.129
  541.8 17.5 %all_to_all.48 = bf16[32,36,1]{1,2,0:T(2,128)(2,1)S(1)} all-to-all(bf16[32,36,1]{1,2,0:T(2,128)(2,1)S(1)} %convert_element_type.129), channel_id=1, replica_groups=mesh['section'=16,'expert'=32] {'expert'}, dimensions={0} | all-to-all | bytes 4608 | tf_op jit(solution)/shard_map/all_to_all | solution.py:83
  559.5 1.4 multiply_convert_fusion.7
  560.9 3.6 convolution_convert_fusion
  564.5 7.2 all_to_all.39
  571.7 5.0 all-to-all-start.3
  576.7 4.9 fusion.2
  581.6 4.3 fusion.4
  586.0 224.0 %all-to-all-done.3 = bf16[32,36,2048]{2,1,0:T(8,128)(2,1)} async-done(((bf16[32,36,2048]{2,1,0:T(8,128)(2,1)}), bf16[32,36,2048]{2,1,0:T(8,128)(2,1)}, u32[]{:S(2)}, u32[]{:S(2)}) %all-to-all-start.3) | async-done | bytes 4718624 | tf_op jit(solution)/shard_map/all_to_all | solution.py:90
  810.0 7.2 all_to_all.41
  817.2 4.2 add_convert_fusion
  (16 shorter events, 0.3 us)
Async XLA Ops:
  0.6 280.7 %copy-start = (bf16[1,1,2048,256]{3,2,1,0:T(8,128)(2,1)S(1)}, bf16[1,1,2048,256]{3,2,1,0:T(8,128)(2,1)}, u32[]{:S(2)}) copy-start(bf16[1,1,2048,256]{3,2,1,0:T(8,128)(2,1)} %param.10) | copy-start | bytes 3145732
  14.0 18.4 %copy-start.2 = (bf16[128,2048]{1,0:T(8,128)(2,1)S(1)}, bf16[128,2048]{1,0:T(8,128)(2,1)}, u32[]{:S(2)}) copy-start(bf16[128,2048]{1,0:T(8,128)(2,1)} %param.7) | copy-start | bytes 1572868
  14.0 27.0 %copy-start.1 = (s32[128,1]{0,1:T(1,128)S(1)}, s32[128,1]{0,1:T(1,128)}, u32[]{:S(2)}) copy-start(s32[128,1]{0,1:T(1,128)} %param.8) | copy-start | bytes 1540
  14.0 249.8 %all-to-all-start.2 = ((bf16[32,36,2048]{2,1,0:T(8,128)(2,1)}), bf16[32,36,2048]{2,1,0:T(8,128)(2,1)}, u32[]{:S(2)}, u32[]{:S(2)}) async-start(bf16[32,36,2048]{2,1,0:T(8,128)(2,1)} %all_to_all.36), calls=%async_computation.2 | async-start | bytes 10485760 | tf_op jit(solution)/shard_map/all_to_all | solution.py:81
  32.4 8.6 %collective-permute-start = (bf16[128,2048]{1,0:T(8,128)(2,1)S(1)}, bf16[128,2048]{1,0:T(8,128)(2,1)S(1)}, u32[]{:S(2)}, u32[]{:S(2)}) collective-permute-start(bf16[128,2048]{1,0:T(8,128)(2,1)S(1)} %copy-done.2), channel_id=1, source_target_pairs={{0,480},{32,0},{64,32},{96,64},{128,96},{160,128},{192,160},{224,1... | collective-permute-start | bytes 1572872 | tf_op jit(solution)/shard_map/ppermute | solution.py:11
  263.8 239.9 %all-to-all-start.1 = ((bf16[32,36,2048]{2,1,0:T(8,128)(2,1)}), bf16[32,36,2048]{2,1,0:T(8,128)(2,1)}, u32[]{:S(2)}, u32[]{:S(2)}) async-start(bf16[32,36,2048]{2,1,0:T(8,128)(2,1)} %all_to_all.33), calls=%async_computation.1 | async-start | bytes 10485760 | tf_op jit(solution)/shard_map/all_to_all | solution.py:82
  285.3 225.7 %copy-start.3 = (bf16[1,1,128,2048]{3,2,1,0:T(8,128)(2,1)S(1)}, bf16[1,1,128,2048]{3,2,1,0:T(8,128)(2,1)}, u32[]{:S(2)}) copy-start(bf16[1,1,128,2048]{3,2,1,0:T(8,128)(2,1)} %param.11) | copy-start | bytes 1572868
  511.0 14.9 %copy-start.4 = (bf16[128,1]{0,1:T(2,128)(2,1)S(1)}, bf16[128,1]{0,1:T(2,128)(2,1)}, u32[]{:S(2)}) copy-start(bf16[128,1]{0,1:T(2,128)(2,1)} %param.9) | copy-start | bytes 772
  516.5 24.0 %all-to-all-start.4 = ((bf16[32,36,1]{1,2,0:T(2,128)(2,1)}), bf16[32,36,1]{1,2,0:T(2,128)(2,1)S(1)}, u32[]{:S(2)}, u32[]{:S(2)}) async-start(bf16[32,36,1]{1,2,0:T(2,128)(2,1)} %convert_element_type.130), calls=%async_computation.4 | async-start | bytes 32768 | tf_op jit(solution)/shard_map/all_to_all | solution.py:91
  571.7 238.3 %all-to-all-start.3 = ((bf16[32,36,2048]{2,1,0:T(8,128)(2,1)}), bf16[32,36,2048]{2,1,0:T(8,128)(2,1)}, u32[]{:S(2)}, u32[]{:S(2)}) async-start(bf16[32,36,2048]{2,1,0:T(8,128)(2,1)} %all_to_all.39), calls=%async_computation.3 | async-start | bytes 10485760 | tf_op jit(solution)/shard_map/all_to_all | solution.py:90
where the time goes:
time: 823 us; the launch traced here: 821 us
  waiting for transfers between devices  676 us (82%)
  starting transfers between devices  44.9 us (5%)
  local copies, waits for them, and re-layouts  44.4 us (5%)
  matrix products  33.3 us (4%)
  blocking collectives  17.5 us (2%)
    all_to_all x1, waiting for transfers between devices, per_device(): lax.all_to_all(part_dx, 'expert', split_axis=0, concat_axis=0, tiled=True)  224 us
    all_to_all x1, waiting for transfers between devices, per_device(): lax.all_to_all(send_g, 'expert', split_axis=0, concat_axis=0, tiled=True)  218 us
    all_to_all x1, waiting for transfers between devices, per_device(): lax.all_to_all(send_x, 'expert', split_axis=0, concat_axis=0, tiled=True)  212 us
    all_to_all x1, starting transfers between devices, per_device(): lax.all_to_all(send_x, 'expert', split_axis=0, concat_axis=0, tiled=True)  18.4 us
    all_to_all x1, blocking collectives, per_device(): lax.all_to_all(send_p, 'expert', split_axis=0, concat_axis=0, tiled=True)  17.5 us
  transfers between devices with their start and end apart: 5, of which 5 were waited for; matrix products, arithmetic and copies ran while one was open for 2% of the time, Pallas kernels for 0%

commit v1 on v0

v1 whole, which is shorter than its diff:
```python
import jax
import jax.numpy as jnp
from jax import lax
from jax.sharding import Mesh, PartitionSpec as P

EXPERTS = 4
SECTION = ("ylo", "x", "core")
AXES = ("ylo", "x", "core", "zb", "zo", "yh")
LINE = 4
BF = jnp.bfloat16
F32 = jnp.float32


def dot(a, b, ca, cb):
    return lax.dot_general(a, b, (((ca,), (cb,)), ((), ())), preferred_element_type=F32)


def right(a, step):
    return lax.ppermute(a, "zo", [(i, i + 1) for i in range(step - 1, LINE - 1)])


def left(a, step):
    return lax.ppermute(a, "zo", [(i + 1, i) for i in range(LINE - step)])


def back_of_right(a, step):
    return lax.ppermute(a, "zo", [(i + 1, i) for i in range(step - 1, LINE - 1)])


def back_of_left(a, step):
    return lax.ppermute(a, "zo", [(i, i + 1) for i in range(LINE - step)])


def across(a):
    return lax.ppermute(a, "yh", [(0, 1), (1, 0)])


def plus(*terms):
    total = terms[0].astype(F32)
    for term in terms[1:]:
        total = total + term.astype(F32)
    return total.astype(BF)


def spread(unit, zo):
    r1, l1 = right(unit, 1), left(unit, 1)
    g1 = jnp.where(zo >= 1, r1, l1)
    r2, l2 = right(r1, 2), left(l1, 2)
    g2 = jnp.where(zo == 0, l2, jnp.where(zo == 3, r2, l1))
    r3, l3 = right(r2, 3), left(l2, 3)
    g3 = jnp.where(zo == 0, l3, jnp.where(zo == 1, l2, jnp.where(zo == 2, r2, r3)))
    own = [unit, g1, g2, g3]
    return own + [across(g) for g in own]


def gather_back(groups, zo):
    own, other = groups[:4], groups[4:]
    total = [None] * 4
    for k in (3, 2, 1, 0):
        total[k] = plus(own[k], across(other[k]))
    unit, g1, g2, g3 = total
    zero = jnp.zeros_like(unit)
    r3, l3 = back_of_right(g3, 3), back_of_left(g3, 3)
    c2r = jnp.where(zo == 3, g2, g3)
    c2l = jnp.where(zo == 0, g2, g3)
    r2 = back_of_right(plus(c2r, r3), 2)
    l2 = back_of_left(plus(c2l, l3), 2)
    r1 = back_of_right(plus(g1, r2), 1)
    c1l = jnp.where(zo == 0, g1, g2)
    l1 = back_of_left(plus(c1l, l2), 1)
    return plus(unit, r1, l1)


def per_device(tokens, upstream, expert_ids, combine, w_gate_up, w_down):
    tok, width = tokens.shape
    capacity = tok * 9 // (8 * EXPERTS)
    rows = EXPERTS * capacity
    wgu = w_gate_up[0, 0]
    wdown = w_down[0, 0]
    hidden = wdown.shape[0]
    zo = lax.axis_index("zo")
    sections = lax.axis_size(SECTION)
    out_grad = lax.ppermute(
        upstream, SECTION, [(i, (i - 1) % sections) for i in range(sections)]
    )

    ids = expert_ids[:, 0]
    onehot = (ids[:, None] == jnp.arange(EXPERTS, dtype=jnp.int32)[None, :]).astype(F32)
    earlier = (jnp.arange(tok)[:, None] > jnp.arange(tok)[None, :]).astype(F32)
    before = dot(earlier, onehot, 1, 0)
    slot = jnp.sum(before * onehot, axis=1).astype(jnp.int32)
    dest = ids * capacity + slot
    place = (jnp.arange(rows, dtype=jnp.int32)[:, None] == dest[None, :]).astype(BF)

    weight = combine.astype(F32)
    scaled = (weight * out_grad.astype(F32)).astype(BF)

    def to_block(a):
        sent = dot(place, a, 1, 0).astype(BF).reshape(EXPERTS, capacity, width)
        return lax.all_to_all(sent, "zb", 0, 0, tiled=True).reshape(rows, width)

    xs = spread(to_block(tokens), zo)
    gs = spread(to_block(scaled), zo)

    hs, dgus, dxs = [], [], []
    for x, g in zip(xs, gs):
        gu = dot(x, wgu, 1, 0)
        gate, upper = gu[:, :hidden], gu[:, hidden:]
        sig = jax.nn.sigmoid(gate)
        act = gate * sig
        hid = act * upper
        draw = dot(g, wdown, 1, 1)
        dp = jnp.sum(hid * draw, axis=1, keepdims=True)
        dgate = draw * upper * sig * (1.0 + gate * (1.0 - sig))
        dupper = draw * act
        dgu = jnp.concatenate([dgate, dupper], axis=1).astype(BF)
        dx = dot(dgu, wgu, 1, 1).astype(BF)
        dxs.append(
            jnp.concatenate([dx, jnp.broadcast_to(dp.astype(BF), (rows, 128))], axis=1)
        )
        hs.append(hid.astype(BF))
        dgus.append(dgu)

    back = gather_back(dxs, zo).reshape(EXPERTS, capacity, width + 128)
    back = lax.all_to_all(back, "zb", 0, 0, tiled=True).reshape(rows, width + 128)
    moe = dot(place, back, 0, 0)
    input_grad = (out_grad.astype(F32) + moe[:, :width]).astype(BF)
    combine_grad = (moe[:, width : width + 1] / weight).astype(BF)

    x_all = jnp.concatenate(xs, axis=0)
    g_all = jnp.concatenate(gs, axis=0)
    grad_gu = dot(x_all, jnp.concatenate(dgus, axis=0), 0, 0).astype(BF)
    grad_down = dot(jnp.concatenate(hs, axis=0), g_all, 0, 0).astype(BF)
    return (input_grad, combine_grad, grad_gu[None, None], grad_down[None, None])


def solution(mesh):
    fine = Mesh(mesh.devices.reshape(2, 4, 2, 4, 4, 2), AXES)
    row = P(AXES, None)
    weights = P(SECTION, ("zb", "zo", "yh"), None, None)
    return jax.shard_map(
        per_device,
        mesh=fine,
        in_specs=(row, row, row, row, weights, weights),
        out_specs=(row, row, weights, weights),
        check_vma=False,
    )
```

time: 823 us -> 351 us (0.43)
  the two profiles are of different devices: /device:TPU:6 before, /device:TPU:54 now
where the time goes in v1:
time: 351 us; the launch traced here: 349 us
  waiting for transfers between devices  167 us (48%)
  starting transfers between devices  127 us (36%)
  matrix products  21.7 us (6%)
  other arithmetic  16.8 us (5%)
  local copies, waits for them, and re-layouts  15.1 us (4%)
    ppermute x12, waiting for transfers between devices, across(): return lax.ppermute(a, 'yh', [(0, 1), (1, 0)])  52.3 us
    all_to_all x2, waiting for transfers between devices, to_block(): return lax.all_to_all(sent, 'zb', 0, 0, tiled=True).reshape(rows, width)  44.3 us
    ppermute x12, starting transfers between devices, across(): return lax.ppermute(a, 'yh', [(0, 1), (1, 0)])  38 us
    ppermute x3, waiting for transfers between devices, back_of_right(): lax.ppermute(a, 'zo', [(i + 1, i) for i in range(step - 1, LINE - 1)])  26.4 us
    ppermute x6, starting transfers between devices, left(): return lax.ppermute(a, 'zo', [(i + 1, i) for i in range(LINE - step)])  25.3 us
    dot_general x30, matrix products, dot(): lax.dot_general(a, b, (((ca,), (cb,)), ((), ())), preferred_element_type=...  21.7 us
    all_to_all x2, starting transfers between devices, to_block(): return lax.all_to_all(sent, 'zb', 0, 0, tiled=True).reshape(rows, width)  19.4 us
    ppermute x3, waiting for transfers between devices, back_of_left(): return lax.ppermute(a, 'zo', [(i, i + 1) for i in range(LINE - step)])  16.6 us
  transfers between devices with their start and end apart: 34, of which 16 were waited for; matrix products, arithmetic and copies ran while one was open for 13% of the time, Pallas kernels for 0%

profile of v1, /device:TPU:54, one launch (start us, length us, event | category | flops | bytes accessed | tf_op | source)
XLA Modules:
  0.0 349.4 jit_solution(15388102123457389122)
XLA Ops:
  4.6 14.2 %all-to-all-start.1 = ((bf16[4,36,2048]{2,1,0:T(8,128)(2,1)}), bf16[4,36,2048]{2,1,0:T(8,128)(2,1)S(1)}, u32[]{:S(2)}, u32[]{:S(2)}) async-start(bf16[4,36,2048]{2,1,0:T(8,128)(2,1)} %reshape.69), calls=%async_computation.1 | async-start | bytes 1310720 | tf_op jit(solution)/shard_map/all_to_all | solution.py:100
  21.4 5.9 %collective-permute-done = bf16[128,2048]{1,0:T(8,128)(2,1)S(1)} collective-permute-done((bf16[128,2048]{1,0:T(8,128)(2,1)S(1)}, bf16[128,2048]{1,0:T(8,128)(2,1)S(1)}, u32[]{:S(2)}, u32[]{:S(2)}) %collective-permute-start) | collective-permute-done | bytes 524320 | tf_op jit(solution)/shard_map/ppermute | solution.py:83
  28.7 25.3 %all-to-all-done.1 = bf16[4,36,2048]{2,1,0:T(8,128)(2,1)S(1)} async-done(((bf16[4,36,2048]{2,1,0:T(8,128)(2,1)}), bf16[4,36,2048]{2,1,0:T(8,128)(2,1)S(1)}, u32[]{:S(2)}, u32[]{:S(2)}) %all-to-all-start.1) | async-done | bytes 589856 | tf_op jit(solution)/shard_map/all_to_all | solution.py:100
  54.1 5.2 %all-to-all-start = ((bf16[4,36,2048]{2,1,0:T(8,128)(2,1)}), bf16[4,36,2048]{2,1,0:T(8,128)(2,1)S(1)}, u32[]{:S(2)}, u32[]{:S(2)}) async-start(bf16[4,36,2048]{2,1,0:T(8,128)(2,1)} %reshape.67), calls=%async_computation | async-start | bytes 1310720 | tf_op jit(solution)/shard_map/all_to_all | solution.py:100
  59.4 2.9 collective-permute-start.6
  62.3 3.7 %collective-permute-start.7 = (bf16[144,2048]{1,0:T(8,128)(2,1)S(1)}, bf16[144,2048]{1,0:T(8,128)(2,1)S(1)}, u32[]{:S(2)}, u32[]{:S(2)}) collective-permute-start(bf16[144,2048]{1,0:T(8,128)(2,1)S(1)} %reshape.70), channel_id=1, source_target_pairs={{2,0},{4,2},{6,4},{3,1},{5,3},{7,5},{10,8},{12,10},{14,12},{11,9},... | collective-permute-start | bytes 1769480 | tf_op jit(solution)/shard_map/ppermute | solution.py:23
  71.7 19.0 %all-to-all-done = bf16[4,36,2048]{2,1,0:T(8,128)(2,1)S(1)} async-done(((bf16[4,36,2048]{2,1,0:T(8,128)(2,1)}), bf16[4,36,2048]{2,1,0:T(8,128)(2,1)S(1)}, u32[]{:S(2)}, u32[]{:S(2)}) %all-to-all-start) | async-done | bytes 589856 | tf_op jit(solution)/shard_map/all_to_all | solution.py:100
  93.7 8.9 %collective-permute-start.5 = (bf16[144,2048]{1,0:T(8,128)(2,1)}, bf16[144,2048]{1,0:T(8,128)(2,1)S(1)}, u32[]{:S(2)}, u32[]{:S(2)}) collective-permute-start(bf16[144,2048]{1,0:T(8,128)(2,1)} %reshape.68), channel_id=1, source_target_pairs={{2,0},{4,2},{6,4},{3,1},{5,3},{7,5},{10,8},{12,10},{14,12},{11,9},... | collective-permute-start | bytes 1769480 | tf_op jit(solution)/shard_map/ppermute | solution.py:23
  110.0 5.1 %collective-permute-start.9 = (bf16[144,2048]{1,0:T(8,128)(2,1)S(1)}, bf16[144,2048]{1,0:T(8,128)(2,1)S(1)}, u32[]{:S(2)}, u32[]{:S(2)}) collective-permute-start(bf16[144,2048]{1,0:T(8,128)(2,1)S(1)} %get-tuple-element.23), channel_id=1, source_target_pairs={{0,1},{1,0},{2,3},{3,2},{4,5},{5,4},{6,7},{7,6},{8,9},{9,8},{10,11... | collective-permute-start | bytes 1769480 | tf_op jit(solution)/shard_map/ppermute | solution.py:35
  118.4 4.1 %collective-permute-start.14 = (bf16[144,2048]{1,0:T(8,128)(2,1)}, bf16[144,2048]{1,0:T(8,128)(2,1)S(1)}, u32[]{:S(2)}, u32[]{:S(2)}) collective-permute-start(bf16[144,2048]{1,0:T(8,128)(2,1)} %collective-permute-done.6), channel_id=1, source_target_pairs={{2,4},{4,6},{3,5},{5,7},{10,12},{12,14},{11,13},{13,15},{18,20},{2... | collective-permute-start | bytes 1769480 | tf_op jit(solution)/shard_map/ppermute | solution.py:19
  126.9 5.1 %collective-permute-start.3 = (bf16[144,2176]{1,0:T(8,128)(2,1)S(1)}, bf16[144,2176]{1,0:T(8,128)(2,1)S(1)}, u32[]{:S(2)}, u32[]{:S(2)}) collective-permute-start(bf16[144,2176]{1,0:T(8,128)(2,1)S(1)} %pad_maximum_fusion), channel_id=1, source_target_pairs={{0,1},{1,0},{2,3},{3,2},{4,5},{5,4},{6,7},{7,6},{8,9},{9,8},{10,11... | collective-permute-start | bytes 1880072 | tf_op jit(solution)/shard_map/ppermute | solution.py:35
  134.9 4.0 %collective-permute-start.12 = (bf16[144,2048]{1,0:T(8,128)(2,1)S(1)}, bf16[144,2048]{1,0:T(8,128)(2,1)S(1)}, u32[]{:S(2)}, u32[]{:S(2)}) collective-permute-start(bf16[144,2048]{1,0:T(8,128)(2,1)S(1)} %collective-permute-done.4), channel_id=1, source_target_pairs={{2,4},{4,6},{3,5},{5,7},{10,12},{12,14},{11,13},{13,15},{18,20},{2... | collective-permute-start | bytes 1769480 | tf_op jit(solution)/shard_map/ppermute | solution.py:19
  145.7 4.4 %collective-permute-start.20 = (bf16[144,2048]{1,0:T(8,128)(2,1)S(1)}, bf16[144,2048]{1,0:T(8,128)(2,1)S(1)}, u32[]{:S(2)}, u32[]{:S(2)}) collective-permute-start(bf16[144,2048]{1,0:T(8,128)(2,1)S(1)} %collective-permute-done.13), channel_id=1, source_target_pairs={{2,0},{3,1},{10,8},{11,9},{18,16},{19,17},{26,24},{27,25},{34,32},... | collective-permute-start | bytes 1769480 | tf_op jit(solution)/shard_map/ppermute | solution.py:23
  155.9 5.8 %collective-permute-done.20 = bf16[144,2048]{1,0:T(8,128)(2,1)S(1)} collective-permute-done((bf16[144,2048]{1,0:T(8,128)(2,1)S(1)}, bf16[144,2048]{1,0:T(8,128)(2,1)S(1)}, u32[]{:S(2)}, u32[]{:S(2)}) %collective-permute-start.20) | collective-permute-done | bytes 589856 | tf_op jit(solution)/shard_map/ppermute | solution.py:23
  161.7 4.4 %collective-permute-start.18 = (bf16[144,2048]{1,0:T(8,128)(2,1)S(1)}, bf16[144,2048]{1,0:T(8,128)(2,1)S(1)}, u32[]{:S(2)}, u32[]{:S(2)}) collective-permute-start(bf16[144,2048]{1,0:T(8,128)(2,1)S(1)} %collective-permute-done.11), channel_id=1, source_target_pairs={{2,0},{3,1},{10,8},{11,9},{18,16},{19,17},{26,24},{27,25},{34,32},... | collective-permute-start | bytes 1769480 | tf_op jit(solution)/shard_map/ppermute | solution.py:23
  169.1 7.6 %collective-permute-done.16 = bf16[144,2048]{1,0:T(8,128)(2,1)S(1)} collective-permute-done((bf16[144,2048]{1,0:T(8,128)(2,1)S(1)}, bf16[144,2048]{1,0:T(8,128)(2,1)S(1)}, u32[]{:S(2)}, u32[]{:S(2)}) %collective-permute-start.16) | collective-permute-done | bytes 589856 | tf_op jit(solution)/shard_map/ppermute | solution.py:35
  179.7 5.3 %collective-permute-start.23 = (bf16[144,2048]{1,0:T(8,128)(2,1)S(1)}, bf16[144,2048]{1,0:T(8,128)(2,1)S(1)}, u32[]{:S(2)}, u32[]{:S(2)}) collective-permute-start(bf16[144,2048]{1,0:T(8,128)(2,1)S(1)} %get-tuple-element.19), channel_id=1, source_target_pairs={{0,1},{1,0},{2,3},{3,2},{4,5},{5,4},{6,7},{7,6},{8,9},{9,8},{10,11... | collective-permute-start | bytes 1769480 | tf_op jit(solution)/shard_map/ppermute | solution.py:35
  190.3 24.7 %collective-permute-done.23 = bf16[144,2048]{1,0:T(8,128)(2,1)S(1)} collective-permute-done((bf16[144,2048]{1,0:T(8,128)(2,1)S(1)}, bf16[144,2048]{1,0:T(8,128)(2,1)S(1)}, u32[]{:S(2)}, u32[]{:S(2)}) %collective-permute-start.23) | collective-permute-done | bytes 589856 | tf_op jit(solution)/shard_map/ppermute | solution.py:35
  215.3 6.0 %collective-permute-done.22 = bf16[144,2048]{1,0:T(8,128)(2,1)S(1)} collective-permute-done((bf16[144,2048]{1,0:T(8,128)(2,1)S(1)}, bf16[144,2048]{1,0:T(8,128)(2,1)S(1)}, u32[]{:S(2)}, u32[]{:S(2)}) %collective-permute-start.22) | collective-permute-done | bytes 589856 | tf_op jit(solution)/shard_map/ppermute | solution.py:35
  222.5 2.7 collective-permute-start.24
  225.3 4.7 %collective-permute-start.17 = (bf16[144,2176]{1,0:T(8,128)(2,1)S(1)}, bf16[144,2176]{1,0:T(8,128)(2,1)S(1)}, u32[]{:S(2)}, u32[]{:S(2)}) collective-permute-start(bf16[144,2176]{1,0:T(8,128)(2,1)S(1)} %pad_maximum_fusion.2), channel_id=1, source_target_pairs={{0,1},{1,0},{2,3},{3,2},{4,5},{5,4},{6,7},{7,6},{8,9},{9,8},{10,11... | collective-permute-start | bytes 1880072 | tf_op jit(solution)/shard_map/ppermute | solution.py:35
  230.9 11.0 %collective-permute-done.24 = bf16[144,2176]{1,0:T(8,128)(2,1)S(1)} collective-permute-done((bf16[144,2176]{1,0:T(8,128)(2,1)S(1)}, bf16[144,2176]{1,0:T(8,128)(2,1)S(1)}, u32[]{:S(2)}, u32[]{:S(2)}) %collective-permute-start.24) | collective-permute-done | bytes 626720 | tf_op jit(solution)/shard_map/ppermute | solution.py:35
  248.7 12.2 %collective-permute-done.28 = bf16[144,2176]{1,0:T(8,128)(2,1)S(1)} collective-permute-done((bf16[144,2176]{1,0:T(8,128)(2,1)S(1)}, bf16[144,2176]{1,0:T(8,128)(2,1)S(1)}, u32[]{:S(2)}, u32[]{:S(2)}) %collective-permute-start.28) | collective-permute-done | bytes 626720 | tf_op jit(solution)/shard_map/ppermute | solution.py:31
  262.7 4.6 %collective-permute-start.29 = (bf16[144,2176]{1,0:T(8,128)(2,1)S(1)}, bf16[144,2176]{1,0:T(8,128)(2,1)S(1)}, u32[]{:S(2)}, u32[]{:S(2)}) collective-permute-start(bf16[144,2176]{1,0:T(8,128)(2,1)S(1)} %get-tuple-element.25), channel_id=1, source_target_pairs={{0,2},{2,4},{1,3},{3,5},{8,10},{10,12},{9,11},{11,13},{16,18},{18,... | collective-permute-start | bytes 1880072 | tf_op jit(solution)/shard_map/ppermute | solution.py:31
  268.8 11.3 %collective-permute-done.26 = bf16[144,2176]{1,0:T(8,128)(2,1)S(1)} collective-permute-done((bf16[144,2176]{1,0:T(8,128)(2,1)S(1)}, bf16[144,2176]{1,0:T(8,128)(2,1)S(1)}, u32[]{:S(2)}, u32[]{:S(2)}) %collective-permute-start.26) | collective-permute-done | bytes 626720 | tf_op jit(solution)/shard_map/ppermute | solution.py:27
  282.6 4.0 %collective-permute-start.27 = (bf16[144,2176]{1,0:T(8,128)(2,1)S(1)}, bf16[144,2176]{1,0:T(8,128)(2,1)S(1)}, u32[]{:S(2)}, u32[]{:S(2)}) collective-permute-start(bf16[144,2176]{1,0:T(8,128)(2,1)S(1)} %get-tuple-element.26), channel_id=1, source_target_pairs={{2,0},{4,2},{6,4},{3,1},{5,3},{7,5},{10,8},{12,10},{14,12},{11,9},... | collective-permute-start | bytes 1880072 | tf_op jit(solution)/shard_map/ppermute | solution.py:27
  288.5 4.4 %collective-permute-done.30 = bf16[144,2176]{1,0:T(8,128)(2,1)S(1)} collective-permute-done((bf16[144,2176]{1,0:T(8,128)(2,1)S(1)}, bf16[144,2176]{1,0:T(8,128)(2,1)S(1)}, u32[]{:S(2)}, u32[]{:S(2)}) %collective-permute-start.30) | collective-permute-done | bytes 626720 | tf_op jit(solution)/shard_map/ppermute | solution.py:31
  292.9 15.2 %collective-permute-done.27 = bf16[144,2176]{1,0:T(8,128)(2,1)S(1)} collective-permute-done((bf16[144,2176]{1,0:T(8,128)(2,1)S(1)}, bf16[144,2176]{1,0:T(8,128)(2,1)S(1)}, u32[]{:S(2)}, u32[]{:S(2)}) %collective-permute-start.27) | collective-permute-done | bytes 626720 | tf_op jit(solution)/shard_map/ppermute | solution.py:27
  309.5 14.7 %all-to-all-start.2 = ((bf16[4,36,2176]{2,1,0:T(8,128)(2,1)}), bf16[4,36,2176]{2,1,0:T(8,128)(2,1)S(1)}, u32[]{:S(2)}, u32[]{:S(2)}) async-start(bf16[4,36,2176]{2,1,0:T(8,128)(2,1)} %reshape.71), calls=%async_computation.2 | async-start | bytes 1392640 | tf_op jit(solution)/shard_map/all_to_all | solution.py:125
  326.9 4.2 %fusion.1 = bf16[1,1,128,2048]{3,2,1,0:T(8,128)(2,1)} fusion(bf16[1152,128]{1,0:T(8,128)(2,1)S(1)} %constant_dynamic-update-slice_fusion.16, bf16[1152,2048]{1,0:T(8,128)(2,1)} %constant_dynamic-update-slice_fusion.24), kind=kOutput, calls=%fused_computation.13 | convolution fusion | flops 604241920 | bytes 5537792 | tf_op jit(solution)/shard_map/dot_general | solution.py:15
  331.1 2.6 fusion
  333.7 13.6 %all-to-all-done.2 = bf16[4,36,2176]{2,1,0:T(8,128)(2,1)S(1)} async-done(((bf16[4,36,2176]{2,1,0:T(8,128)(2,1)}), bf16[4,36,2176]{2,1,0:T(8,128)(2,1)S(1)}, u32[]{:S(2)}, u32[]{:S(2)}) %all-to-all-start.2) | async-done | bytes 626720 | tf_op jit(solution)/shard_map/all_to_all | solution.py:125
  (168 shorter events, 81.5 us)
Async XLA Ops:
  4.6 49.5 %all-to-all-start.1 = ((bf16[4,36,2048]{2,1,0:T(8,128)(2,1)}), bf16[4,36,2048]{2,1,0:T(8,128)(2,1)S(1)}, u32[]{:S(2)}, u32[]{:S(2)}) async-start(bf16[4,36,2048]{2,1,0:T(8,128)(2,1)} %reshape.69), calls=%async_computation.1 | async-start | bytes 1310720 | tf_op jit(solution)/shard_map/all_to_all | solution.py:100
  54.1 36.6 %all-to-all-start = ((bf16[4,36,2048]{2,1,0:T(8,128)(2,1)}), bf16[4,36,2048]{2,1,0:T(8,128)(2,1)S(1)}, u32[]{:S(2)}, u32[]{:S(2)}) async-start(bf16[4,36,2048]{2,1,0:T(8,128)(2,1)} %reshape.67), calls=%async_computation | async-start | bytes 1310720 | tf_op jit(solution)/shard_map/all_to_all | solution.py:100
  59.4 46.3 %collective-permute-start.6 = (bf16[144,2048]{1,0:T(8,128)(2,1)S(1)}, bf16[144,2048]{1,0:T(8,128)(2,1)}, u32[]{:S(2)}, u32[]{:S(2)}) collective-permute-start(bf16[144,2048]{1,0:T(8,128)(2,1)S(1)} %reshape.70), channel_id=1, source_target_pairs={{0,2},{2,4},{4,6},{1,3},{3,5},{5,7},{8,10},{10,12},{12,14},{9,11},... | collective-permute-start | bytes 1769480 | tf_op jit(solution)/shard_map/ppermute | solution.py:19
  62.3 45.7 %collective-permute-start.7 = (bf16[144,2048]{1,0:T(8,128)(2,1)S(1)}, bf16[144,2048]{1,0:T(8,128)(2,1)S(1)}, u32[]{:S(2)}, u32[]{:S(2)}) collective-permute-start(bf16[144,2048]{1,0:T(8,128)(2,1)S(1)} %reshape.70), channel_id=1, source_target_pairs={{2,0},{4,2},{6,4},{3,1},{5,3},{7,5},{10,8},{12,10},{14,12},{11,9},... | collective-permute-start | bytes 1769480 | tf_op jit(solution)/shard_map/ppermute | solution.py:23
  66.0 50.1 %collective-permute-start.2 = (bf16[144,2048]{1,0:T(8,128)(2,1)S(1)}, bf16[144,2048]{1,0:T(8,128)(2,1)S(1)}, u32[]{:S(2)}, u32[]{:S(2)}) collective-permute-start(bf16[144,2048]{1,0:T(8,128)(2,1)S(1)} %reshape.70), channel_id=1, source_target_pairs={{0,1},{1,0},{2,3},{3,2},{4,5},{5,4},{6,7},{7,6},{8,9},{9,8},{10,11... | collective-permute-start | bytes 1769480 | tf_op jit(solution)/shard_map/ppermute | solution.py:35
  91.6 26.7 %collective-permute-start.4 = (bf16[144,2048]{1,0:T(8,128)(2,1)}, bf16[144,2048]{1,0:T(8,128)(2,1)S(1)}, u32[]{:S(2)}, u32[]{:S(2)}) collective-permute-start(bf16[144,2048]{1,0:T(8,128)(2,1)} %reshape.68), channel_id=1, source_target_pairs={{0,2},{2,4},{4,6},{1,3},{3,5},{5,7},{8,10},{10,12},{12,14},{9,11},... | collective-permute-start | bytes 1769480 | tf_op jit(solution)/shard_map/ppermute | solution.py:19
  93.7 28.8 %collective-permute-start.5 = (bf16[144,2048]{1,0:T(8,128)(2,1)}, bf16[144,2048]{1,0:T(8,128)(2,1)S(1)}, u32[]{:S(2)}, u32[]{:S(2)}) collective-permute-start(bf16[144,2048]{1,0:T(8,128)(2,1)} %reshape.68), channel_id=1, source_target_pairs={{2,0},{4,2},{6,4},{3,1},{5,3},{7,5},{10,8},{12,10},{14,12},{11,9},... | collective-permute-start | bytes 1769480 | tf_op jit(solution)/shard_map/ppermute | solution.py:23
  105.7 20.1 %collective-permute-start.1 = (bf16[144,2048]{1,0:T(8,128)(2,1)S(1)}, bf16[144,2048]{1,0:T(8,128)(2,1)S(1)}, u32[]{:S(2)}, u32[]{:S(2)}) collective-permute-start(bf16[144,2048]{1,0:T(8,128)(2,1)S(1)} %copy-done.1), channel_id=1, source_target_pairs={{0,1},{1,0},{2,3},{3,2},{4,5},{5,4},{6,7},{7,6},{8,9},{9,8},{10,11... | collective-permute-start | bytes 1769480 | tf_op jit(solution)/shard_map/ppermute | solution.py:35
  110.0 31.0 %collective-permute-start.9 = (bf16[144,2048]{1,0:T(8,128)(2,1)S(1)}, bf16[144,2048]{1,0:T(8,128)(2,1)S(1)}, u32[]{:S(2)}, u32[]{:S(2)}) collective-permute-start(bf16[144,2048]{1,0:T(8,128)(2,1)S(1)} %get-tuple-element.23), channel_id=1, source_target_pairs={{0,1},{1,0},{2,3},{3,2},{4,5},{5,4},{6,7},{7,6},{8,9},{9,8},{10,11... | collective-permute-start | bytes 1769480 | tf_op jit(solution)/shard_map/ppermute | solution.py:35
  116.1 16.8 %collective-permute-start.13 = (bf16[144,2048]{1,0:T(8,128)(2,1)S(1)}, bf16[144,2048]{1,0:T(8,128)(2,1)S(1)}, u32[]{:S(2)}, u32[]{:S(2)}) collective-permute-start(bf16[144,2048]{1,0:T(8,128)(2,1)S(1)} %collective-permute-done.7), channel_id=1, source_target_pairs={{2,0},{4,2},{3,1},{5,3},{10,8},{12,10},{11,9},{13,11},{18,16},{20,... | collective-permute-start | bytes 1769480 | tf_op jit(solution)/shard_map/ppermute | solution.py:23
  118.4 16.5 %collective-permute-start.14 = (bf16[144,2048]{1,0:T(8,128)(2,1)}, bf16[144,2048]{1,0:T(8,128)(2,1)S(1)}, u32[]{:S(2)}, u32[]{:S(2)}) collective-permute-start(bf16[144,2048]{1,0:T(8,128)(2,1)} %collective-permute-done.6), channel_id=1, source_target_pairs={{2,4},{4,6},{3,5},{5,7},{10,12},{12,14},{11,13},{13,15},{18,20},{2... | collective-permute-start | bytes 1769480 | tf_op jit(solution)/shard_map/ppermute | solution.py:19
  123.5 29.4 %collective-permute-start.8 = (bf16[144,2048]{1,0:T(8,128)(2,1)S(1)}, bf16[144,2048]{1,0:T(8,128)(2,1)S(1)}, u32[]{:S(2)}, u32[]{:S(2)}) collective-permute-start(bf16[144,2048]{1,0:T(8,128)(2,1)S(1)} %get-tuple-element.17), channel_id=1, source_target_pairs={{0,1},{1,0},{2,3},{3,2},{4,5},{5,4},{6,7},{7,6},{8,9},{9,8},{10,11... | collective-permute-start | bytes 1769480 | tf_op jit(solution)/shard_map/ppermute | solution.py:35
  126.9 161.6 %collective-permute-start.3 = (bf16[144,2176]{1,0:T(8,128)(2,1)S(1)}, bf16[144,2176]{1,0:T(8,128)(2,1)S(1)}, u32[]{:S(2)}, u32[]{:S(2)}) collective-permute-start(bf16[144,2176]{1,0:T(8,128)(2,1)S(1)} %pad_maximum_fusion), channel_id=1, source_target_pairs={{0,1},{1,0},{2,3},{3,2},{4,5},{5,4},{6,7},{7,6},{8,9},{9,8},{10,11... | collective-permute-start | bytes 1880072 | tf_op jit(solution)/shard_map/ppermute | solution.py:35
  132.9 12.8 %collective-permute-start.11 = (bf16[144,2048]{1,0:T(8,128)(2,1)S(1)}, bf16[144,2048]{1,0:T(8,128)(2,1)S(1)}, u32[]{:S(2)}, u32[]{:S(2)}) collective-permute-start(bf16[144,2048]{1,0:T(8,128)(2,1)S(1)} %collective-permute-done.5), channel_id=1, source_target_pairs={{2,0},{4,2},{3,1},{5,3},{10,8},{12,10},{11,9},{13,11},{18,16},{20,... | collective-permute-start | bytes 1769480 | tf_op jit(solution)/shard_map/ppermute | solution.py:23
  134.9 15.3 %collective-permute-start.12 = (bf16[144,2048]{1,0:T(8,128)(2,1)S(1)}, bf16[144,2048]{1,0:T(8,128)(2,1)S(1)}, u32[]{:S(2)}, u32[]{:S(2)}) collective-permute-start(bf16[144,2048]{1,0:T(8,128)(2,1)S(1)} %collective-permute-done.4), channel_id=1, source_target_pairs={{2,4},{4,6},{3,5},{5,7},{10,12},{12,14},{11,13},{13,15},{18,20},{2... | collective-permute-start | bytes 1769480 | tf_op jit(solution)/shard_map/ppermute | solution.py:19
  141.0 35.7 %collective-permute-start.16 = (bf16[144,2048]{1,0:T(8,128)(2,1)S(1)}, bf16[144,2048]{1,0:T(8,128)(2,1)S(1)}, u32[]{:S(2)}, u32[]{:S(2)}) collective-permute-start(bf16[144,2048]{1,0:T(8,128)(2,1)S(1)} %get-tuple-element.21), channel_id=1, source_target_pairs={{0,1},{1,0},{2,3},{3,2},{4,5},{5,4},{6,7},{7,6},{8,9},{9,8},{10,11... | collective-permute-start | bytes 1769480 | tf_op jit(solution)/shard_map/ppermute | solution.py:35
  145.7 16.0 %collective-permute-start.20 = (bf16[144,2048]{1,0:T(8,128)(2,1)S(1)}, bf16[144,2048]{1,0:T(8,128)(2,1)S(1)}, u32[]{:S(2)}, u32[]{:S(2)}) collective-permute-start(bf16[144,2048]{1,0:T(8,128)(2,1)S(1)} %collective-permute-done.13), channel_id=1, source_target_pairs={{2,0},{3,1},{10,8},{11,9},{18,16},{19,17},{26,24},{27,25},{34,32},... | collective-permute-start | bytes 1769480 | tf_op jit(solution)/shard_map/ppermute | solution.py:23
  150.1 16.0 %collective-permute-start.21 = (bf16[144,2048]{1,0:T(8,128)(2,1)S(1)}, bf16[144,2048]{1,0:T(8,128)(2,1)S(1)}, u32[]{:S(2)}, u32[]{:S(2)}) collective-permute-start(bf16[144,2048]{1,0:T(8,128)(2,1)S(1)} %collective-permute-done.14), channel_id=1, source_target_pairs={{4,6},{5,7},{12,14},{13,15},{20,22},{21,23},{28,30},{29,31},{36,38... | collective-permute-start | bytes 1769480 | tf_op jit(solution)/shard_map/ppermute | solution.py:19
  152.9 36.4 %collective-permute-start.15 = (bf16[144,2048]{1,0:T(8,128)(2,1)S(1)}, bf16[144,2048]{1,0:T(8,128)(2,1)S(1)}, u32[]{:S(2)}, u32[]{:S(2)}) collective-permute-start(bf16[144,2048]{1,0:T(8,128)(2,1)S(1)} %get-tuple-element.15), channel_id=1, source_target_pairs={{0,1},{1,0},{2,3},{3,2},{4,5},{5,4},{6,7},{7,6},{8,9},{9,8},{10,11... | collective-permute-start | bytes 1769480 | tf_op jit(solution)/shard_map/ppermute | solution.py:35
  161.7 18.0 %collective-permute-start.18 = (bf16[144,2048]{1,0:T(8,128)(2,1)S(1)}, bf16[144,2048]{1,0:T(8,128)(2,1)S(1)}, u32[]{:S(2)}, u32[]{:S(2)}) collective-permute-start(bf16[144,2048]{1,0:T(8,128)(2,1)S(1)} %collective-permute-done.11), channel_id=1, source_target_pairs={{2,0},{3,1},{10,8},{11,9},{18,16},{19,17},{26,24},{27,25},{34,32},... | collective-permute-start | bytes 1769480 | tf_op jit(solution)/shard_map/ppermute | solution.py:23
  166.1 18.9 %collective-permute-start.19 = (bf16[144,2048]{1,0:T(8,128)(2,1)S(1)}, bf16[144,2048]{1,0:T(8,128)(2,1)S(1)}, u32[]{:S(2)}, u32[]{:S(2)}) collective-permute-start(bf16[144,2048]{1,0:T(8,128)(2,1)S(1)} %collective-permute-done.12), channel_id=1, source_target_pairs={{4,6},{5,7},{12,14},{13,15},{20,22},{21,23},{28,30},{29,31},{36,38... | collective-permute-start | bytes 1769480 | tf_op jit(solution)/shard_map/ppermute | solution.py:19
  176.7 92.1 %collective-permute-start.10 = (bf16[144,2176]{1,0:T(8,128)(2,1)S(1)}, bf16[144,2176]{1,0:T(8,128)(2,1)S(1)}, u32[]{:S(2)}, u32[]{:S(2)}) collective-permute-start(bf16[144,2176]{1,0:T(8,128)(2,1)S(1)} %pad_maximum_fusion.1), channel_id=1, source_target_pairs={{0,1},{1,0},{2,3},{3,2},{4,5},{5,4},{6,7},{7,6},{8,9},{9,8},{10,11... | collective-permute-start | bytes 1880072 | tf_op jit(solution)/shard_map/ppermute | solution.py:35
  179.7 35.2 %collective-permute-start.23 = (bf16[144,2048]{1,0:T(8,128)(2,1)S(1)}, bf16[144,2048]{1,0:T(8,128)(2,1)S(1)}, u32[]{:S(2)}, u32[]{:S(2)}) collective-permute-start(bf16[144,2048]{1,0:T(8,128)(2,1)S(1)} %get-tuple-element.19), channel_id=1, source_target_pairs={{0,1},{1,0},{2,3},{3,2},{4,5},{5,4},{6,7},{7,6},{8,9},{9,8},{10,11... | collective-permute-start | bytes 1769480 | tf_op jit(solution)/shard_map/ppermute | solution.py:35
  186.3 35.0 %collective-permute-start.22 = (bf16[144,2048]{1,0:T(8,128)(2,1)S(1)}, bf16[144,2048]{1,0:T(8,128)(2,1)S(1)}, u32[]{:S(2)}, u32[]{:S(2)}) collective-permute-start(bf16[144,2048]{1,0:T(8,128)(2,1)S(1)} %get-tuple-element.13), channel_id=1, source_target_pairs={{0,1},{1,0},{2,3},{3,2},{4,5},{5,4},{6,7},{7,6},{8,9},{9,8},{10,11... | collective-permute-start | bytes 1769480 | tf_op jit(solution)/shard_map/ppermute | solution.py:35
  222.5 19.5 %collective-permute-start.24 = (bf16[144,2176]{1,0:T(8,128)(2,1)S(1)}, bf16[144,2176]{1,0:T(8,128)(2,1)S(1)}, u32[]{:S(2)}, u32[]{:S(2)}) collective-permute-start(bf16[144,2176]{1,0:T(8,128)(2,1)S(1)} %pad_maximum_fusion.3), channel_id=1, source_target_pairs={{0,1},{1,0},{2,3},{3,2},{4,5},{5,4},{6,7},{7,6},{8,9},{9,8},{10,11... | collective-permute-start | bytes 1880072 | tf_op jit(solution)/shard_map/ppermute | solution.py:35
  225.3 23.4 %collective-permute-start.17 = (bf16[144,2176]{1,0:T(8,128)(2,1)S(1)}, bf16[144,2176]{1,0:T(8,128)(2,1)S(1)}, u32[]{:S(2)}, u32[]{:S(2)}) collective-permute-start(bf16[144,2176]{1,0:T(8,128)(2,1)S(1)} %pad_maximum_fusion.2), channel_id=1, source_target_pairs={{0,1},{1,0},{2,3},{3,2},{4,5},{5,4},{6,7},{7,6},{8,9},{9,8},{10,11... | collective-permute-start | bytes 1880072 | tf_op jit(solution)/shard_map/ppermute | solution.py:35
  242.9 17.9 %collective-permute-start.28 = (bf16[144,2176]{1,0:T(8,128)(2,1)S(1)}, bf16[144,2176]{1,0:T(8,128)(2,1)S(1)}, u32[]{:S(2)}, u32[]{:S(2)}) collective-permute-start(bf16[144,2176]{1,0:T(8,128)(2,1)S(1)} %add_convert_fusion.5), channel_id=1, source_target_pairs={{0,2},{1,3},{8,10},{9,11},{16,18},{17,19},{24,26},{25,27},{32,34},... | collective-permute-start | bytes 1880072 | tf_op jit(solution)/shard_map/ppermute | solution.py:31
  261.4 18.7 %collective-permute-start.26 = (bf16[144,2176]{1,0:T(8,128)(2,1)S(1)}, bf16[144,2176]{1,0:T(8,128)(2,1)S(1)}, u32[]{:S(2)}, u32[]{:S(2)}) collective-permute-start(bf16[144,2176]{1,0:T(8,128)(2,1)S(1)} %get-tuple-element.24), channel_id=1, source_target_pairs={{4,2},{6,4},{5,3},{7,5},{12,10},{14,12},{13,11},{15,13},{20,18},{2... | collective-permute-start | bytes 1880072 | tf_op jit(solution)/shard_map/ppermute | solution.py:27
  262.7 17.4 %collective-permute-start.29 = (bf16[144,2176]{1,0:T(8,128)(2,1)S(1)}, bf16[144,2176]{1,0:T(8,128)(2,1)S(1)}, u32[]{:S(2)}, u32[]{:S(2)}) collective-permute-start(bf16[144,2176]{1,0:T(8,128)(2,1)S(1)} %get-tuple-element.25), channel_id=1, source_target_pairs={{0,2},{2,4},{1,3},{3,5},{8,10},{10,12},{9,11},{11,13},{16,18},{18,... | collective-permute-start | bytes 1880072 | tf_op jit(solution)/shard_map/ppermute | solution.py:31
  280.7 12.2 %collective-permute-start.30 = (bf16[144,2176]{1,0:T(8,128)(2,1)S(1)}, bf16[144,2176]{1,0:T(8,128)(2,1)S(1)}, u32[]{:S(2)}, u32[]{:S(2)}) collective-permute-start(bf16[144,2176]{1,0:T(8,128)(2,1)S(1)} %get-tuple-element.27), channel_id=1, source_target_pairs={{0,2},{2,4},{4,6},{1,3},{3,5},{5,7},{8,10},{10,12},{12,14},{9,11},... | collective-permute-start | bytes 1880072 | tf_op jit(solution)/shard_map/ppermute | solution.py:31
  282.6 25.4 %collective-permute-start.27 = (bf16[144,2176]{1,0:T(8,128)(2,1)S(1)}, bf16[144,2176]{1,0:T(8,128)(2,1)S(1)}, u32[]{:S(2)}, u32[]{:S(2)}) collective-permute-start(bf16[144,2176]{1,0:T(8,128)(2,1)S(1)} %get-tuple-element.26), channel_id=1, source_target_pairs={{2,0},{4,2},{6,4},{3,1},{5,3},{7,5},{10,8},{12,10},{14,12},{11,9},... | collective-permute-start | bytes 1880072 | tf_op jit(solution)/shard_map/ppermute | solution.py:27
  309.5 37.8 %all-to-all-start.2 = ((bf16[4,36,2176]{2,1,0:T(8,128)(2,1)}), bf16[4,36,2176]{2,1,0:T(8,128)(2,1)S(1)}, u32[]{:S(2)}, u32[]{:S(2)}) async-start(bf16[4,36,2176]{2,1,0:T(8,128)(2,1)} %reshape.71), calls=%async_computation.2 | async-start | bytes 1392640 | tf_op jit(solution)/shard_map/all_to_all | solution.py:125
  (23 other events, 267.3 us)

commit v2 on v1

v2 whole, which is shorter than its diff:
```python
import jax
import jax.numpy as jnp
from jax import lax
from jax.sharding import Mesh, PartitionSpec as P

EXPERTS = 4
SECTION = ("ylo", "x", "core")
AXES = ("ylo", "x", "core", "zb", "zo", "yh")
LINE = 4
RING = 16
BF = jnp.bfloat16
F32 = jnp.float32


def dot(a, b, ca, cb):
    return lax.dot_general(a, b, (((ca,), (cb,)), ((), ())), preferred_element_type=F32)


def up(a):
    return lax.ppermute(a, ("zb", "zo"), [(i, (i + 1) % RING) for i in range(RING)])


def down(a):
    return lax.ppermute(a, ("zb", "zo"), [((i + 1) % RING, i) for i in range(RING)])


def opposite(a):
    return lax.ppermute(a, "zb", [(i, (i + 2) % EXPERTS) for i in range(EXPERTS)])


def line_up(a, first, last):
    return lax.ppermute(a, "zo", [(i, i + 1) for i in range(first, last)])


def line_down(a, first, last):
    return lax.ppermute(a, "zo", [(i + 1, i) for i in range(first, last)])


def across(a):
    return lax.ppermute(a, "yh", [(0, 1), (1, 0)])


def plus(*terms):
    total = terms[0].astype(F32)
    for term in terms[1:]:
        total = total + term.astype(F32)
    return total.astype(BF)


def per_device(tokens, upstream, expert_ids, combine, w_gate_up, w_down):
    tok, width = tokens.shape
    cap = tok * 9 // (8 * EXPERTS)
    pitch = cap + 4
    wgu = w_gate_up[0, 0]
    wdown = w_down[0, 0]
    hidden = wdown.shape[0]
    zb, zo, yh = lax.axis_index("zb"), lax.axis_index("zo"), lax.axis_index("yh")
    member = zo * 2 + yh
    sections = lax.axis_size(SECTION)
    out_grad = lax.ppermute(
        upstream, SECTION, [(i, (i - 1) % sections) for i in range(sections)]
    )

    ids = expert_ids[:, 0]
    onehot = (ids[:, None] == jnp.arange(EXPERTS, dtype=jnp.int32)[None, :]).astype(F32)
    earlier = (jnp.arange(tok)[:, None] > jnp.arange(tok)[None, :]).astype(F32)
    before = dot(earlier, onehot, 1, 0)
    slot = jnp.sum(before * onehot, axis=1).astype(jnp.int32)
    rel = (ids - zb) % EXPERTS
    weight = combine.astype(F32)
    scaled = (weight * out_grad.astype(F32)).astype(BF)

    pick_x = rel * (2 * cap) + slot
    picks = jnp.concatenate([pick_x, pick_x + cap])
    place = (
        jnp.arange(EXPERTS * 2 * cap, dtype=jnp.int32)[:, None] == picks[None, :]
    ).astype(BF)
    sent = dot(place, jnp.concatenate([tokens, scaled], axis=0), 1, 0).astype(BF)
    sent = sent.reshape(EXPERTS, 2 * cap, width)

    ups, downs = [None, up(sent[1])], [None, down(sent[3])]
    far = opposite(sent[2])
    unit = jnp.concatenate([sent[0], far], axis=0)
    for _ in range(6):
        ups.append(up(ups[-1]))
        downs.append(down(downs[-1]))
    r1, l1 = line_up(unit, 0, 3), line_down(unit, 0, 3)
    r2, l2 = line_up(r1, 1, 3), line_down(l1, 0, 2)
    r3, l3 = line_up(r2, 2, 3), line_down(l2, 0, 1)
    where = jnp.where
    first, last, low = zo == 0, zo == 3, zo <= 1
    t1 = where(first, l1, r1)
    t2 = where(first, l2, where(last, r2, l1))
    t3 = where(first, l3, where(zo == 1, l2, where(last, r3, r2)))
    s2 = where(low, ups[2], downs[2])
    s6 = where(low, downs[6], ups[6])
    s1 = where(first, ups[1], where(last, downs[1], ups[3]))
    s3 = where(first, ups[3], downs[3])
    s5 = where(last, ups[5], downs[5])
    s7 = where(first, downs[7], where(last, ups[7], ups[5]))
    groups = [
        jnp.concatenate([unit, s2], axis=0),
        jnp.concatenate([t1, s1, s3], axis=0),
        jnp.concatenate([t2, ups[4], downs[4]], axis=0),
        jnp.concatenate([t3, s5, s6], axis=0),
        s7,
    ]

    lane = jnp.arange(width, dtype=jnp.int32)
    mine = ((lane // 128) == member).astype(F32)

    def expert(rows):
        count = rows.shape[0] // (2 * cap)
        gu = dot(rows, wgu, 1, 0).reshape(count, 2 * cap, 2 * hidden)[:, :cap]
        draw = dot(rows, wdown, 1, 1).reshape(count, 2 * cap, hidden)[:, cap:]
        gate, upper = gu[:, :, :hidden], gu[:, :, hidden:]
        sig = jax.nn.sigmoid(gate)
        act = gate * sig
        hid = act * upper
        dp = jnp.sum(hid * draw, axis=2)
        dgate = draw * upper * sig * (1.0 + gate * (1.0 - sig))
        dupper = draw * act
        dgu = jnp.concatenate([dgate, dupper], axis=2).astype(BF)
        pads = lambda a, lo, hi: jnp.pad(a, ((0, 0), (lo, hi), (0, 0)))
        dx = dot(pads(dgu, 0, 4).reshape(count * pitch, 2 * hidden), wgu, 1, 1)
        dp = jnp.tile(jnp.pad(dp, ((0, 0), (0, 128 - cap))), (1, width // 128)) * mine
        dp = pads(dp[:, None, :], cap, 3).reshape(count * pitch, width)
        dx = (dx + dp).astype(BF)
        dgu = pads(dgu, 0, cap).reshape(count * 2 * cap, 2 * hidden)
        hid = pads(hid.astype(BF), cap, 0).reshape(count * 2 * cap, hidden)
        return dx, dgu, hid

    others = [across(g) for g in groups]
    own_dx, other_dx, dgus, hids = [], [], [], []
    for g, o in zip(groups, others):
        dx, dgu, hid = expert(g)
        own_dx.append(dx)
        dgus.append(dgu)
        hids.append(hid)
        dx, dgu, hid = expert(o)
        other_dx.append(dx)
        dgus.append(dgu)
        hids.append(hid)

    total = [None] * 5
    for k in (4, 3, 2, 1, 0):
        total[k] = plus(own_dx[k], across(other_dx[k]))
    part = lambda a, lo, hi: a[lo * pitch : hi * pitch]
    b_unit, b_s2 = part(total[0], 0, 2), part(total[0], 2, 3)
    b_t1, b_s1, b_s3 = part(total[1], 0, 2), part(total[1], 2, 3), part(total[1], 3, 4)
    b_t2, b_u4, b_d4 = part(total[2], 0, 2), part(total[2], 2, 3), part(total[2], 3, 4)
    b_t3, b_s5, b_s6 = part(total[3], 0, 2), part(total[3], 2, 3), part(total[3], 3, 4)
    b_s7 = total[4]
    zero = jnp.zeros((), BF)
    mid = (zo == 1) | (zo == 2)
    from_ups = [
        where(first, b_s1, zero),
        where(low, b_s2, zero),
        where(first, b_s3, where(last, zero, b_s1)),
        b_u4,
        where(last, b_s5, where(first, zero, b_s7)),
        where(low, zero, b_s6),
        where(last, b_s7, zero),
    ]
    from_downs = [
        where(last, b_s1, zero),
        where(low, zero, b_s2),
        where(first, zero, b_s3),
        b_d4,
        where(last, zero, b_s5),
        where(low, b_s6, zero),
        where(first, b_s7, zero),
    ]
    back_next, back_prev = down(from_ups[6]), up(from_downs[6])
    for k in (5, 4, 3, 2, 1, 0):
        back_next = down(plus(from_ups[k], back_next))
        back_prev = up(plus(from_downs[k], back_prev))
    q3, m3 = line_down(b_t3, 2, 3), line_up(b_t3, 0, 1)
    q2 = line_down(plus(where(last, b_t2, b_t3), q3), 1, 3)
    m2 = line_up(plus(where(first, b_t2, b_t3), m3), 0, 2)
    q1 = line_down(plus(b_t1, q2), 0, 3)
    m1 = line_up(plus(where(first, b_t1, b_t2), m2), 0, 3)
    back_unit = plus(b_unit, q1, m1)
    back_far = opposite(back_unit[pitch:])
    back = jnp.concatenate([back_unit[:pitch], back_next, back_far, back_prev], axis=0)

    put = (
        jnp.arange(EXPERTS * pitch, dtype=jnp.int32)[:, None]
        == (rel * pitch + slot)[None, :]
    ).astype(BF)
    moe = dot(put, back, 0, 0)
    input_grad = (out_grad.astype(F32) + moe).astype(BF)
    dp = back.reshape(EXPERTS, pitch, width)[:, cap, : 8 * 128].astype(F32)
    dp = jnp.sum(dp.reshape(EXPERTS, 8, 128), axis=1)
    pick = (rel[:, None] == jnp.arange(EXPERTS)[None, :])[:, :, None] & (
        slot[:, None] == jnp.arange(128)[None, :]
    )[:, None, :]
    dp = jnp.sum(jnp.where(pick, dp[None], 0.0), axis=(1, 2))
    combine_grad = (dp[:, None] / weight).astype(BF)

    rows = jnp.concatenate([a for pair in zip(groups, others) for a in pair], axis=0)
    grad_gu = dot(rows, jnp.concatenate(dgus, axis=0), 0, 0).astype(BF)
    grad_down = dot(jnp.concatenate(hids, axis=0), rows, 0, 0).astype(BF)
    return (input_grad, combine_grad, grad_gu[None, None], grad_down[None, None])


def solution(mesh):
    fine = Mesh(mesh.devices.reshape(2, 4, 2, 4, 4, 2), AXES)
    row = P(AXES, None)
    weights = P(SECTION, ("zb", "zo", "yh"), None, None)
    return jax.shard_map(
        per_device,
        mesh=fine,
        in_specs=(row, row, row, row, weights, weights),
        out_specs=(row, row, weights, weights),
        check_vma=False,
    )
```

time: 351 us -> 389 us (1.11)
  the two profiles are of different devices: /device:TPU:54 before, /device:TPU:6 now
where the time goes in v2:
time: 389 us; the launch traced here: 387 us
  starting transfers between devices  176 us (45%)
  waiting for transfers between devices  176 us (45%)
  matrix products  23.2 us (6%)
  other arithmetic  6.73 us (2%)
    ppermute x10, waiting for transfers between devices, across(): return lax.ppermute(a, 'yh', [(0, 1), (1, 0)])  87.2 us
    ppermute x14, starting transfers between devices, down(): lax.ppermute(a, ('zb', 'zo'), [((i + 1) % RING, i) for i in range(RING)])  55.8 us
    ppermute x14, starting transfers between devices, up(): lax.ppermute(a, ('zb', 'zo'), [(i, (i + 1) % RING) for i in range(RING)])  43.7 us
    ppermute x14, waiting for transfers between devices, up(): lax.ppermute(a, ('zb', 'zo'), [(i, (i + 1) % RING) for i in range(RING)])  36.8 us
    ppermute x10, starting transfers between devices, across(): return lax.ppermute(a, 'yh', [(0, 1), (1, 0)])  34 us
    ppermute x2, waiting for transfers between devices, opposite(): lax.ppermute(a, 'zb', [(i, (i + 2) % EXPERTS) for i in range(EXPERTS)])  25.8 us
    dot_general x35, matrix products, dot(): lax.dot_general(a, b, (((ca,), (cb,)), ((), ())), preferred_element_type=...  23.2 us
    ppermute x14, waiting for transfers between devices, down(): lax.ppermute(a, ('zb', 'zo'), [((i + 1) % RING, i) for i in range(RING)])  18.8 us
  transfers between devices with their start and end apart: 53, of which 22 were waited for; matrix products, arithmetic and copies ran while one was open for 7% of the time, Pallas kernels for 0%

profile of v2, /device:TPU:6, one launch (start us, length us, event | category | flops | bytes accessed | tf_op | source)
XLA Modules:
  0.0 387.1 jit_solution(4532531856513817987)
XLA Ops:
  5.3 4.7 %collective-permute-done = bf16[128,2048]{1,0:T(8,128)(2,1)S(1)} collective-permute-done((bf16[128,2048]{1,0:T(8,128)(2,1)}, bf16[128,2048]{1,0:T(8,128)(2,1)S(1)}, u32[]{:S(2)}, u32[]{:S(2)}) %collective-permute-start) | collective-permute-done | bytes 524320 | tf_op jit(solution)/shard_map/ppermute | solution.py:60
  16.4 9.5 %collective-permute-start.4 = (bf16[72,2048]{1,0:T(8,128)(2,1)S(1)}, bf16[72,2048]{1,0:T(8,128)(2,1)S(1)}, u32[]{:S(2)}, u32[]{:S(2)}) collective-permute-start(bf16[72,2048]{1,0:T(8,128)(2,1)S(1)} %get-tuple-element.29), channel_id=1, source_target_pairs={{2,0},{4,2},{6,4},{8,6},{10,8},{12,10},{14,12},{16,14},{18,16},{20... | collective-permute-start | bytes 884744 | tf_op jit(solution)/shard_map/ppermute | solution.py:24
  25.9 9.5 %collective-permute-start.1 = (bf16[72,2048]{1,0:T(8,128)(2,1)S(1)}, bf16[72,2048]{1,0:T(8,128)(2,1)S(1)}, u32[]{:S(2)}, u32[]{:S(2)}) collective-permute-start(bf16[72,2048]{1,0:T(8,128)(2,1)S(1)} %get-tuple-element.31), channel_id=1, source_target_pairs={{0,16},{8,24},{16,0},{24,8},{1,17},{9,25},{17,1},{25,9},{2,18},{10... | collective-permute-start | bytes 884744 | tf_op jit(solution)/shard_map/ppermute | solution.py:28
  37.3 5.1 %collective-permute-start.5 = (bf16[72,2048]{1,0:T(8,128)(2,1)S(1)}, bf16[72,2048]{1,0:T(8,128)(2,1)S(1)}, u32[]{:S(2)}, u32[]{:S(2)}) collective-permute-start(bf16[72,2048]{1,0:T(8,128)(2,1)S(1)} %collective-permute-done.4), channel_id=1, source_target_pairs={{2,0},{4,2},{6,4},{8,6},{10,8},{12,10},{14,12},{16,14},{18,16},{20... | collective-permute-start | bytes 884744 | tf_op jit(solution)/shard_map/ppermute | solution.py:24
  42.5 16.9 %collective-permute-done.1 = bf16[72,2048]{1,0:T(8,128)(2,1)S(1)} collective-permute-done((bf16[72,2048]{1,0:T(8,128)(2,1)S(1)}, bf16[72,2048]{1,0:T(8,128)(2,1)S(1)}, u32[]{:S(2)}, u32[]{:S(2)}) %collective-permute-start.1) | collective-permute-done | bytes 294944 | tf_op jit(solution)/shard_map/ppermute | solution.py:28
  60.1 6.4 %collective-permute-done.3 = bf16[72,2048]{1,0:T(8,128)(2,1)S(1)} collective-permute-done((bf16[72,2048]{1,0:T(8,128)(2,1)S(1)}, bf16[72,2048]{1,0:T(8,128)(2,1)S(1)}, u32[]{:S(2)}, u32[]{:S(2)}) %collective-permute-start.3) | collective-permute-done | bytes 294944 | tf_op jit(solution)/shard_map/ppermute | solution.py:20
  68.1 5.1 %collective-permute-start.6 = (bf16[216,2048]{1,0:T(8,128)(2,1)S(1)}, bf16[216,2048]{1,0:T(8,128)(2,1)S(1)}, u32[]{:S(2)}, u32[]{:S(2)}) collective-permute-start(bf16[216,2048]{1,0:T(8,128)(2,1)S(1)} %pad_maximum_fusion.3), channel_id=1, source_target_pairs={{0,1},{1,0},{2,3},{3,2},{4,5},{5,4},{6,7},{7,6},{8,9},{9,8},{10,11... | collective-permute-start | bytes 2654216 | tf_op jit(solution)/shard_map/ppermute | solution.py:40
  74.7 5.0 %collective-permute-start.9 = (bf16[144,2048]{1,0:T(8,128)(2,1)S(1)}, bf16[144,2048]{1,0:T(8,128)(2,1)S(1)}, u32[]{:S(2)}, u32[]{:S(2)}) collective-permute-start(bf16[144,2048]{1,0:T(8,128)(2,1)S(1)} %pad_maximum_fusion.5), channel_id=1, source_target_pairs={{0,2},{2,4},{4,6},{1,3},{3,5},{5,7},{8,10},{10,12},{12,14},{9,11},... | collective-permute-start | bytes 1769480 | tf_op jit(solution)/shard_map/ppermute | solution.py:32
  79.7 3.9 %collective-permute-start.10 = (bf16[72,2048]{1,0:T(8,128)(2,1)S(1)}, bf16[72,2048]{1,0:T(8,128)(2,1)S(1)}, u32[]{:S(2)}, u32[]{:S(2)}) collective-permute-start(bf16[72,2048]{1,0:T(8,128)(2,1)S(1)} %collective-permute-done.3), channel_id=1, source_target_pairs={{0,2},{2,4},{4,6},{6,8},{8,10},{10,12},{12,14},{14,16},{16,18},{18... | collective-permute-start | bytes 884744 | tf_op jit(solution)/shard_map/ppermute | solution.py:20
  87.7 11.1 %collective-permute-done.10 = bf16[72,2048]{1,0:T(8,128)(2,1)S(1)} collective-permute-done((bf16[72,2048]{1,0:T(8,128)(2,1)S(1)}, bf16[72,2048]{1,0:T(8,128)(2,1)S(1)}, u32[]{:S(2)}, u32[]{:S(2)}) %collective-permute-start.10) | collective-permute-done | bytes 294944 | tf_op jit(solution)/shard_map/ppermute | solution.py:20
  98.8 4.4 %collective-permute-start.16 = (bf16[72,2048]{1,0:T(8,128)(2,1)S(1)}, bf16[72,2048]{1,0:T(8,128)(2,1)S(1)}, u32[]{:S(2)}, u32[]{:S(2)}) collective-permute-start(bf16[72,2048]{1,0:T(8,128)(2,1)S(1)} %collective-permute-done.10), channel_id=1, source_target_pairs={{0,2},{2,4},{4,6},{6,8},{8,10},{10,12},{12,14},{14,16},{16,18},{18... | collective-permute-start | bytes 884744 | tf_op jit(solution)/shard_map/ppermute | solution.py:20
  110.0 5.1 %collective-permute-start.22 = (bf16[72,2048]{1,0:T(8,128)(2,1)S(1)}, bf16[72,2048]{1,0:T(8,128)(2,1)S(1)}, u32[]{:S(2)}, u32[]{:S(2)}) collective-permute-start(bf16[72,2048]{1,0:T(8,128)(2,1)S(1)} %collective-permute-done.16), channel_id=1, source_target_pairs={{0,2},{2,4},{4,6},{6,8},{8,10},{10,12},{12,14},{14,16},{16,18},{18... | collective-permute-start | bytes 884744 | tf_op jit(solution)/shard_map/ppermute | solution.py:20
  122.4 5.1 %collective-permute-start.7 = (bf16[120,2048]{1,0:T(8,128)(2,1)S(1)}, bf16[120,2048]{1,0:T(8,128)(2,1)S(1)}, u32[]{:S(2)}, u32[]{:S(2)}) collective-permute-start(bf16[120,2048]{1,0:T(8,128)(2,1)S(1)} %fusion.13), channel_id=1, source_target_pairs={{0,1},{1,0},{2,3},{3,2},{4,5},{5,4},{6,7},{7,6},{8,9},{9,8},{10,11... | collective-permute-start | bytes 1474568 | tf_op jit(solution)/shard_map/ppermute | solution.py:40
  127.7 4.1 %collective-permute-done.23 = bf16[72,2048]{1,0:T(8,128)(2,1)S(1)} collective-permute-done((bf16[72,2048]{1,0:T(8,128)(2,1)S(1)}, bf16[72,2048]{1,0:T(8,128)(2,1)S(1)}, u32[]{:S(2)}, u32[]{:S(2)}) %collective-permute-start.23) | collective-permute-done | bytes 294944 | tf_op jit(solution)/shard_map/ppermute | solution.py:24
  134.9 4.0 %collective-permute-start.24 = (bf16[72,2048]{1,0:T(8,128)(2,1)S(1)}, bf16[72,2048]{1,0:T(8,128)(2,1)S(1)}, u32[]{:S(2)}, u32[]{:S(2)}) collective-permute-start(bf16[72,2048]{1,0:T(8,128)(2,1)S(1)} %collective-permute-done.23), channel_id=1, source_target_pairs={{2,0},{4,2},{6,4},{8,6},{10,8},{12,10},{14,12},{16,14},{18,16},{20... | collective-permute-start | bytes 884744 | tf_op jit(solution)/shard_map/ppermute | solution.py:24
  142.5 4.7 %collective-permute-done.24 = bf16[72,2048]{1,0:T(8,128)(2,1)S(1)} collective-permute-done((bf16[72,2048]{1,0:T(8,128)(2,1)S(1)}, bf16[72,2048]{1,0:T(8,128)(2,1)S(1)}, u32[]{:S(2)}, u32[]{:S(2)}) %collective-permute-start.24) | collective-permute-done | bytes 294944 | tf_op jit(solution)/shard_map/ppermute | solution.py:24
  149.1 9.0 %collective-permute-done.7 = bf16[120,2048]{1,0:T(8,128)(2,1)S(1)} collective-permute-done((bf16[120,2048]{1,0:T(8,128)(2,1)S(1)}, bf16[120,2048]{1,0:T(8,128)(2,1)S(1)}, u32[]{:S(2)}, u32[]{:S(2)}) %collective-permute-start.7) | collective-permute-done | bytes 491552 | tf_op jit(solution)/shard_map/ppermute | solution.py:40
  165.7 23.4 %collective-permute-done.18 = bf16[288,2048]{1,0:T(8,128)(2,1)S(1)} collective-permute-done((bf16[288,2048]{1,0:T(8,128)(2,1)S(1)}, bf16[288,2048]{1,0:T(8,128)(2,1)S(1)}, u32[]{:S(2)}, u32[]{:S(2)}) %collective-permute-start.18) | collective-permute-done | bytes 1179680 | tf_op jit(solution)/shard_map/ppermute | solution.py:40
  194.6 23.4 %collective-permute-done.26 = bf16[288,2048]{1,0:T(8,128)(2,1)S(1)} collective-permute-done((bf16[288,2048]{1,0:T(8,128)(2,1)S(1)}, bf16[288,2048]{1,0:T(8,128)(2,1)S(1)}, u32[]{:S(2)}, u32[]{:S(2)}) %collective-permute-start.26) | collective-permute-done | bytes 1179680 | tf_op jit(solution)/shard_map/ppermute | solution.py:40
  222.9 5.1 %collective-permute-start.19 = (bf16[160,2048]{1,0:T(8,128)(2,1)S(1)}, bf16[160,2048]{1,0:T(8,128)(2,1)S(1)}, u32[]{:S(2)}, u32[]{:S(2)}) collective-permute-start(bf16[160,2048]{1,0:T(8,128)(2,1)S(1)} %fusion.6), channel_id=1, source_target_pairs={{0,1},{1,0},{2,3},{3,2},{4,5},{5,4},{6,7},{7,6},{8,9},{9,8},{10,11... | collective-permute-start | bytes 1966088 | tf_op jit(solution)/shard_map/ppermute | solution.py:40
  231.6 5.1 %collective-permute-start.13 = (bf16[160,2048]{1,0:T(8,128)(2,1)S(1)}, bf16[160,2048]{1,0:T(8,128)(2,1)S(1)}, u32[]{:S(2)}, u32[]{:S(2)}) collective-permute-start(bf16[160,2048]{1,0:T(8,128)(2,1)S(1)} %fusion.3), channel_id=1, source_target_pairs={{0,1},{1,0},{2,3},{3,2},{4,5},{5,4},{6,7},{7,6},{8,9},{9,8},{10,11... | collective-permute-start | bytes 1966088 | tf_op jit(solution)/shard_map/ppermute | solution.py:40
  240.8 31.5 %collective-permute-done.37 = bf16[40,2048]{1,0:T(8,128)(2,1)S(1)} collective-permute-done((bf16[40,2048]{1,0:T(8,128)(2,1)S(1)}, bf16[40,2048]{1,0:T(8,128)(2,1)S(1)}, u32[]{:S(2)}, u32[]{:S(2)}) %collective-permute-start.37) | collective-permute-done | bytes 163872 | tf_op jit(solution)/shard_map/ppermute | solution.py:40
  274.7 3.9 %collective-permute-start.46 = (bf16[40,2048]{1,0:T(8,128)(2,1)S(1)}, bf16[40,2048]{1,0:T(8,128)(2,1)S(1)}, u32[]{:S(2)}, u32[]{:S(2)}) collective-permute-start(bf16[40,2048]{1,0:T(8,128)(2,1)S(1)} %get-tuple-element.79), channel_id=1, source_target_pairs={{0,2},{2,4},{4,6},{6,8},{8,10},{10,12},{12,14},{14,16},{16,18},{18... | collective-permute-start | bytes 491528 | tf_op jit(solution)/shard_map/ppermute | solution.py:20
  283.6 5.2 %collective-permute-done.39 = bf16[40,2048]{1,0:T(8,128)(2,1)S(1)} collective-permute-done((bf16[40,2048]{1,0:T(8,128)(2,1)S(1)}, bf16[40,2048]{1,0:T(8,128)(2,1)S(1)}, u32[]{:S(2)}, u32[]{:S(2)}) %collective-permute-start.39) | collective-permute-done | bytes 163872 | tf_op jit(solution)/shard_map/ppermute | solution.py:24
  299.7 5.7 %collective-permute-start.40 = (bf16[40,2048]{1,0:T(8,128)(2,1)S(1)}, bf16[40,2048]{1,0:T(8,128)(2,1)S(1)}, u32[]{:S(2)}, u32[]{:S(2)}) collective-permute-start(bf16[40,2048]{1,0:T(8,128)(2,1)S(1)} %get-tuple-element.38), channel_id=1, source_target_pairs={{2,0},{4,2},{6,4},{8,6},{10,8},{12,10},{14,12},{16,14},{18,16},{20... | collective-permute-start | bytes 491528 | tf_op jit(solution)/shard_map/ppermute | solution.py:24
  308.2 5.7 %collective-permute-done.48 = bf16[40,2048]{1,0:T(8,128)(2,1)S(1)} collective-permute-done((bf16[40,2048]{1,0:T(8,128)(2,1)S(1)}, bf16[40,2048]{1,0:T(8,128)(2,1)S(1)}, u32[]{:S(2)}, u32[]{:S(2)}) %collective-permute-start.48) | collective-permute-done | bytes 163872 | tf_op jit(solution)/shard_map/ppermute | solution.py:20
  324.6 5.3 %collective-permute-start.42 = (bf16[40,2048]{1,0:T(8,128)(2,1)S(1)}, bf16[40,2048]{1,0:T(8,128)(2,1)S(1)}, u32[]{:S(2)}, u32[]{:S(2)}) collective-permute-start(bf16[40,2048]{1,0:T(8,128)(2,1)S(1)} %get-tuple-element.34), channel_id=1, source_target_pairs={{2,0},{4,2},{6,4},{8,6},{10,8},{12,10},{14,12},{16,14},{18,16},{20... | collective-permute-start | bytes 491528 | tf_op jit(solution)/shard_map/ppermute | solution.py:24
  334.6 7.3 %collective-permute-done.50 = bf16[40,2048]{1,0:T(8,128)(2,1)S(1)} collective-permute-done((bf16[40,2048]{1,0:T(8,128)(2,1)S(1)}, bf16[40,2048]{1,0:T(8,128)(2,1)S(1)}, u32[]{:S(2)}, u32[]{:S(2)}) %collective-permute-start.50) | collective-permute-done | bytes 163872 | tf_op jit(solution)/shard_map/ppermute | solution.py:20
  349.3 4.6 %collective-permute-start.33 = (bf16[80,2048]{1,0:T(8,128)(2,1)S(1)}, bf16[80,2048]{1,0:T(8,128)(2,1)S(1)}, u32[]{:S(2)}, u32[]{:S(2)}) collective-permute-start(bf16[80,2048]{1,0:T(8,128)(2,1)S(1)} %get-tuple-element.41), channel_id=1, source_target_pairs={{0,2},{2,4},{4,6},{1,3},{3,5},{5,7},{8,10},{10,12},{12,14},{9,11},... | collective-permute-start | bytes 983048 | tf_op jit(solution)/shard_map/ppermute | solution.py:32
  354.0 7.2 %collective-permute-start.44 = (bf16[40,2048]{1,0:T(8,128)(2,1)S(1)}, bf16[40,2048]{1,0:T(8,128)(2,1)S(1)}, u32[]{:S(2)}, u32[]{:S(2)}) collective-permute-start(bf16[40,2048]{1,0:T(8,128)(2,1)S(1)} %get-tuple-element.32), channel_id=1, source_target_pairs={{2,0},{4,2},{6,4},{8,6},{10,8},{12,10},{14,12},{16,14},{18,16},{20... | collective-permute-start | bytes 491528 | tf_op jit(solution)/shard_map/ppermute | solution.py:24
  365.7 8.3 %collective-permute-start.45 = (bf16[40,2048]{1,0:T(8,128)(2,1)S(1)}, bf16[40,2048]{1,0:T(8,128)(2,1)S(1)}, u32[]{:S(2)}, u32[]{:S(2)}) collective-permute-start(bf16[40,2048]{1,0:T(8,128)(2,1)S(1)} %get-tuple-element.63), channel_id=1, source_target_pairs={{0,16},{8,24},{16,0},{24,8},{1,17},{9,25},{17,1},{25,9},{2,18},{10... | collective-permute-start | bytes 491528 | tf_op jit(solution)/shard_map/ppermute | solution.py:28
  376.2 8.9 %collective-permute-done.45 = bf16[40,2048]{1,0:T(8,128)(2,1)S(1)} collective-permute-done((bf16[40,2048]{1,0:T(8,128)(2,1)S(1)}, bf16[40,2048]{1,0:T(8,128)(2,1)S(1)}, u32[]{:S(2)}, u32[]{:S(2)}) %collective-permute-start.45) | collective-permute-done | bytes 163872 | tf_op jit(solution)/shard_map/ppermute | solution.py:28
  (257 shorter events, 120.8 us)
Async XLA Ops:
  12.5 22.8 %collective-permute-start.2 = (bf16[72,2048]{1,0:T(8,128)(2,1)S(1)}, bf16[72,2048]{1,0:T(8,128)(2,1)S(1)}, u32[]{:S(2)}, u32[]{:S(2)}) collective-permute-start(bf16[72,2048]{1,0:T(8,128)(2,1)S(1)} %get-tuple-element.30), channel_id=1, source_target_pairs={{0,2},{2,4},{4,6},{6,8},{8,10},{10,12},{12,14},{14,16},{16,18},{18... | collective-permute-start | bytes 884744 | tf_op jit(solution)/shard_map/ppermute | solution.py:20
  16.4 21.0 %collective-permute-start.4 = (bf16[72,2048]{1,0:T(8,128)(2,1)S(1)}, bf16[72,2048]{1,0:T(8,128)(2,1)S(1)}, u32[]{:S(2)}, u32[]{:S(2)}) collective-permute-start(bf16[72,2048]{1,0:T(8,128)(2,1)S(1)} %get-tuple-element.29), channel_id=1, source_target_pairs={{2,0},{4,2},{6,4},{8,6},{10,8},{12,10},{14,12},{16,14},{18,16},{20... | collective-permute-start | bytes 884744 | tf_op jit(solution)/shard_map/ppermute | solution.py:24
  25.9 33.5 %collective-permute-start.1 = (bf16[72,2048]{1,0:T(8,128)(2,1)S(1)}, bf16[72,2048]{1,0:T(8,128)(2,1)S(1)}, u32[]{:S(2)}, u32[]{:S(2)}) collective-permute-start(bf16[72,2048]{1,0:T(8,128)(2,1)S(1)} %get-tuple-element.31), channel_id=1, source_target_pairs={{0,16},{8,24},{16,0},{24,8},{1,17},{9,25},{17,1},{25,9},{2,18},{10... | collective-permute-start | bytes 884744 | tf_op jit(solution)/shard_map/ppermute | solution.py:28
  35.4 31.2 %collective-permute-start.3 = (bf16[72,2048]{1,0:T(8,128)(2,1)S(1)}, bf16[72,2048]{1,0:T(8,128)(2,1)S(1)}, u32[]{:S(2)}, u32[]{:S(2)}) collective-permute-start(bf16[72,2048]{1,0:T(8,128)(2,1)S(1)} %collective-permute-done.2), channel_id=1, source_target_pairs={{0,2},{2,4},{4,6},{6,8},{8,10},{10,12},{12,14},{14,16},{16,18},{18... | collective-permute-start | bytes 884744 | tf_op jit(solution)/shard_map/ppermute | solution.py:20
  37.3 29.9 %collective-permute-start.5 = (bf16[72,2048]{1,0:T(8,128)(2,1)S(1)}, bf16[72,2048]{1,0:T(8,128)(2,1)S(1)}, u32[]{:S(2)}, u32[]{:S(2)}) collective-permute-start(bf16[72,2048]{1,0:T(8,128)(2,1)S(1)} %collective-permute-done.4), channel_id=1, source_target_pairs={{2,0},{4,2},{6,4},{8,6},{10,8},{12,10},{14,12},{16,14},{18,16},{20... | collective-permute-start | bytes 884744 | tf_op jit(solution)/shard_map/ppermute | solution.py:24
  68.1 48.9 %collective-permute-start.6 = (bf16[216,2048]{1,0:T(8,128)(2,1)S(1)}, bf16[216,2048]{1,0:T(8,128)(2,1)S(1)}, u32[]{:S(2)}, u32[]{:S(2)}) collective-permute-start(bf16[216,2048]{1,0:T(8,128)(2,1)S(1)} %pad_maximum_fusion.3), channel_id=1, source_target_pairs={{0,1},{1,0},{2,3},{3,2},{4,5},{5,4},{6,7},{7,6},{8,9},{9,8},{10,11... | collective-permute-start | bytes 2654216 | tf_op jit(solution)/shard_map/ppermute | solution.py:40
  73.3 32.6 %collective-permute-start.8 = (bf16[144,2048]{1,0:T(8,128)(2,1)S(1)}, bf16[144,2048]{1,0:T(8,128)(2,1)S(1)}, u32[]{:S(2)}, u32[]{:S(2)}) collective-permute-start(bf16[144,2048]{1,0:T(8,128)(2,1)S(1)} %pad_maximum_fusion.5), channel_id=1, source_target_pairs={{2,0},{4,2},{6,4},{3,1},{5,3},{7,5},{10,8},{12,10},{14,12},{11,9},... | collective-permute-start | bytes 1769480 | tf_op jit(solution)/shard_map/ppermute | solution.py:36
  74.7 32.5 %collective-permute-start.9 = (bf16[144,2048]{1,0:T(8,128)(2,1)S(1)}, bf16[144,2048]{1,0:T(8,128)(2,1)S(1)}, u32[]{:S(2)}, u32[]{:S(2)}) collective-permute-start(bf16[144,2048]{1,0:T(8,128)(2,1)S(1)} %pad_maximum_fusion.5), channel_id=1, source_target_pairs={{0,2},{2,4},{4,6},{1,3},{3,5},{5,7},{8,10},{10,12},{12,14},{9,11},... | collective-permute-start | bytes 1769480 | tf_op jit(solution)/shard_map/ppermute | solution.py:32
  79.7 19.0 %collective-permute-start.10 = (bf16[72,2048]{1,0:T(8,128)(2,1)S(1)}, bf16[72,2048]{1,0:T(8,128)(2,1)S(1)}, u32[]{:S(2)}, u32[]{:S(2)}) collective-permute-start(bf16[72,2048]{1,0:T(8,128)(2,1)S(1)} %collective-permute-done.3), channel_id=1, source_target_pairs={{0,2},{2,4},{4,6},{6,8},{8,10},{10,12},{12,14},{14,16},{16,18},{18... | collective-permute-start | bytes 884744 | tf_op jit(solution)/shard_map/ppermute | solution.py:20
  83.6 19.5 %collective-permute-start.11 = (bf16[72,2048]{1,0:T(8,128)(2,1)S(1)}, bf16[72,2048]{1,0:T(8,128)(2,1)S(1)}, u32[]{:S(2)}, u32[]{:S(2)}) collective-permute-start(bf16[72,2048]{1,0:T(8,128)(2,1)S(1)} %collective-permute-done.5), channel_id=1, source_target_pairs={{2,0},{4,2},{6,4},{8,6},{10,8},{12,10},{14,12},{16,14},{18,16},{20... | collective-permute-start | bytes 884744 | tf_op jit(solution)/shard_map/ppermute | solution.py:24
  106.0 29.0 %collective-permute-start.14 = (bf16[144,2048]{1,0:T(8,128)(2,1)S(1)}, bf16[144,2048]{1,0:T(8,128)(2,1)S(1)}, u32[]{:S(2)}, u32[]{:S(2)}) collective-permute-start(bf16[144,2048]{1,0:T(8,128)(2,1)S(1)} %collective-permute-done.8), channel_id=1, source_target_pairs={{2,0},{4,2},{3,1},{5,3},{10,8},{12,10},{11,9},{13,11},{18,16},{20,... | collective-permute-start | bytes 1769480 | tf_op jit(solution)/shard_map/ppermute | solution.py:36
  107.3 31.7 %collective-permute-start.15 = (bf16[144,2048]{1,0:T(8,128)(2,1)S(1)}, bf16[144,2048]{1,0:T(8,128)(2,1)S(1)}, u32[]{:S(2)}, u32[]{:S(2)}) collective-permute-start(bf16[144,2048]{1,0:T(8,128)(2,1)S(1)} %collective-permute-done.9), channel_id=1, source_target_pairs={{2,4},{4,6},{3,5},{5,7},{10,12},{12,14},{11,13},{13,15},{18,20},{2... | collective-permute-start | bytes 1769480 | tf_op jit(solution)/shard_map/ppermute | solution.py:32
  115.1 16.7 %collective-permute-start.23 = (bf16[72,2048]{1,0:T(8,128)(2,1)S(1)}, bf16[72,2048]{1,0:T(8,128)(2,1)S(1)}, u32[]{:S(2)}, u32[]{:S(2)}) collective-permute-start(bf16[72,2048]{1,0:T(8,128)(2,1)S(1)} %collective-permute-done.17), channel_id=1, source_target_pairs={{2,0},{4,2},{6,4},{8,6},{10,8},{12,10},{14,12},{16,14},{18,16},{20... | collective-permute-start | bytes 884744 | tf_op jit(solution)/shard_map/ppermute | solution.py:24
  118.5 42.2 %collective-permute-start.12 = (bf16[288,2048]{1,0:T(8,128)(2,1)S(1)}, bf16[288,2048]{1,0:T(8,128)(2,1)S(1)}, u32[]{:S(2)}, u32[]{:S(2)}) collective-permute-start(bf16[288,2048]{1,0:T(8,128)(2,1)S(1)} %pad_maximum_fusion), channel_id=1, source_target_pairs={{0,1},{1,0},{2,3},{3,2},{4,5},{5,4},{6,7},{7,6},{8,9},{9,8},{10,11... | collective-permute-start | bytes 3538952 | tf_op jit(solution)/shard_map/ppermute | solution.py:40
  122.4 35.7 %collective-permute-start.7 = (bf16[120,2048]{1,0:T(8,128)(2,1)S(1)}, bf16[120,2048]{1,0:T(8,128)(2,1)S(1)}, u32[]{:S(2)}, u32[]{:S(2)}) collective-permute-start(bf16[120,2048]{1,0:T(8,128)(2,1)S(1)} %fusion.13), channel_id=1, source_target_pairs={{0,1},{1,0},{2,3},{3,2},{4,5},{5,4},{6,7},{7,6},{8,9},{9,8},{10,11... | collective-permute-start | bytes 1474568 | tf_op jit(solution)/shard_map/ppermute | solution.py:40
  139.0 51.2 %collective-permute-start.20 = (bf16[144,2048]{1,0:T(8,128)(2,1)S(1)}, bf16[144,2048]{1,0:T(8,128)(2,1)S(1)}, u32[]{:S(2)}, u32[]{:S(2)}) collective-permute-start(bf16[144,2048]{1,0:T(8,128)(2,1)S(1)} %collective-permute-done.14), channel_id=1, source_target_pairs={{2,0},{3,1},{10,8},{11,9},{18,16},{19,17},{26,24},{27,25},{34,32},... | collective-permute-start | bytes 1769480 | tf_op jit(solution)/shard_map/ppermute | solution.py:36
  141.8 48.4 %collective-permute-start.21 = (bf16[144,2048]{1,0:T(8,128)(2,1)S(1)}, bf16[144,2048]{1,0:T(8,128)(2,1)S(1)}, u32[]{:S(2)}, u32[]{:S(2)}) collective-permute-start(bf16[144,2048]{1,0:T(8,128)(2,1)S(1)} %collective-permute-done.15), channel_id=1, source_target_pairs={{4,6},{5,7},{12,14},{13,15},{20,22},{21,23},{28,30},{29,31},{36,38... | collective-permute-start | bytes 1769480 | tf_op jit(solution)/shard_map/ppermute | solution.py:32
  147.2 70.8 %collective-permute-start.35 = (bf16[72,2048]{1,0:T(8,128)(2,1)S(1)}, bf16[72,2048]{1,0:T(8,128)(2,1)S(1)}, u32[]{:S(2)}, u32[]{:S(2)}) collective-permute-start(bf16[72,2048]{1,0:T(8,128)(2,1)S(1)} %collective-permute-done.25), channel_id=1, source_target_pairs={{0,2},{2,4},{4,6},{6,8},{8,10},{10,12},{12,14},{14,16},{16,18},{18... | collective-permute-start | bytes 884744 | tf_op jit(solution)/shard_map/ppermute | solution.py:20
  158.0 60.0 %collective-permute-start.34 = (bf16[72,2048]{1,0:T(8,128)(2,1)S(1)}, bf16[72,2048]{1,0:T(8,128)(2,1)S(1)}, u32[]{:S(2)}, u32[]{:S(2)}) collective-permute-start(bf16[72,2048]{1,0:T(8,128)(2,1)S(1)} %collective-permute-done.24), channel_id=1, source_target_pairs={{2,0},{4,2},{6,4},{8,6},{10,8},{12,10},{14,12},{16,14},{18,16},{20... | collective-permute-start | bytes 884744 | tf_op jit(solution)/shard_map/ppermute | solution.py:24
  161.1 28.0 %collective-permute-start.18 = (bf16[288,2048]{1,0:T(8,128)(2,1)S(1)}, bf16[288,2048]{1,0:T(8,128)(2,1)S(1)}, u32[]{:S(2)}, u32[]{:S(2)}) collective-permute-start(bf16[288,2048]{1,0:T(8,128)(2,1)S(1)} %pad_maximum_fusion.1), channel_id=1, source_target_pairs={{0,1},{1,0},{2,3},{3,2},{4,5},{5,4},{6,7},{7,6},{8,9},{9,8},{10,11... | collective-permute-start | bytes 3538952 | tf_op jit(solution)/shard_map/ppermute | solution.py:40
  190.9 27.0 %collective-permute-start.26 = (bf16[288,2048]{1,0:T(8,128)(2,1)S(1)}, bf16[288,2048]{1,0:T(8,128)(2,1)S(1)}, u32[]{:S(2)}, u32[]{:S(2)}) collective-permute-start(bf16[288,2048]{1,0:T(8,128)(2,1)S(1)} %pad_maximum_fusion.2), channel_id=1, source_target_pairs={{0,1},{1,0},{2,3},{3,2},{4,5},{5,4},{6,7},{7,6},{8,9},{9,8},{10,11... | collective-permute-start | bytes 3538952 | tf_op jit(solution)/shard_map/ppermute | solution.py:40
  218.8 18.2 %collective-permute-start.36 = (bf16[72,2048]{1,0:T(8,128)(2,1)S(1)}, bf16[72,2048]{1,0:T(8,128)(2,1)S(1)}, u32[]{:S(2)}, u32[]{:S(2)}) collective-permute-start(bf16[72,2048]{1,0:T(8,128)(2,1)S(1)} %get-tuple-element.5), channel_id=1, source_target_pairs={{0,1},{1,0},{2,3},{3,2},{4,5},{5,4},{6,7},{7,6},{8,9},{9,8},{10,11... | collective-permute-start | bytes 884744 | tf_op jit(solution)/shard_map/ppermute | solution.py:40
  222.9 82.5 %collective-permute-start.19 = (bf16[160,2048]{1,0:T(8,128)(2,1)S(1)}, bf16[160,2048]{1,0:T(8,128)(2,1)S(1)}, u32[]{:S(2)}, u32[]{:S(2)}) collective-permute-start(bf16[160,2048]{1,0:T(8,128)(2,1)S(1)} %fusion.6), channel_id=1, source_target_pairs={{0,1},{1,0},{2,3},{3,2},{4,5},{5,4},{6,7},{7,6},{8,9},{9,8},{10,11... | collective-permute-start | bytes 1966088 | tf_op jit(solution)/shard_map/ppermute | solution.py:40
  228.7 49.9 %collective-permute-start.27 = (bf16[160,2048]{1,0:T(8,128)(2,1)S(1)}, bf16[160,2048]{1,0:T(8,128)(2,1)S(1)}, u32[]{:S(2)}, u32[]{:S(2)}) collective-permute-start(bf16[160,2048]{1,0:T(8,128)(2,1)S(1)} %fusion.9), channel_id=1, source_target_pairs={{0,1},{1,0},{2,3},{3,2},{4,5},{5,4},{6,7},{7,6},{8,9},{9,8},{10,11... | collective-permute-start | bytes 1966088 | tf_op jit(solution)/shard_map/ppermute | solution.py:40
  231.6 88.2 %collective-permute-start.13 = (bf16[160,2048]{1,0:T(8,128)(2,1)S(1)}, bf16[160,2048]{1,0:T(8,128)(2,1)S(1)}, u32[]{:S(2)}, u32[]{:S(2)}) collective-permute-start(bf16[160,2048]{1,0:T(8,128)(2,1)S(1)} %fusion.3), channel_id=1, source_target_pairs={{0,1},{1,0},{2,3},{3,2},{4,5},{5,4},{6,7},{7,6},{8,9},{9,8},{10,11... | collective-permute-start | bytes 1966088 | tf_op jit(solution)/shard_map/ppermute | solution.py:40
  238.2 34.1 %collective-permute-start.37 = (bf16[40,2048]{1,0:T(8,128)(2,1)S(1)}, bf16[40,2048]{1,0:T(8,128)(2,1)S(1)}, u32[]{:S(2)}, u32[]{:S(2)}) collective-permute-start(bf16[40,2048]{1,0:T(8,128)(2,1)S(1)} %fusion.17), channel_id=1, source_target_pairs={{0,1},{1,0},{2,3},{3,2},{4,5},{5,4},{6,7},{7,6},{8,9},{9,8},{10,11... | collective-permute-start | bytes 491528 | tf_op jit(solution)/shard_map/ppermute | solution.py:40
  296.3 35.6 %collective-permute-start.28 = (bf16[80,2048]{1,0:T(8,128)(2,1)S(1)}, bf16[80,2048]{1,0:T(8,128)(2,1)S(1)}, u32[]{:S(2)}, u32[]{:S(2)}) collective-permute-start(bf16[80,2048]{1,0:T(8,128)(2,1)S(1)} %slice.265), channel_id=1, source_target_pairs={{6,4},{7,5},{14,12},{15,13},{22,20},{23,21},{30,28},{31,29},{38,36... | collective-permute-start | bytes 983048 | tf_op jit(solution)/shard_map/ppermute | solution.py:36
  297.0 34.9 %collective-permute-start.31 = (bf16[80,2048]{1,0:T(8,128)(2,1)S(1)}, bf16[80,2048]{1,0:T(8,128)(2,1)S(1)}, u32[]{:S(2)}, u32[]{:S(2)}) collective-permute-start(bf16[80,2048]{1,0:T(8,128)(2,1)S(1)} %slice.265), channel_id=1, source_target_pairs={{0,2},{1,3},{8,10},{9,11},{16,18},{17,19},{24,26},{25,27},{32,34},... | collective-permute-start | bytes 983048 | tf_op jit(solution)/shard_map/ppermute | solution.py:32
  332.1 15.7 %collective-permute-start.29 = (bf16[80,2048]{1,0:T(8,128)(2,1)S(1)}, bf16[80,2048]{1,0:T(8,128)(2,1)S(1)}, u32[]{:S(2)}, u32[]{:S(2)}) collective-permute-start(bf16[80,2048]{1,0:T(8,128)(2,1)S(1)} %get-tuple-element.25), channel_id=1, source_target_pairs={{4,2},{6,4},{5,3},{7,5},{12,10},{14,12},{13,11},{15,13},{20,18},{2... | collective-permute-start | bytes 983048 | tf_op jit(solution)/shard_map/ppermute | solution.py:36
  349.3 16.2 %collective-permute-start.33 = (bf16[80,2048]{1,0:T(8,128)(2,1)S(1)}, bf16[80,2048]{1,0:T(8,128)(2,1)S(1)}, u32[]{:S(2)}, u32[]{:S(2)}) collective-permute-start(bf16[80,2048]{1,0:T(8,128)(2,1)S(1)} %get-tuple-element.41), channel_id=1, source_target_pairs={{0,2},{2,4},{4,6},{1,3},{3,5},{5,7},{8,10},{10,12},{12,14},{9,11},... | collective-permute-start | bytes 983048 | tf_op jit(solution)/shard_map/ppermute | solution.py:32
  354.0 22.1 %collective-permute-start.44 = (bf16[40,2048]{1,0:T(8,128)(2,1)S(1)}, bf16[40,2048]{1,0:T(8,128)(2,1)S(1)}, u32[]{:S(2)}, u32[]{:S(2)}) collective-permute-start(bf16[40,2048]{1,0:T(8,128)(2,1)S(1)} %get-tuple-element.32), channel_id=1, source_target_pairs={{2,0},{4,2},{6,4},{8,6},{10,8},{12,10},{14,12},{16,14},{18,16},{20... | collective-permute-start | bytes 491528 | tf_op jit(solution)/shard_map/ppermute | solution.py:24
  365.7 19.4 %collective-permute-start.45 = (bf16[40,2048]{1,0:T(8,128)(2,1)S(1)}, bf16[40,2048]{1,0:T(8,128)(2,1)S(1)}, u32[]{:S(2)}, u32[]{:S(2)}) collective-permute-start(bf16[40,2048]{1,0:T(8,128)(2,1)S(1)} %get-tuple-element.63), channel_id=1, source_target_pairs={{0,16},{8,24},{16,0},{24,8},{1,17},{9,25},{17,1},{25,9},{2,18},{10... | collective-permute-start | bytes 491528 | tf_op jit(solution)/shard_map/ppermute | solution.py:28
  (26 other events, 378.2 us)

commit v3 on v1

v3 whole, which is shorter than its diff:
```python
import jax
import jax.numpy as jnp
from jax import lax
from jax.sharding import Mesh, PartitionSpec as P

EXPERTS = 4
SECTION = ("ylo", "x", "core")
AXES = ("ylo", "x", "core", "zb", "zo", "yh")
RING = 16
LINE = 4
BF = jnp.bfloat16
F32 = jnp.float32


def dot(a, b, ca, cb):
    return lax.dot_general(a, b, (((ca,), (cb,)), ((), ())), preferred_element_type=F32)


def up(a):
    return lax.ppermute(a, ("zb", "zo"), [(i, (i + 1) % RING) for i in range(RING)])


def down(a):
    return lax.ppermute(a, ("zb", "zo"), [((i + 1) % RING, i) for i in range(RING)])


def across(a):
    return lax.ppermute(a, "yh", [(0, 1), (1, 0)])


def after(a, *others):
    return lax.optimization_barrier((a, *others))[0]


def per_device(tokens, upstream, expert_ids, combine, w_gate_up, w_down):
    tok, width = tokens.shape
    cap = tok * 9 // (8 * EXPERTS)
    pitch = cap + 4
    wgu = w_gate_up[0, 0]
    wdown = w_down[0, 0]
    hidden = wdown.shape[0]
    zo = lax.axis_index("zo")
    sections = lax.axis_size(SECTION)
    out_grad = lax.ppermute(
        upstream, SECTION, [(i, (i - 1) % sections) for i in range(sections)]
    )

    ids = expert_ids[:, 0]
    onehot = (ids[:, None] == jnp.arange(EXPERTS, dtype=jnp.int32)[None, :]).astype(F32)
    earlier = (jnp.arange(tok)[:, None] > jnp.arange(tok)[None, :]).astype(F32)
    before = dot(earlier, onehot, 1, 0)
    slot = jnp.sum(before * onehot, axis=1).astype(jnp.int32)
    weight = combine.astype(F32)
    scaled = (weight * out_grad.astype(F32)).astype(BF)
    place = (
        jnp.arange(EXPERTS * cap, dtype=jnp.int32)[:, None]
        == (ids * cap + slot)[None, :]
    ).astype(BF)

    def to_blocks(a):
        sent = dot(place, a, 1, 0).astype(BF).reshape(EXPERTS, cap, width)
        unit = lax.all_to_all(sent, "zb", 0, 0, tiled=True)
        return unit.reshape(EXPERTS * cap, width)

    where = jnp.where
    first, last = zo == 0, zo == 3

    def relay(unit):
        r1, l1 = up(unit), down(unit)
        t1 = where(first, l1, r1)
        r2, l2 = up(r1), down(l1)
        t2 = where(first, l2, where(last, r2, l1))
        r3, l3 = up(r2), down(l2)
        t3 = where(first, l3, where(last, r3, where(zo == 1, l2, r2)))
        return [unit, t1, t2, t3]

    xs = relay(to_blocks(tokens))
    gs = relay(to_blocks(scaled))

    wgu_all = jnp.concatenate([wgu, across(after(wgu, xs[0]))], axis=1)
    wdown_all = jnp.concatenate([wdown, across(after(wdown, xs[0]))], axis=0)

    rows = EXPERTS * cap
    lane = jnp.arange(width, dtype=jnp.int32)
    mine = ((lane // 128) == zo).astype(F32)

    def forward(x):
        gu = dot(x, wgu_all, 1, 0).reshape(rows, 2, 2 * hidden)
        return gu[:, :, :hidden].reshape(rows, -1), gu[:, :, hidden:].reshape(rows, -1)

    def expert(gate, upper, g):
        draw = dot(g, wdown_all, 1, 1)
        sig = jax.nn.sigmoid(gate)
        act = gate * sig
        hid = act * upper
        dp = jnp.sum(hid * draw, axis=1)
        dgate = draw * upper * sig * (1.0 + gate * (1.0 - sig))
        dupper = draw * act
        split = lambda a: a.reshape(rows, 2, hidden)
        dgu = jnp.concatenate([split(dgate), split(dupper)], axis=2).astype(BF)
        return dgu.reshape(rows, 4 * hidden), hid.astype(BF), dp

    late = gs[1:] + [gs[3]]
    gus = [forward(after(x, l)) for x, l in zip(xs, (xs[1], xs[2], xs[3], xs[3]))]
    done = [expert(*gu, after(g, l)) for gu, g, l in zip(gus, gs, late)]
    dgus = jnp.stack([d[0] for d in done])

    order = jnp.array([[0, 1, 2, 3], [1, 0, 2, 3], [3, 1, 0, 2], [3, 2, 1, 0]])[zo]
    pads = lambda a: jnp.pad(
        a.reshape(LINE, EXPERTS, cap, -1), ((0, 0), (0, 0), (0, 4), (0, 0))
    )
    sorted_dgu = pads(dgus[order]).reshape(LINE * EXPERTS * pitch, 4 * hidden)
    dps = jnp.stack([d[2] for d in done])[order].reshape(LINE, EXPERTS, cap)
    dps = jnp.pad(dps, ((0, 0), (0, 0), (0, 128 - cap)))
    dps = jnp.tile(dps, (1, 1, width // 128)) * mine
    dps = jnp.pad(dps[:, :, None, :], ((0, 0), (0, 0), (cap, 3), (0, 0)))
    dx = dot(sorted_dgu, wgu_all, 1, 1) + dps.reshape(-1, width)
    dx = dx.astype(BF).reshape(LINE, EXPERTS * pitch, width)

    dx = lax.all_to_all(dx, "zo", 0, 0, tiled=True)
    dx = jnp.sum(dx.astype(F32), axis=0).astype(BF).reshape(EXPERTS, pitch, width)
    back = lax.all_to_all(dx, "zb", 0, 0, tiled=True).reshape(-1, width)

    put = (
        jnp.arange(EXPERTS * pitch, dtype=jnp.int32)[:, None]
        == (ids * pitch + slot)[None, :]
    ).astype(BF)
    moe = dot(put, back, 0, 0)
    input_grad = (out_grad.astype(F32) + moe).astype(BF)
    dp = back.reshape(EXPERTS, pitch, width)[:, cap, : LINE * 128].astype(F32)
    dp = jnp.sum(dp.reshape(EXPERTS, LINE, 128), axis=1)
    pick = (ids[:, None] == jnp.arange(EXPERTS)[None, :])[:, :, None] & (
        slot[:, None] == jnp.arange(128)[None, :]
    )[:, None, :]
    dp = jnp.sum(jnp.where(pick, dp[None], 0.0), axis=(1, 2))
    combine_grad = (dp[:, None] / weight).astype(BF)

    x_all = jnp.concatenate(xs, axis=0)
    g_all = jnp.concatenate(gs, axis=0)
    dgu_all = dgus.reshape(LINE * rows, 4 * hidden)
    hid_all = jnp.concatenate([d[1] for d in done], axis=0)
    other_gu = dot(x_all, dgu_all[:, 2 * hidden :], 0, 0).astype(BF)
    other_down = dot(hid_all[:, hidden:], g_all, 0, 0).astype(BF)
    other_gu, other_down = across(other_gu), across(other_down)
    grad_gu = dot(x_all, dgu_all[:, : 2 * hidden], 0, 0) + other_gu.astype(F32)
    grad_down = dot(hid_all[:, :hidden], g_all, 0, 0) + other_down.astype(F32)
    grad_gu, grad_down = grad_gu.astype(BF), grad_down.astype(BF)
    return (input_grad, combine_grad, grad_gu[None, None], grad_down[None, None])


def solution(mesh):
    fine = Mesh(mesh.devices.reshape(2, 4, 2, 4, 4, 2), AXES)
    row = P(AXES, None)
    weights = P(SECTION, ("zb", "zo", "yh"), None, None)
    return jax.shard_map(
        per_device,
        mesh=fine,
        in_specs=(row, row, row, row, weights, weights),
        out_specs=(row, row, weights, weights),
        check_vma=False,
    )
```

time: 351 us -> 307 us (0.87)
  the two profiles are of different devices: /device:TPU:54 before, /device:TPU:6 now
where the time goes in v3:
time: 307 us; the launch traced here: 306 us
  waiting for transfers between devices  111 us (36%)
  starting transfers between devices  81.8 us (27%)
  blocking collectives  58.1 us (19%)
  matrix products  31.7 us (10%)
  local copies, waits for them, and re-layouts  12 us (4%)
  other arithmetic  9.1 us (3%)
    all_to_all x1, blocking collectives, per_device(): dx = lax.all_to_all(dx, 'zo', 0, 0, tiled=True)  58.1 us
    all_to_all x2, waiting for transfers between devices, to_blocks(): unit = lax.all_to_all(sent, 'zb', 0, 0, tiled=True)  53.5 us
    ppermute x4, waiting for transfers between devices, across(): return lax.ppermute(a, 'yh', [(0, 1), (1, 0)])  32.7 us
    dot_general x17, matrix products, dot(): lax.dot_general(a, b, (((ca,), (cb,)), ((), ())), preferred_element_type=...  31.7 us
    ppermute x6, starting transfers between devices, down(): lax.ppermute(a, ('zb', 'zo'), [((i + 1) % RING, i) for i in range(RING)])  20.8 us
    all_to_all x2, starting transfers between devices, to_blocks(): unit = lax.all_to_all(sent, 'zb', 0, 0, tiled=True)  18.6 us
    ppermute x6, waiting for transfers between devices, down(): lax.ppermute(a, ('zb', 'zo'), [((i + 1) % RING, i) for i in range(RING)])  18.3 us
    ppermute x4, starting transfers between devices, across(): return lax.ppermute(a, 'yh', [(0, 1), (1, 0)])  17.5 us
  transfers between devices with their start and end apart: 20, of which 10 were waited for; matrix products, arithmetic and copies ran while one was open for 9% of the time, Pallas kernels for 0%

profile of v3, /device:TPU:6, one launch (start us, length us, event | category | flops | bytes accessed | tf_op | source)
XLA Modules:
  0.0 305.6 jit_solution(3090286150908962640)
XLA Ops:
  4.1 15.1 %all-to-all-start.1 = ((bf16[4,36,2048]{2,1,0:T(8,128)(2,1)}), bf16[4,36,2048]{2,1,0:T(8,128)(2,1)S(1)}, u32[]{:S(2)}, u32[]{:S(2)}) async-start(bf16[4,36,2048]{2,1,0:T(8,128)(2,1)} %reshape.281), calls=%async_computation.1 | async-start | bytes 1310720 | tf_op jit(solution)/shard_map/all_to_all | solution.py:62
  21.1 6.7 %collective-permute-done = bf16[128,2048]{1,0:T(8,128)(2,1)S(1)} collective-permute-done((bf16[128,2048]{1,0:T(8,128)(2,1)S(1)}, bf16[128,2048]{1,0:T(8,128)(2,1)S(1)}, u32[]{:S(2)}, u32[]{:S(2)}) %collective-permute-start) | collective-permute-done | bytes 524320 | tf_op jit(solution)/shard_map/ppermute | solution.py:44
  29.9 27.1 %all-to-all-done.1 = bf16[4,36,2048]{2,1,0:T(8,128)(2,1)S(1)} async-done(((bf16[4,36,2048]{2,1,0:T(8,128)(2,1)}), bf16[4,36,2048]{2,1,0:T(8,128)(2,1)S(1)}, u32[]{:S(2)}, u32[]{:S(2)}) %all-to-all-start.1) | async-done | bytes 589856 | tf_op jit(solution)/shard_map/all_to_all | solution.py:62
  57.1 3.5 %all-to-all-start = ((bf16[4,36,2048]{2,1,0:T(8,128)(2,1)}), bf16[4,36,2048]{2,1,0:T(8,128)(2,1)S(1)}, u32[]{:S(2)}, u32[]{:S(2)}) async-start(bf16[4,36,2048]{2,1,0:T(8,128)(2,1)} %reshape.279), calls=%async_computation | async-start | bytes 1310720 | tf_op jit(solution)/shard_map/all_to_all | solution.py:62
  61.5 6.4 %collective-permute-start.4 = (bf16[144,2048]{1,0:T(8,128)(2,1)}, bf16[144,2048]{1,0:T(8,128)(2,1)S(1)}, u32[]{:S(2)}, u32[]{:S(2)}) collective-permute-start(bf16[144,2048]{1,0:T(8,128)(2,1)} %reshape.282), channel_id=1, source_target_pairs={{2,0},{4,2},{6,4},{8,6},{10,8},{12,10},{14,12},{16,14},{18,16},{20... | collective-permute-start | bytes 1769480 | tf_op jit(solution)/shard_map/ppermute | solution.py:24
  69.9 26.4 %all-to-all-done = bf16[4,36,2048]{2,1,0:T(8,128)(2,1)S(1)} async-done(((bf16[4,36,2048]{2,1,0:T(8,128)(2,1)}), bf16[4,36,2048]{2,1,0:T(8,128)(2,1)S(1)}, u32[]{:S(2)}, u32[]{:S(2)}) %all-to-all-start) | async-done | bytes 589856 | tf_op jit(solution)/shard_map/all_to_all | solution.py:62
  99.1 3.9 %collective-permute-start.2 = (bf16[144,2048]{1,0:T(8,128)(2,1)}, bf16[144,2048]{1,0:T(8,128)(2,1)S(1)}, u32[]{:S(2)}, u32[]{:S(2)}) collective-permute-start(bf16[144,2048]{1,0:T(8,128)(2,1)} %reshape.280), channel_id=1, source_target_pairs={{0,2},{2,4},{4,6},{6,8},{8,10},{10,12},{12,14},{14,16},{16,18},{18... | collective-permute-start | bytes 1769480 | tf_op jit(solution)/shard_map/ppermute | solution.py:20
  103.1 3.1 %collective-permute-start.9 = (bf16[144,2048]{1,0:T(8,128)(2,1)S(1)}, bf16[144,2048]{1,0:T(8,128)(2,1)S(1)}, u32[]{:S(2)}, u32[]{:S(2)}) collective-permute-start(bf16[144,2048]{1,0:T(8,128)(2,1)S(1)} %collective-permute-done.4), channel_id=1, source_target_pairs={{2,0},{4,2},{6,4},{8,6},{10,8},{12,10},{14,12},{16,14},{18,16},{20... | collective-permute-start | bytes 1769480 | tf_op jit(solution)/shard_map/ppermute | solution.py:24
  106.2 2.7 collective-permute-start.10
  109.0 6.6 %collective-permute-done.1 = bf16[144,2048]{1,0:T(8,128)(2,1)S(1)} collective-permute-done((bf16[144,2048]{1,0:T(8,128)(2,1)}, bf16[144,2048]{1,0:T(8,128)(2,1)S(1)}, u32[]{:S(2)}, u32[]{:S(2)}) %collective-permute-start.1) | collective-permute-done | bytes 589856 | tf_op jit(solution)/shard_map/ppermute | solution.py:24
  115.6 3.1 %collective-permute-start.7 = (bf16[144,2048]{1,0:T(8,128)(2,1)S(1)}, bf16[144,2048]{1,0:T(8,128)(2,1)}, u32[]{:S(2)}, u32[]{:S(2)}) collective-permute-start(bf16[144,2048]{1,0:T(8,128)(2,1)S(1)} %collective-permute-done.1), channel_id=1, source_target_pairs={{2,0},{4,2},{6,4},{8,6},{10,8},{12,10},{14,12},{16,14},{18,16},{20... | collective-permute-start | bytes 1769480 | tf_op jit(solution)/shard_map/ppermute | solution.py:24
  118.7 2.7 collective-permute-start.8
  121.5 6.8 %collective-permute-done.9 = bf16[144,2048]{1,0:T(8,128)(2,1)S(1)} collective-permute-done((bf16[144,2048]{1,0:T(8,128)(2,1)S(1)}, bf16[144,2048]{1,0:T(8,128)(2,1)S(1)}, u32[]{:S(2)}, u32[]{:S(2)}) %collective-permute-start.9) | collective-permute-done | bytes 589856 | tf_op jit(solution)/shard_map/ppermute | solution.py:24
  128.2 3.1 %collective-permute-start.13 = (bf16[144,2048]{1,0:T(8,128)(2,1)S(1)}, bf16[144,2048]{1,0:T(8,128)(2,1)}, u32[]{:S(2)}, u32[]{:S(2)}) collective-permute-start(bf16[144,2048]{1,0:T(8,128)(2,1)S(1)} %collective-permute-done.9), channel_id=1, source_target_pairs={{2,0},{4,2},{6,4},{8,6},{10,8},{12,10},{14,12},{16,14},{18,16},{20... | collective-permute-start | bytes 1769480 | tf_op jit(solution)/shard_map/ppermute | solution.py:24
  131.5 2.6 collective-permute-start.14
  134.1 5.1 %collective-permute-start.6 = (bf16[2048,256]{1,0:T(8,128)(2,1)}, bf16[2048,256]{1,0:T(8,128)(2,1)}, u32[]{:S(2)}, u32[]{:S(2)}) collective-permute-start(bf16[2048,256]{1,0:T(8,128)(2,1)} %bitcast.225), channel_id=1, source_target_pairs={{0,1},{1,0},{2,3},{3,2},{4,5},{5,4},{6,7},{7,6},{8,9},{9,8},{10,11... | collective-permute-start | bytes 3145736 | tf_op jit(solution)/shard_map/ppermute | solution.py:28
  141.0 5.1 %collective-permute-start.3 = (bf16[128,2048]{1,0:T(8,128)(2,1)}, bf16[128,2048]{1,0:T(8,128)(2,1)}, u32[]{:S(2)}, u32[]{:S(2)}) collective-permute-start(bf16[128,2048]{1,0:T(8,128)(2,1)} %bitcast.231), channel_id=1, source_target_pairs={{0,1},{1,0},{2,3},{3,2},{4,5},{5,4},{6,7},{7,6},{8,9},{9,8},{10,11... | collective-permute-start | bytes 1572872 | tf_op jit(solution)/shard_map/ppermute | solution.py:28
  146.1 3.1 %collective-permute-start.11 = (bf16[144,2048]{1,0:T(8,128)(2,1)}, bf16[144,2048]{1,0:T(8,128)(2,1)}, u32[]{:S(2)}, u32[]{:S(2)}) collective-permute-start(bf16[144,2048]{1,0:T(8,128)(2,1)} %collective-permute-done.7), channel_id=1, source_target_pairs={{2,0},{4,2},{6,4},{8,6},{10,8},{12,10},{14,12},{16,14},{18,16},{20... | collective-permute-start | bytes 1769480 | tf_op jit(solution)/shard_map/ppermute | solution.py:24
  149.2 4.4 %collective-permute-done.13 = bf16[144,2048]{1,0:T(8,128)(2,1)} collective-permute-done((bf16[144,2048]{1,0:T(8,128)(2,1)S(1)}, bf16[144,2048]{1,0:T(8,128)(2,1)}, u32[]{:S(2)}, u32[]{:S(2)}) %collective-permute-start.13) | collective-permute-done | bytes 589856 | tf_op jit(solution)/shard_map/ppermute | solution.py:24
  153.6 2.1 collective-permute-start.12
  157.6 6.1 %collective-permute-done.6 = bf16[2048,256]{1,0:T(8,128)(2,1)} collective-permute-done((bf16[2048,256]{1,0:T(8,128)(2,1)}, bf16[2048,256]{1,0:T(8,128)(2,1)}, u32[]{:S(2)}, u32[]{:S(2)}) %collective-permute-start.6) | collective-permute-done | bytes 1048608 | tf_op jit(solution)/shard_map/ppermute | solution.py:28
  179.0 2.2 fusion.24
  181.6 2.2 fusion.31
  189.8 2.8 fusion
  192.6 58.1 %all_to_all.20 = bf16[4,160,2048]{2,1,0:T(8,128)(2,1)S(1)} all-to-all(bf16[4,160,2048]{2,1,0:T(8,128)(2,1)S(1)} %bitcast.203), channel_id=1, replica_groups=mesh['ylo'=2,'x'=4,'core'=2,'zb'=4,'zo'=4,'yh'=2] {'zo'}, dimensions={0} | all-to-all | bytes 5242880 | tf_op jit(solution)/shard_map/all_to_all | solution.py:120
  252.2 6.9 %all-to-all-start.3 = ((bf16[4,40,2048]{2,1,0:T(8,128)(2,1)}), bf16[4,40,2048]{2,1,0:T(8,128)(2,1)S(1)}, u32[]{:S(2)}, u32[]{:S(2)}) async-start(bf16[4,40,2048]{2,1,0:T(8,128)(2,1)} %bitcast.204), calls=%async_computation.3 | async-start | bytes 1310720 | tf_op jit(solution)/shard_map/all_to_all | solution.py:122
  259.2 2.9 convolution_convert_fusion
  262.1 5.1 %collective-permute-start.15 = (bf16[2048,256]{1,0:T(8,128)(2,1)S(1)}, bf16[2048,256]{1,0:T(8,128)(2,1)S(1)}, u32[]{:S(2)}, u32[]{:S(2)}) collective-permute-start(bf16[2048,256]{1,0:T(8,128)(2,1)S(1)} %convolution_convert_fusion), channel_id=1, source_target_pairs={{0,1},{1,0},{2,3},{3,2},{4,5},{5,4},{6,7},{7,6},{8,9},{9,8},{10,11... | collective-permute-start | bytes 3145736 | tf_op jit(solution)/shard_map/ppermute | solution.py:28
  269.0 2.2 collective-permute-start.16
  271.4 26.6 %collective-permute-done.16 = bf16[128,2048]{1,0:T(8,128)(2,1)S(1)} collective-permute-done((bf16[128,2048]{1,0:T(8,128)(2,1)S(1)}, bf16[128,2048]{1,0:T(8,128)(2,1)S(1)}, u32[]{:S(2)}, u32[]{:S(2)}) %collective-permute-start.16) | collective-permute-done | bytes 524320 | tf_op jit(solution)/shard_map/ppermute | solution.py:28
  298.0 2.5 fusion.5
  300.5 3.2 %fusion.2 = bf16[1,1,2048,256]{3,2,1,0:T(8,128)(2,1)} fusion(bf16[2048,256]{1,0:T(8,128)(2,1)S(1)} %collective-permute-done.15, bf16[144,2048]{1,0:T(8,128)(2,1)S(1)} %copy-done.8, bf16[144,2048]{1,0:T(8,128)(2,1)S(1)} %copy-done.6, bf16[144,2048]{1,0:T(8,128)(2,1)S(1)} %copy-done.10, bf16[144,2048]{1,0:T(8,128)(2,1)} %reshape.282, ...), kind=kOutput, calls=%fused_computation.7 | convolution fusion | flops 614989824 | bytes 4751360 | tf_op jit(solution)/shard_map/dot_general | solution.py:16
  (161 shorter events, 43.5 us)
Async XLA Ops:
  0.6 18.5 %copy-start.33 = (bf16[128,2048]{1,0:T(8,128)(2,1)S(1)}, bf16[128,2048]{1,0:T(8,128)(2,1)}, u32[]{:S(2)}) copy-start(bf16[128,2048]{1,0:T(8,128)(2,1)} %param.8) | copy-start | bytes 1572868
  0.7 20.5 %copy-start.36 = (bf16[128,1]{0,1:T(2,128)(2,1)S(1)}, bf16[128,1]{0,1:T(2,128)(2,1)}, u32[]{:S(2)}) copy-start(bf16[128,1]{0,1:T(2,128)(2,1)} %param.10) | copy-start | bytes 772
  4.1 52.9 %all-to-all-start.1 = ((bf16[4,36,2048]{2,1,0:T(8,128)(2,1)}), bf16[4,36,2048]{2,1,0:T(8,128)(2,1)S(1)}, u32[]{:S(2)}, u32[]{:S(2)}) async-start(bf16[4,36,2048]{2,1,0:T(8,128)(2,1)} %reshape.281), calls=%async_computation.1 | async-start | bytes 1310720 | tf_op jit(solution)/shard_map/all_to_all | solution.py:62
  19.2 8.6 %collective-permute-start = (bf16[128,2048]{1,0:T(8,128)(2,1)S(1)}, bf16[128,2048]{1,0:T(8,128)(2,1)S(1)}, u32[]{:S(2)}, u32[]{:S(2)}) collective-permute-start(bf16[128,2048]{1,0:T(8,128)(2,1)S(1)} %copy-done.33), channel_id=1, source_target_pairs={{0,480},{32,0},{64,32},{96,64},{128,96},{160,128},{192,160},{224,1... | collective-permute-start | bytes 1572872 | tf_op jit(solution)/shard_map/ppermute | solution.py:44
  57.1 39.2 %all-to-all-start = ((bf16[4,36,2048]{2,1,0:T(8,128)(2,1)}), bf16[4,36,2048]{2,1,0:T(8,128)(2,1)S(1)}, u32[]{:S(2)}, u32[]{:S(2)}) async-start(bf16[4,36,2048]{2,1,0:T(8,128)(2,1)} %reshape.279), calls=%async_computation | async-start | bytes 1310720 | tf_op jit(solution)/shard_map/all_to_all | solution.py:62
  61.5 41.6 %collective-permute-start.4 = (bf16[144,2048]{1,0:T(8,128)(2,1)}, bf16[144,2048]{1,0:T(8,128)(2,1)S(1)}, u32[]{:S(2)}, u32[]{:S(2)}) collective-permute-start(bf16[144,2048]{1,0:T(8,128)(2,1)} %reshape.282), channel_id=1, source_target_pairs={{2,0},{4,2},{6,4},{8,6},{10,8},{12,10},{14,12},{16,14},{18,16},{20... | collective-permute-start | bytes 1769480 | tf_op jit(solution)/shard_map/ppermute | solution.py:24
  67.9 38.3 %collective-permute-start.5 = (bf16[144,2048]{1,0:T(8,128)(2,1)}, bf16[144,2048]{1,0:T(8,128)(2,1)}, u32[]{:S(2)}, u32[]{:S(2)}) collective-permute-start(bf16[144,2048]{1,0:T(8,128)(2,1)} %reshape.282), channel_id=1, source_target_pairs={{0,2},{2,4},{4,6},{6,8},{8,10},{10,12},{12,14},{14,16},{16,18},{18... | collective-permute-start | bytes 1769480 | tf_op jit(solution)/shard_map/ppermute | solution.py:20
  97.2 18.4 %collective-permute-start.1 = (bf16[144,2048]{1,0:T(8,128)(2,1)}, bf16[144,2048]{1,0:T(8,128)(2,1)S(1)}, u32[]{:S(2)}, u32[]{:S(2)}) collective-permute-start(bf16[144,2048]{1,0:T(8,128)(2,1)} %reshape.280), channel_id=1, source_target_pairs={{2,0},{4,2},{6,4},{8,6},{10,8},{12,10},{14,12},{16,14},{18,16},{20... | collective-permute-start | bytes 1769480 | tf_op jit(solution)/shard_map/ppermute | solution.py:24
  99.1 19.6 %collective-permute-start.2 = (bf16[144,2048]{1,0:T(8,128)(2,1)}, bf16[144,2048]{1,0:T(8,128)(2,1)S(1)}, u32[]{:S(2)}, u32[]{:S(2)}) collective-permute-start(bf16[144,2048]{1,0:T(8,128)(2,1)} %reshape.280), channel_id=1, source_target_pairs={{0,2},{2,4},{4,6},{6,8},{8,10},{10,12},{12,14},{14,16},{16,18},{18... | collective-permute-start | bytes 1769480 | tf_op jit(solution)/shard_map/ppermute | solution.py:20
  103.1 52.6 %copy-start.19 = (bf16[144,2048]{1,0:T(8,128)(2,1)}, bf16[144,2048]{1,0:T(8,128)(2,1)S(1)}, u32[]{:S(2)}) copy-start(bf16[144,2048]{1,0:T(8,128)(2,1)S(1)} %collective-permute-done.4) | copy-start | bytes 1769476
  103.1 25.1 %collective-permute-start.9 = (bf16[144,2048]{1,0:T(8,128)(2,1)S(1)}, bf16[144,2048]{1,0:T(8,128)(2,1)S(1)}, u32[]{:S(2)}, u32[]{:S(2)}) collective-permute-start(bf16[144,2048]{1,0:T(8,128)(2,1)S(1)} %collective-permute-done.4), channel_id=1, source_target_pairs={{2,0},{4,2},{6,4},{8,6},{10,8},{12,10},{14,12},{16,14},{18,16},{20... | collective-permute-start | bytes 1769480 | tf_op jit(solution)/shard_map/ppermute | solution.py:24
  106.2 25.2 %collective-permute-start.10 = (bf16[144,2048]{1,0:T(8,128)(2,1)}, bf16[144,2048]{1,0:T(8,128)(2,1)}, u32[]{:S(2)}, u32[]{:S(2)}) collective-permute-start(bf16[144,2048]{1,0:T(8,128)(2,1)} %collective-permute-done.5), channel_id=1, source_target_pairs={{0,2},{2,4},{4,6},{6,8},{8,10},{10,12},{12,14},{14,16},{16,18},{18... | collective-permute-start | bytes 1769480 | tf_op jit(solution)/shard_map/ppermute | solution.py:20
  115.6 25.4 %collective-permute-start.7 = (bf16[144,2048]{1,0:T(8,128)(2,1)S(1)}, bf16[144,2048]{1,0:T(8,128)(2,1)}, u32[]{:S(2)}, u32[]{:S(2)}) collective-permute-start(bf16[144,2048]{1,0:T(8,128)(2,1)S(1)} %collective-permute-done.1), channel_id=1, source_target_pairs={{2,0},{4,2},{6,4},{8,6},{10,8},{12,10},{14,12},{16,14},{18,16},{20... | collective-permute-start | bytes 1769480 | tf_op jit(solution)/shard_map/ppermute | solution.py:24
  118.7 37.0 %copy-start.17 = (bf16[144,2048]{1,0:T(8,128)(2,1)}, bf16[144,2048]{1,0:T(8,128)(2,1)S(1)}, u32[]{:S(2)}) copy-start(bf16[144,2048]{1,0:T(8,128)(2,1)S(1)} %collective-permute-done.2) | copy-start | bytes 1769476
  118.7 27.3 %collective-permute-start.8 = (bf16[144,2048]{1,0:T(8,128)(2,1)S(1)}, bf16[144,2048]{1,0:T(8,128)(2,1)}, u32[]{:S(2)}, u32[]{:S(2)}) collective-permute-start(bf16[144,2048]{1,0:T(8,128)(2,1)S(1)} %collective-permute-done.2), channel_id=1, source_target_pairs={{0,2},{2,4},{4,6},{6,8},{8,10},{10,12},{12,14},{14,16},{16,18},{18... | collective-permute-start | bytes 1769480 | tf_op jit(solution)/shard_map/ppermute | solution.py:20
  128.2 27.5 %copy-start.20 = (bf16[144,2048]{1,0:T(8,128)(2,1)}, bf16[144,2048]{1,0:T(8,128)(2,1)S(1)}, u32[]{:S(2)}) copy-start(bf16[144,2048]{1,0:T(8,128)(2,1)S(1)} %collective-permute-done.9) | copy-start | bytes 1769476
  128.2 25.4 %collective-permute-start.13 = (bf16[144,2048]{1,0:T(8,128)(2,1)S(1)}, bf16[144,2048]{1,0:T(8,128)(2,1)}, u32[]{:S(2)}, u32[]{:S(2)}) collective-permute-start(bf16[144,2048]{1,0:T(8,128)(2,1)S(1)} %collective-permute-done.9), channel_id=1, source_target_pairs={{2,0},{4,2},{6,4},{8,6},{10,8},{12,10},{14,12},{16,14},{18,16},{20... | collective-permute-start | bytes 1769480 | tf_op jit(solution)/shard_map/ppermute | solution.py:24
  131.5 24.3 %collective-permute-start.14 = (bf16[144,2048]{1,0:T(8,128)(2,1)}, bf16[144,2048]{1,0:T(8,128)(2,1)}, u32[]{:S(2)}, u32[]{:S(2)}) collective-permute-start(bf16[144,2048]{1,0:T(8,128)(2,1)} %collective-permute-done.10), channel_id=1, source_target_pairs={{0,2},{2,4},{4,6},{6,8},{8,10},{10,12},{12,14},{14,16},{16,18},{18... | collective-permute-start | bytes 1769480 | tf_op jit(solution)/shard_map/ppermute | solution.py:20
  134.1 29.5 %collective-permute-start.6 = (bf16[2048,256]{1,0:T(8,128)(2,1)}, bf16[2048,256]{1,0:T(8,128)(2,1)}, u32[]{:S(2)}, u32[]{:S(2)}) collective-permute-start(bf16[2048,256]{1,0:T(8,128)(2,1)} %bitcast.225), channel_id=1, source_target_pairs={{0,1},{1,0},{2,3},{3,2},{4,5},{5,4},{6,7},{7,6},{8,9},{9,8},{10,11... | collective-permute-start | bytes 3145736 | tf_op jit(solution)/shard_map/ppermute | solution.py:28
  140.5 23.1 %copy-start.31 = (bf16[1,1,2048,256]{3,2,1,0:T(8,128)(2,1)S(1)}, bf16[1,1,2048,256]{3,2,1,0:T(8,128)(2,1)}, u32[]{:S(2)}) copy-start(bf16[1,1,2048,256]{3,2,1,0:T(8,128)(2,1)} %param.11) | copy-start | bytes 3145732
  141.0 35.1 %collective-permute-start.3 = (bf16[128,2048]{1,0:T(8,128)(2,1)}, bf16[128,2048]{1,0:T(8,128)(2,1)}, u32[]{:S(2)}, u32[]{:S(2)}) collective-permute-start(bf16[128,2048]{1,0:T(8,128)(2,1)} %bitcast.231), channel_id=1, source_target_pairs={{0,1},{1,0},{2,3},{3,2},{4,5},{5,4},{6,7},{7,6},{8,9},{9,8},{10,11... | collective-permute-start | bytes 1572872 | tf_op jit(solution)/shard_map/ppermute | solution.py:28
  146.1 28.3 %collective-permute-start.11 = (bf16[144,2048]{1,0:T(8,128)(2,1)}, bf16[144,2048]{1,0:T(8,128)(2,1)}, u32[]{:S(2)}, u32[]{:S(2)}) collective-permute-start(bf16[144,2048]{1,0:T(8,128)(2,1)} %collective-permute-done.7), channel_id=1, source_target_pairs={{2,0},{4,2},{6,4},{8,6},{10,8},{12,10},{14,12},{16,14},{18,16},{20... | collective-permute-start | bytes 1769480 | tf_op jit(solution)/shard_map/ppermute | solution.py:24
  153.6 20.7 %collective-permute-start.12 = (bf16[144,2048]{1,0:T(8,128)(2,1)}, bf16[144,2048]{1,0:T(8,128)(2,1)}, u32[]{:S(2)}, u32[]{:S(2)}) collective-permute-start(bf16[144,2048]{1,0:T(8,128)(2,1)} %collective-permute-done.8), channel_id=1, source_target_pairs={{0,2},{2,4},{4,6},{6,8},{8,10},{10,12},{12,14},{14,16},{16,18},{18... | collective-permute-start | bytes 1769480 | tf_op jit(solution)/shard_map/ppermute | solution.py:20
  157.6 11.2 %copy-start.5 = (bf16[144,2048]{1,0:T(8,128)(2,1)}, bf16[144,2048]{1,0:T(8,128)(2,1)S(1)}, u32[]{:S(2)}) copy-start(bf16[144,2048]{1,0:T(8,128)(2,1)S(1)} %get-tuple-element.21) | copy-start | bytes 1769476
  157.6 13.5 %copy-start.7 = (bf16[144,2048]{1,0:T(8,128)(2,1)}, bf16[144,2048]{1,0:T(8,128)(2,1)S(1)}, u32[]{:S(2)}) copy-start(bf16[144,2048]{1,0:T(8,128)(2,1)S(1)} %get-tuple-element.23) | copy-start | bytes 1769476
  252.2 51.5 %all-to-all-start.3 = ((bf16[4,40,2048]{2,1,0:T(8,128)(2,1)}), bf16[4,40,2048]{2,1,0:T(8,128)(2,1)S(1)}, u32[]{:S(2)}, u32[]{:S(2)}) async-start(bf16[4,40,2048]{2,1,0:T(8,128)(2,1)} %bitcast.204), calls=%async_computation.3 | async-start | bytes 1310720 | tf_op jit(solution)/shard_map/all_to_all | solution.py:122
  262.1 38.4 %collective-permute-start.15 = (bf16[2048,256]{1,0:T(8,128)(2,1)S(1)}, bf16[2048,256]{1,0:T(8,128)(2,1)S(1)}, u32[]{:S(2)}, u32[]{:S(2)}) collective-permute-start(bf16[2048,256]{1,0:T(8,128)(2,1)S(1)} %convolution_convert_fusion), channel_id=1, source_target_pairs={{0,1},{1,0},{2,3},{3,2},{4,5},{5,4},{6,7},{7,6},{8,9},{9,8},{10,11... | collective-permute-start | bytes 3145736 | tf_op jit(solution)/shard_map/ppermute | solution.py:28
  269.0 29.0 %collective-permute-start.16 = (bf16[128,2048]{1,0:T(8,128)(2,1)S(1)}, bf16[128,2048]{1,0:T(8,128)(2,1)S(1)}, u32[]{:S(2)}, u32[]{:S(2)}) collective-permute-start(bf16[128,2048]{1,0:T(8,128)(2,1)S(1)} %convolution_convert_fusion.3), channel_id=1, source_target_pairs={{0,1},{1,0},{2,3},{3,2},{4,5},{5,4},{6,7},{7,6},{8,9},{9,8},{10,11... | collective-permute-start | bytes 1572872 | tf_op jit(solution)/shard_map/ppermute | solution.py:28
  271.4 29.1 %copy-start.4 = (bf16[4,144,512]{2,1,0:T(8,128)(2,1)S(1)}, bf16[4,144,512]{2,1,0:T(8,128)(2,1)}, u32[]{:S(2)}) copy-start(bf16[4,144,512]{2,1,0:T(8,128)(2,1)} %copy-done.3) | copy-start | bytes 1769476
  271.4 29.1 %copy-start.6 = (bf16[144,2048]{1,0:T(8,128)(2,1)S(1)}, bf16[144,2048]{1,0:T(8,128)(2,1)}, u32[]{:S(2)}) copy-start(bf16[144,2048]{1,0:T(8,128)(2,1)} %copy-done.5) | copy-start | bytes 1769476
  271.4 29.1 %copy-start.8 = (bf16[144,2048]{1,0:T(8,128)(2,1)S(1)}, bf16[144,2048]{1,0:T(8,128)(2,1)}, u32[]{:S(2)}) copy-start(bf16[144,2048]{1,0:T(8,128)(2,1)} %copy-done.7) | copy-start | bytes 1769476
  271.4 29.1 %copy-start.10 = (bf16[144,2048]{1,0:T(8,128)(2,1)S(1)}, bf16[144,2048]{1,0:T(8,128)(2,1)}, u32[]{:S(2)}) copy-start(bf16[144,2048]{1,0:T(8,128)(2,1)} %copy-done.9) | copy-start | bytes 1769476
  (26 other events, 106.7 us)

commit v4 on v3

v4 whole, which is shorter than its diff:
```python
import functools

import jax
import jax.numpy as jnp
from jax import lax
from jax.experimental import pallas as pl
from jax.experimental.pallas import tpu as pltpu
from jax.sharding import Mesh, PartitionSpec as P

EXPERTS = 4
SECTION = ("ylo", "x", "core")
AXES = ("ylo", "x", "core", "zb", "zo", "yh")
RING = 16
LINE = 4
LANES = 256
BF = jnp.bfloat16
F32 = jnp.float32


def dot(a, b, ca, cb):
    return lax.dot_general(a, b, (((ca,), (cb,)), ((), ())), preferred_element_type=F32)


def up(a):
    return lax.ppermute(a, ("zb", "zo"), [(i, (i + 1) % RING) for i in range(RING)])


def down(a):
    return lax.ppermute(a, ("zb", "zo"), [((i + 1) % RING, i) for i in range(RING)])


def line(a, *pairs):
    return lax.ppermute(a, "zo", pairs)


def across(a):
    return lax.ppermute(a, "yh", [(0, 1), (1, 0)])


def after(a, *others):
    return lax.optimization_barrier((a, *others))[0]


def slice_kernel(cap, zo_ref, gu_ref, g_ref, w_ref, wd_ref, own_ref, other_ref, h_ref, dx_ref):
    rows, hid2 = h_ref.shape
    hidden = hid2 // 2
    padded, width = dx_ref.shape
    pitch = padded // EXPERTS
    gate, upper = gu_ref[:, :hid2], gu_ref[:, hid2:]
    draw = dot(g_ref[...], wd_ref[...], 1, 1)
    sig = jax.nn.sigmoid(gate)
    act = gate * sig
    hid = act * upper
    h_ref[...] = hid.astype(BF)
    dgate = (draw * upper * sig * (1.0 + gate * (1.0 - sig))).astype(BF)
    dupper = (draw * act).astype(BF)
    own_ref[:, :hidden] = dgate[:, :hidden]
    own_ref[:, hidden:] = dupper[:, :hidden]
    other_ref[:, :hidden] = dgate[:, hidden:]
    other_ref[:, hidden:] = dupper[:, hidden:]
    to = lax.broadcasted_iota(jnp.int32, (padded, rows), 0)
    of = lax.broadcasted_iota(jnp.int32, (padded, rows), 1)
    pick = ((to // pitch * cap + to % pitch == of) & (to % pitch < cap)).astype(BF)
    dgu = jnp.concatenate([dgate, dupper], axis=1)
    dgu = dot(pick, dgu, 1, 0).astype(BF)
    dx = dot(dgu, w_ref[...], 1, 1)
    line = lax.dot_general(
        jnp.ones((8, hid2), F32),
        hid * draw,
        (((1,), (1,)), ((), ())),
        preferred_element_type=F32,
        precision=lax.Precision.HIGHEST,
    )
    line = jnp.concatenate([line, jnp.zeros((8, LANES - rows), F32)], axis=1)
    line = jnp.concatenate([line] * (width // LANES), axis=1)[:1]
    lane = lax.broadcasted_iota(jnp.int32, (1, width), 1)
    line = jnp.where(lane // LANES == zo_ref[0], line, 0.0)
    row = lax.broadcasted_iota(jnp.int32, (padded, width), 0)
    dx_ref[...] = jnp.where(row % pitch == cap, line, dx).astype(BF)


def slice_backward(cap, zo, gu, g, w, wd):
    rows, width = g.shape
    hid2 = wd.shape[0]
    whole = pl.BlockSpec(memory_space=pltpu.VMEM)
    return pl.pallas_call(
        functools.partial(slice_kernel, cap),
        out_shape=(
            jax.ShapeDtypeStruct((rows, hid2), BF),
            jax.ShapeDtypeStruct((rows, hid2), BF),
            jax.ShapeDtypeStruct((rows, hid2), BF),
            jax.ShapeDtypeStruct((EXPERTS * (cap + 4), width), BF),
        ),
        in_specs=[pl.BlockSpec(memory_space=pltpu.SMEM)] + [whole] * 4,
        out_specs=(whole,) * 4,
        compiler_params=pltpu.CompilerParams(vmem_limit_bytes=32 * 2**20),
        cost_estimate=pl.CostEstimate(
            flops=2 * rows * width * 3 * hid2, bytes_accessed=5 * 2**20, transcendentals=0
        ),
    )(zo, gu, g, w, wd)


def per_device(tokens, upstream, expert_ids, combine, w_gate_up, w_down):
    tok, width = tokens.shape
    cap = tok * 9 // (8 * EXPERTS)
    pitch = cap + 4
    wgu = w_gate_up[0, 0]
    wdown = w_down[0, 0]
    hidden = wdown.shape[0]
    zb, zo = lax.axis_index("zb"), lax.axis_index("zo")
    sections = lax.axis_size(SECTION)
    out_grad = lax.ppermute(
        upstream, SECTION, [(i, (i - 1) % sections) for i in range(sections)]
    )

    ids = expert_ids[:, 0]
    onehot = (ids[:, None] == jnp.arange(EXPERTS, dtype=jnp.int32)[None, :]).astype(F32)
    earlier = (jnp.arange(tok)[:, None] > jnp.arange(tok)[None, :]).astype(F32)
    before = dot(earlier, onehot, 1, 0)
    slot = jnp.sum(before * onehot, axis=1).astype(jnp.int32)
    weight = combine.astype(F32)
    scaled = (weight * out_grad.astype(F32)).astype(BF)
    place = (
        jnp.arange(EXPERTS * cap, dtype=jnp.int32)[:, None]
        == (ids * cap + slot)[None, :]
    ).astype(BF)

    def to_blocks(a):
        sent = dot(place, a, 1, 0).astype(BF).reshape(EXPERTS, cap, width)
        unit = lax.all_to_all(sent, "zb", 0, 0, tiled=True)
        return unit.reshape(EXPERTS * cap, width)

    where = jnp.where
    first, last, odd = zo == 0, zo == 3, (zo % 2) == 1

    def relay(unit):
        r1, l1 = up(unit), down(unit)
        r2, l2 = up(r1), down(l1)
        r3, l3 = line(r2, (2, 3)), line(l2, (1, 0))
        early = where(odd, l1, r1)
        whole = lambda *others: where(
            first, after(l3, *others), where(last, after(r3, *others), early)
        )
        return [unit, where(odd, r1, l1), early, where(zo < 2, l2, r2)], whole

    unit_x = to_blocks(tokens)
    unit_g = to_blocks(scaled)
    wgu_other, wdown_other = across(wgu), across(wdown)
    unit_x, wgu_other = lax.optimization_barrier((unit_x, wgu_other))
    unit_g, wdown_other = lax.optimization_barrier((unit_g, wdown_other))
    parts = [a[:, k : k + hidden] for k in (0, hidden) for a in (wgu, wgu_other)]
    wgu_all = jnp.concatenate(parts, axis=1)
    wdown_all = jnp.concatenate([wdown, wdown_other], axis=0)
    (xs, x3), (gs, g3) = relay(unit_x), relay(unit_g)

    forward = lambda x: dot(x, wgu_all, 1, 0)
    expert = lambda gu, g: slice_backward(cap, zo[None], gu, g, wgu_all, wdown_all)
    gus = [forward(after(xs[k], xs[l])) for k, l in ((0, 1), (1, 3), (2, 3))]
    x3 = x3(*gus)
    gus.append(forward(after(xs[3], gs[1])))
    gu3 = forward(x3)
    early = (xs[3], xs[3], xs[3], gs[3])
    done = [expert(gu, after(g, e)) for gu, g, e in zip(gus, gs, early)]

    add = lambda *terms: sum(a.astype(F32) for a in terms).astype(BF)
    d0, d1, d3_early, d2 = (d[3] for d in done)
    near = line(d1, (0, 1), (3, 2))
    r2, l2 = line(d2, (0, 1), (1, 2)), line(d2, (3, 2), (2, 1))
    to_r1 = add(where(zo == 1, d3_early, d1), r2)
    to_l1 = add(where(zo == 2, d3_early, d1), l2)
    r1, l1 = line(to_r1, (1, 2), (2, 3)), line(to_l1, (2, 1), (1, 0))
    g3 = g3(to_r1, to_l1, gu3)
    done[2] = expert(gu3, g3)
    far = line(done[2][3], (0, 3), (3, 0))
    own, other, hids, _ = zip(*(done[k] for k in (0, 1, 3, 2)))

    cat = lambda arrays: jnp.concatenate(arrays, axis=0)
    x_all, g_all = cat([xs[0], xs[1], xs[3], x3]), cat([gs[0], gs[1], gs[3], g3])
    hid_all = cat(hids)
    other_gu = dot(x_all, cat(other), 0, 0).astype(BF)
    other_down = dot(hid_all[:, hidden:], g_all, 0, 0).astype(BF)

    dx = add(d0, near, r1, l1, after(far, other_gu, other_down))
    dx = dx.reshape(EXPERTS, pitch, width)
    back = lax.all_to_all(dx, "zb", 0, 0, tiled=True).reshape(-1, width)
    other_gu, other_down = across(other_gu), across(other_down)
    grad_gu = (dot(x_all, cat(own), 0, 0) + other_gu.astype(F32)).astype(BF)
    grad_down = dot(hid_all[:, :hidden], g_all, 0, 0) + other_down.astype(F32)
    grad_down = grad_down.astype(BF)
    back, grad_gu, grad_down = lax.optimization_barrier((back, grad_gu, grad_down))

    put = (
        jnp.arange(EXPERTS * pitch, dtype=jnp.int32)[:, None]
        == (ids * pitch + slot)[None, :]
    ).astype(BF)
    moe = dot(put, back, 0, 0)
    input_grad = (out_grad.astype(F32) + moe).astype(BF)
    dp = back.reshape(EXPERTS, pitch, width)[:, cap, : LINE * LANES].astype(F32)
    dp = jnp.sum(dp.reshape(EXPERTS, LINE, LANES), axis=1)
    pick = (ids[:, None] == jnp.arange(EXPERTS)[None, :])[:, :, None] & (
        (zb * cap + slot)[:, None] == jnp.arange(LANES)[None, :]
    )[:, None, :]
    dp = jnp.sum(jnp.where(pick, dp[None], 0.0), axis=(1, 2))
    combine_grad = (dp[:, None] / weight).astype(BF)

    return (input_grad, combine_grad, grad_gu[None, None], grad_down[None, None])


def solution(mesh):
    fine = Mesh(mesh.devices.reshape(2, 4, 2, 4, 4, 2), AXES)
    row = P(AXES, None)
    weights = P(SECTION, ("zb", "zo", "yh"), None, None)
    return jax.shard_map(
        per_device,
        mesh=fine,
        in_specs=(row, row, row, row, weights, weights),
        out_specs=(row, row, weights, weights),
        check_vma=False,
    )
```

time: 307 us -> 260 us (0.85)
  blocking collectives: 58.1 us -> 0 us
  matrix products: 31.7 us -> 16.5 us
  starting transfers between devices: 81.8 us -> 95.4 us
  Pallas kernels: 0 us -> 9.47 us
  waiting for transfers between devices: 111 us -> 119 us
  local copies, waits for them, and re-layouts: 12 us -> 7.35 us
    all_to_all x1 -> x0, blocking collectives: 58.1 us -> none  [per_device(): dx = lax.all_to_all(dx, 'zo', 0, 0, tiled=True)]
    ppermute x0 -> x10, waiting for transfers between devices: none -> 32.3 us  [line(): return lax.ppermute(a, 'zo', pairs)]
    ppermute x0 -> x10, starting transfers between devices: none -> 16.9 us  [line(): return lax.ppermute(a, 'zo', pairs)]
    dot_general x17 -> x13, matrix products: 31.7 us -> 16.5 us  [dot(): lax.dot_general(a, b, (((ca,), (cb,)), ((), ())), preferred_element_type=...]
    ppermute x6 -> x4, waiting for transfers between devices: 18.3 us -> 5.32 us  [down(): lax.ppermute(a, ('zb', 'zo'), [((i + 1) % RING, i) for i in range(RING)])]
    all_to_all x2, waiting for transfers between devices: 53.5 us -> 41.3 us  [to_blocks(): unit = lax.all_to_all(sent, 'zb', 0, 0, tiled=True)]
    pallas_call x0 -> x5, Pallas kernels: none -> 9.47 us  [slice_backward(): pl.pallas_call(functools.partial(slice_kernel, cap), out_shape=(jax.Shape...]
    ppermute x6 -> x4, starting transfers between devices: 16 us -> 8.04 us  [up(): lax.ppermute(a, ('zb', 'zo'), [(i, (i + 1) % RING) for i in range(RING)])]
  transfers between devices with their start and end apart: 20 -> 26, of which waited for: 10 -> 12; matrix products, arithmetic and copies ran while one was open for 9% -> 9% of each run, Pallas kernels for 0% -> 4%
where the time goes in v4:
time: 260 us; the launch traced here: 256 us
  waiting for transfers between devices  119 us (46%)
  starting transfers between devices  95.4 us (37%)
  matrix products  16.5 us (6%)
  Pallas kernels  9.47 us (4%)
  other arithmetic  7.67 us (3%)
  local copies, waits for them, and re-layouts  7.35 us (3%)
    all_to_all x2, waiting for transfers between devices, to_blocks(): unit = lax.all_to_all(sent, 'zb', 0, 0, tiled=True)  41.3 us
    ppermute x10, waiting for transfers between devices, line(): return lax.ppermute(a, 'zo', pairs)  32.3 us
    ppermute x4, waiting for transfers between devices, across(): return lax.ppermute(a, 'yh', [(0, 1), (1, 0)])  31.5 us
    ppermute x4, starting transfers between devices, down(): lax.ppermute(a, ('zb', 'zo'), [((i + 1) % RING, i) for i in range(RING)])  20.8 us
    all_to_all x2, starting transfers between devices, to_blocks(): unit = lax.all_to_all(sent, 'zb', 0, 0, tiled=True)  19.3 us
    ppermute x4, starting transfers between devices, across(): return lax.ppermute(a, 'yh', [(0, 1), (1, 0)])  17.5 us
    ppermute x10, starting transfers between devices, line(): return lax.ppermute(a, 'zo', pairs)  16.9 us
    dot_general x13, matrix products, dot(): lax.dot_general(a, b, (((ca,), (cb,)), ((), ())), preferred_element_type=...  16.5 us
  transfers between devices with their start and end apart: 26, of which 12 were waited for; matrix products, arithmetic and copies ran while one was open for 9% of the time, Pallas kernels for 4%

profile of v4, /device:TPU:6, one launch (start us, length us, event | category | flops | bytes accessed | tf_op | source)
XLA Modules:
  0.0 256.4 jit_solution(2440757294042241974)
XLA Ops:
  3.6 15.1 %all-to-all-start = ((bf16[4,36,2048]{2,1,0:T(8,128)(2,1)}), bf16[4,36,2048]{2,1,0:T(8,128)(2,1)S(1)}, u32[]{:S(2)}, u32[]{:S(2)}) async-start(bf16[4,36,2048]{2,1,0:T(8,128)(2,1)} %reshape.94), calls=%async_computation | async-start | bytes 1310720 | tf_op jit(solution)/shard_map/all_to_all | solution.py:130
  18.7 1.9 collective-permute-start
  20.6 5.1 %collective-permute-start.1 = (bf16[2048,256]{1,0:T(8,128)(2,1)S(1)}, bf16[2048,256]{1,0:T(8,128)(2,1)}, u32[]{:S(2)}, u32[]{:S(2)}) collective-permute-start(bf16[2048,256]{1,0:T(8,128)(2,1)S(1)} %bitcast.30), channel_id=1, source_target_pairs={{0,1},{1,0},{2,3},{3,2},{4,5},{5,4},{6,7},{7,6},{8,9},{9,8},{10,11... | collective-permute-start | bytes 3145736 | tf_op jit(solution)/shard_map/ppermute | solution.py:37
  29.5 27.1 %all-to-all-done = bf16[4,36,2048]{2,1,0:T(8,128)(2,1)S(1)} async-done(((bf16[4,36,2048]{2,1,0:T(8,128)(2,1)}), bf16[4,36,2048]{2,1,0:T(8,128)(2,1)S(1)}, u32[]{:S(2)}, u32[]{:S(2)}) %all-to-all-start) | async-done | bytes 589856 | tf_op jit(solution)/shard_map/all_to_all | solution.py:130
  56.5 4.2 %all-to-all-start.1 = ((bf16[4,36,2048]{2,1,0:T(8,128)(2,1)}), bf16[4,36,2048]{2,1,0:T(8,128)(2,1)}, u32[]{:S(2)}, u32[]{:S(2)}) async-start(bf16[4,36,2048]{2,1,0:T(8,128)(2,1)} %reshape.96), calls=%async_computation.1 | async-start | bytes 1310720 | tf_op jit(solution)/shard_map/all_to_all | solution.py:130
  60.7 5.1 %collective-permute-start.4 = (bf16[128,2048]{1,0:T(8,128)(2,1)}, bf16[128,2048]{1,0:T(8,128)(2,1)}, u32[]{:S(2)}, u32[]{:S(2)}) collective-permute-start(bf16[128,2048]{1,0:T(8,128)(2,1)} %bitcast.4), channel_id=1, source_target_pairs={{0,1},{1,0},{2,3},{3,2},{4,5},{5,4},{6,7},{7,6},{8,9},{9,8},{10,11... | collective-permute-start | bytes 1572872 | tf_op jit(solution)/shard_map/ppermute | solution.py:37
  67.8 6.5 %collective-permute-start.3 = (bf16[144,2048]{1,0:T(8,128)(2,1)}, bf16[144,2048]{1,0:T(8,128)(2,1)}, u32[]{:S(2)}, u32[]{:S(2)}) collective-permute-start(bf16[144,2048]{1,0:T(8,128)(2,1)} %reshape.95), channel_id=1, source_target_pairs={{2,0},{4,2},{6,4},{8,6},{10,8},{12,10},{14,12},{16,14},{18,16},{20... | collective-permute-start | bytes 1769480 | tf_op jit(solution)/shard_map/ppermute | solution.py:29
  74.4 1.9 collective-permute-start.2
  77.9 14.2 %all-to-all-done.1 = bf16[4,36,2048]{2,1,0:T(8,128)(2,1)} async-done(((bf16[4,36,2048]{2,1,0:T(8,128)(2,1)}), bf16[4,36,2048]{2,1,0:T(8,128)(2,1)}, u32[]{:S(2)}, u32[]{:S(2)}) %all-to-all-start.1) | async-done | bytes 589856 | tf_op jit(solution)/shard_map/all_to_all | solution.py:130
  93.3 5.1 %collective-permute-start.8 = (bf16[144,2048]{1,0:T(8,128)(2,1)S(1)}, bf16[144,2048]{1,0:T(8,128)(2,1)S(1)}, u32[]{:S(2)}, u32[]{:S(2)}) collective-permute-start(bf16[144,2048]{1,0:T(8,128)(2,1)S(1)} %reshape.97.g_ref), channel_id=1, source_target_pairs={{2,0},{4,2},{6,4},{8,6},{10,8},{12,10},{14,12},{16,14},{18,16},{20... | collective-permute-start | bytes 1769480 | tf_op jit(solution)/shard_map/ppermute | solution.py:29
  98.4 1.9 collective-permute-start.7
  104.6 3.6 %collective-permute-start.5 = (bf16[144,2048]{1,0:T(8,128)(2,1)}, bf16[144,2048]{1,0:T(8,128)(2,1)S(1)}, u32[]{:S(2)}, u32[]{:S(2)}) collective-permute-start(bf16[144,2048]{1,0:T(8,128)(2,1)} %collective-permute-done.3), channel_id=1, source_target_pairs={{2,0},{4,2},{6,4},{8,6},{10,8},{12,10},{14,12},{16,14},{18,16},{20... | collective-permute-start | bytes 1769480 | tf_op jit(solution)/shard_map/ppermute | solution.py:29
  108.2 2.3 collective-permute-start.6
  112.2 5.6 %collective-permute-start.10 = (bf16[144,2048]{1,0:T(8,128)(2,1)S(1)}, bf16[144,2048]{1,0:T(8,128)(2,1)S(1)}, u32[]{:S(2)}, u32[]{:S(2)}) collective-permute-start(bf16[144,2048]{1,0:T(8,128)(2,1)S(1)} %collective-permute-done.8), channel_id=1, source_target_pairs={{2,0},{4,2},{6,4},{8,6},{10,8},{12,10},{14,12},{16,14},{18,16},{20... | collective-permute-start | bytes 1769480 | tf_op jit(solution)/shard_map/ppermute | solution.py:29
  117.8 1.9 collective-permute-start.11
  119.8 5.1 %collective-permute-done.5 = bf16[144,2048]{1,0:T(8,128)(2,1)S(1)} collective-permute-done((bf16[144,2048]{1,0:T(8,128)(2,1)}, bf16[144,2048]{1,0:T(8,128)(2,1)S(1)}, u32[]{:S(2)}, u32[]{:S(2)}) %collective-permute-start.5) | collective-permute-done | bytes 589856 | tf_op jit(solution)/shard_map/ppermute | solution.py:29
  124.9 5.0 %collective-permute-done.6 = bf16[144,2048]{1,0:T(8,128)(2,1)S(1)} collective-permute-done((bf16[144,2048]{1,0:T(8,128)(2,1)}, bf16[144,2048]{1,0:T(8,128)(2,1)S(1)}, u32[]{:S(2)}, u32[]{:S(2)}) %collective-permute-start.6) | collective-permute-done | bytes 589856 | tf_op jit(solution)/shard_map/ppermute | solution.py:25
  131.0 1.9 shard_map.94
  140.8 1.9 shard_map.96
  143.4 5.2 %collective-permute-start.12 = (bf16[160,2048]{1,0:T(8,128)(2,1)S(1)}, bf16[160,2048]{1,0:T(8,128)(2,1)S(1)}, u32[]{:S(2)}, u32[]{:S(2)}) collective-permute-start(bf16[160,2048]{1,0:T(8,128)(2,1)S(1)} %get-tuple-element.56), channel_id=1, source_target_pairs={{0,2},{2,4},{1,3},{3,5},{8,10},{10,12},{9,11},{11,13},{16,18},{18,... | collective-permute-start | bytes 1966088 | tf_op jit(solution)/shard_map/ppermute | solution.py:33
  152.4 11.8 %collective-permute-done.12 = bf16[160,2048]{1,0:T(8,128)(2,1)S(1)} collective-permute-done((bf16[160,2048]{1,0:T(8,128)(2,1)S(1)}, bf16[160,2048]{1,0:T(8,128)(2,1)S(1)}, u32[]{:S(2)}, u32[]{:S(2)}) %collective-permute-start.12) | collective-permute-done | bytes 655392 | tf_op jit(solution)/shard_map/ppermute | solution.py:33
  167.1 1.9 shard_map.97
  169.0 3.4 %collective-permute-start.20 = (bf16[160,2048]{1,0:T(8,128)(2,1)S(1)}, bf16[160,2048]{1,0:T(8,128)(2,1)S(1)}, u32[]{:S(2)}, u32[]{:S(2)}) collective-permute-start(bf16[160,2048]{1,0:T(8,128)(2,1)S(1)} %get-tuple-element.61), channel_id=1, source_target_pairs={{0,6},{6,0},{1,7},{7,1},{8,14},{14,8},{9,15},{15,9},{16,22},{22,16... | collective-permute-start | bytes 1966088 | tf_op jit(solution)/shard_map/ppermute | solution.py:33
  172.5 3.2 %convolution_convert_fusion = bf16[2048,256]{1,0:T(8,128)(2,1)} fusion(bf16[144,2048]{1,0:T(8,128)(2,1)S(1)} %select_select_fusion.1, bf16[144,2048]{1,0:T(8,128)(2,1)S(1)} %broadcast_select_fusion.1, bf16[144,2048]{1,0:T(8,128)(2,1)S(1)} %get-tuple-element.48, bf16[144,2048]{1,0:T(8,128)(2,1)} %reshape.95, bf16[144,256]{1,0:T(8,128)(2,1)S(1)} %get-tuple-element.65, ...), kind=kOutput, calls=%fused_computation.1 | convolution fusion | flops 615120896 | bytes 3702784 | tf_op jit(solution)/shard_map/dot_general | solution.py:21
  177.1 10.8 %collective-permute-done.20 = bf16[160,2048]{1,0:T(8,128)(2,1)S(1)} collective-permute-done((bf16[160,2048]{1,0:T(8,128)(2,1)S(1)}, bf16[160,2048]{1,0:T(8,128)(2,1)S(1)}, u32[]{:S(2)}, u32[]{:S(2)}) %collective-permute-start.20) | collective-permute-done | bytes 655392 | tf_op jit(solution)/shard_map/ppermute | solution.py:33
  187.9 8.6 %collective-permute-done.15 = bf16[160,2048]{1,0:T(8,128)(2,1)S(1)} collective-permute-done((bf16[160,2048]{1,0:T(8,128)(2,1)S(1)}, bf16[160,2048]{1,0:T(8,128)(2,1)S(1)}, u32[]{:S(2)}, u32[]{:S(2)}) %collective-permute-start.15) | collective-permute-done | bytes 655392 | tf_op jit(solution)/shard_map/ppermute | solution.py:33
  197.8 11.0 %all-to-all-start.2 = ((bf16[4,40,2048]{2,1,0:T(8,128)(2,1)}), bf16[4,40,2048]{2,1,0:T(8,128)(2,1)}, u32[]{:S(2)}, u32[]{:S(2)}) async-start(bf16[4,40,2048]{2,1,0:T(8,128)(2,1)} %bitcast.29), calls=%async_computation.2 | async-start | bytes 1310720 | tf_op jit(solution)/shard_map/all_to_all | solution.py:185
  208.8 3.6 %collective-permute-start.21 = (bf16[2048,256]{1,0:T(8,128)(2,1)}, bf16[2048,256]{1,0:T(8,128)(2,1)S(1)}, u32[]{:S(2)}, u32[]{:S(2)}) collective-permute-start(bf16[2048,256]{1,0:T(8,128)(2,1)} %convolution_convert_fusion), channel_id=1, source_target_pairs={{0,1},{1,0},{2,3},{3,2},{4,5},{5,4},{6,7},{7,6},{8,9},{9,8},{10,11... | collective-permute-start | bytes 3145736 | tf_op jit(solution)/shard_map/ppermute | solution.py:37
  212.4 3.8 %collective-permute-start.22 = (bf16[128,2048]{1,0:T(8,128)(2,1)}, bf16[128,2048]{1,0:T(8,128)(2,1)S(1)}, u32[]{:S(2)}, u32[]{:S(2)}) collective-permute-start(bf16[128,2048]{1,0:T(8,128)(2,1)} %convolution_convert_fusion.3), channel_id=1, source_target_pairs={{0,1},{1,0},{2,3},{3,2},{4,5},{5,4},{6,7},{7,6},{8,9},{9,8},{10,11... | collective-permute-start | bytes 1572872 | tf_op jit(solution)/shard_map/ppermute | solution.py:37
  216.3 31.5 %collective-permute-done.22 = bf16[128,2048]{1,0:T(8,128)(2,1)S(1)} collective-permute-done((bf16[128,2048]{1,0:T(8,128)(2,1)}, bf16[128,2048]{1,0:T(8,128)(2,1)S(1)}, u32[]{:S(2)}, u32[]{:S(2)}) %collective-permute-start.22) | collective-permute-done | bytes 524320 | tf_op jit(solution)/shard_map/ppermute | solution.py:37
  249.3 3.2 %fusion = bf16[2048,256]{1,0:T(8,128)(2,1)} fusion(bf16[2048,256]{1,0:T(8,128)(2,1)S(1)} %collective-permute-done.21, bf16[144,2048]{1,0:T(8,128)(2,1)S(1)} %copy-done.13, bf16[144,2048]{1,0:T(8,128)(2,1)S(1)} %copy-done.11, bf16[144,2048]{1,0:T(8,128)(2,1)S(1)} %copy-done.9, bf16[144,2048]{1,0:T(8,128)(2,1)} %reshape.95, ...), kind=kOutput, calls=%fused_computation.2 | convolution fusion | flops 616169472 | bytes 4751360 | tf_op jit(solution)/shard_map/dot_general | solution.py:21
  254.2 2.2 fusion.2
  (115 shorter events, 39.5 us)
Async XLA Ops:
  3.6 53.0 %all-to-all-start = ((bf16[4,36,2048]{2,1,0:T(8,128)(2,1)}), bf16[4,36,2048]{2,1,0:T(8,128)(2,1)S(1)}, u32[]{:S(2)}, u32[]{:S(2)}) async-start(bf16[4,36,2048]{2,1,0:T(8,128)(2,1)} %reshape.94), calls=%async_computation | async-start | bytes 1310720 | tf_op jit(solution)/shard_map/all_to_all | solution.py:130
  18.7 8.6 %collective-permute-start = (bf16[128,2048]{1,0:T(8,128)(2,1)S(1)}, bf16[128,2048]{1,0:T(8,128)(2,1)S(1)}, u32[]{:S(2)}, u32[]{:S(2)}) collective-permute-start(bf16[128,2048]{1,0:T(8,128)(2,1)S(1)} %copy-done.22), channel_id=1, source_target_pairs={{0,480},{32,0},{64,32},{96,64},{128,96},{160,128},{192,160},{224,1... | collective-permute-start | bytes 1572872 | tf_op jit(solution)/shard_map/ppermute | solution.py:112
  20.6 47.2 %collective-permute-start.1 = (bf16[2048,256]{1,0:T(8,128)(2,1)S(1)}, bf16[2048,256]{1,0:T(8,128)(2,1)}, u32[]{:S(2)}, u32[]{:S(2)}) collective-permute-start(bf16[2048,256]{1,0:T(8,128)(2,1)S(1)} %bitcast.30), channel_id=1, source_target_pairs={{0,1},{1,0},{2,3},{3,2},{4,5},{5,4},{6,7},{7,6},{8,9},{9,8},{10,11... | collective-permute-start | bytes 3145736 | tf_op jit(solution)/shard_map/ppermute | solution.py:37
  56.5 35.5 %all-to-all-start.1 = ((bf16[4,36,2048]{2,1,0:T(8,128)(2,1)}), bf16[4,36,2048]{2,1,0:T(8,128)(2,1)}, u32[]{:S(2)}, u32[]{:S(2)}) async-start(bf16[4,36,2048]{2,1,0:T(8,128)(2,1)} %reshape.96), calls=%async_computation.1 | async-start | bytes 1310720 | tf_op jit(solution)/shard_map/all_to_all | solution.py:130
  60.7 32.6 %collective-permute-start.4 = (bf16[128,2048]{1,0:T(8,128)(2,1)}, bf16[128,2048]{1,0:T(8,128)(2,1)}, u32[]{:S(2)}, u32[]{:S(2)}) collective-permute-start(bf16[128,2048]{1,0:T(8,128)(2,1)} %bitcast.4), channel_id=1, source_target_pairs={{0,1},{1,0},{2,3},{3,2},{4,5},{5,4},{6,7},{7,6},{8,9},{9,8},{10,11... | collective-permute-start | bytes 1572872 | tf_op jit(solution)/shard_map/ppermute | solution.py:37
  67.8 33.8 %collective-permute-start.3 = (bf16[144,2048]{1,0:T(8,128)(2,1)}, bf16[144,2048]{1,0:T(8,128)(2,1)}, u32[]{:S(2)}, u32[]{:S(2)}) collective-permute-start(bf16[144,2048]{1,0:T(8,128)(2,1)} %reshape.95), channel_id=1, source_target_pairs={{2,0},{4,2},{6,4},{8,6},{10,8},{12,10},{14,12},{16,14},{18,16},{20... | collective-permute-start | bytes 1769480 | tf_op jit(solution)/shard_map/ppermute | solution.py:29
  74.4 28.9 %collective-permute-start.2 = (bf16[144,2048]{1,0:T(8,128)(2,1)}, bf16[144,2048]{1,0:T(8,128)(2,1)}, u32[]{:S(2)}, u32[]{:S(2)}) collective-permute-start(bf16[144,2048]{1,0:T(8,128)(2,1)} %reshape.95), channel_id=1, source_target_pairs={{0,2},{2,4},{4,6},{6,8},{8,10},{10,12},{12,14},{14,16},{16,18},{18... | collective-permute-start | bytes 1769480 | tf_op jit(solution)/shard_map/ppermute | solution.py:25
  93.3 18.9 %collective-permute-start.8 = (bf16[144,2048]{1,0:T(8,128)(2,1)S(1)}, bf16[144,2048]{1,0:T(8,128)(2,1)S(1)}, u32[]{:S(2)}, u32[]{:S(2)}) collective-permute-start(bf16[144,2048]{1,0:T(8,128)(2,1)S(1)} %reshape.97.g_ref), channel_id=1, source_target_pairs={{2,0},{4,2},{6,4},{8,6},{10,8},{12,10},{14,12},{16,14},{18,16},{20... | collective-permute-start | bytes 1769480 | tf_op jit(solution)/shard_map/ppermute | solution.py:29
  98.4 19.4 %collective-permute-start.7 = (bf16[144,2048]{1,0:T(8,128)(2,1)S(1)}, bf16[144,2048]{1,0:T(8,128)(2,1)S(1)}, u32[]{:S(2)}, u32[]{:S(2)}) collective-permute-start(bf16[144,2048]{1,0:T(8,128)(2,1)S(1)} %reshape.97.g_ref), channel_id=1, source_target_pairs={{0,2},{2,4},{4,6},{6,8},{8,10},{10,12},{12,14},{14,16},{16,18},{18... | collective-permute-start | bytes 1769480 | tf_op jit(solution)/shard_map/ppermute | solution.py:25
  104.6 67.8 %copy-start.8 = (bf16[144,2048]{1,0:T(8,128)(2,1)}, bf16[144,2048]{1,0:T(8,128)(2,1)S(1)}, u32[]{:S(2)}) copy-start(bf16[144,2048]{1,0:T(8,128)(2,1)S(1)} %get-tuple-element.48) | copy-start | bytes 1769476
  104.6 20.3 %collective-permute-start.5 = (bf16[144,2048]{1,0:T(8,128)(2,1)}, bf16[144,2048]{1,0:T(8,128)(2,1)S(1)}, u32[]{:S(2)}, u32[]{:S(2)}) collective-permute-start(bf16[144,2048]{1,0:T(8,128)(2,1)} %collective-permute-done.3), channel_id=1, source_target_pairs={{2,0},{4,2},{6,4},{8,6},{10,8},{12,10},{14,12},{16,14},{18,16},{20... | collective-permute-start | bytes 1769480 | tf_op jit(solution)/shard_map/ppermute | solution.py:29
  108.2 21.8 %collective-permute-start.6 = (bf16[144,2048]{1,0:T(8,128)(2,1)}, bf16[144,2048]{1,0:T(8,128)(2,1)S(1)}, u32[]{:S(2)}, u32[]{:S(2)}) collective-permute-start(bf16[144,2048]{1,0:T(8,128)(2,1)} %collective-permute-done.2), channel_id=1, source_target_pairs={{0,2},{2,4},{4,6},{6,8},{8,10},{10,12},{12,14},{14,16},{16,18},{18... | collective-permute-start | bytes 1769480 | tf_op jit(solution)/shard_map/ppermute | solution.py:25
  112.2 28.5 %collective-permute-start.10 = (bf16[144,2048]{1,0:T(8,128)(2,1)S(1)}, bf16[144,2048]{1,0:T(8,128)(2,1)S(1)}, u32[]{:S(2)}, u32[]{:S(2)}) collective-permute-start(bf16[144,2048]{1,0:T(8,128)(2,1)S(1)} %collective-permute-done.8), channel_id=1, source_target_pairs={{2,0},{4,2},{6,4},{8,6},{10,8},{12,10},{14,12},{16,14},{18,16},{20... | collective-permute-start | bytes 1769480 | tf_op jit(solution)/shard_map/ppermute | solution.py:29
  117.8 22.9 %collective-permute-start.11 = (bf16[144,2048]{1,0:T(8,128)(2,1)S(1)}, bf16[144,2048]{1,0:T(8,128)(2,1)S(1)}, u32[]{:S(2)}, u32[]{:S(2)}) collective-permute-start(bf16[144,2048]{1,0:T(8,128)(2,1)S(1)} %collective-permute-done.7), channel_id=1, source_target_pairs={{0,2},{2,4},{4,6},{6,8},{8,10},{10,12},{12,14},{14,16},{16,18},{18... | collective-permute-start | bytes 1769480 | tf_op jit(solution)/shard_map/ppermute | solution.py:25
  130.0 42.5 %copy-start.10 = (bf16[144,2048]{1,0:T(8,128)(2,1)}, bf16[144,2048]{1,0:T(8,128)(2,1)S(1)}, u32[]{:S(2)}) copy-start(bf16[144,2048]{1,0:T(8,128)(2,1)S(1)} %broadcast_select_fusion.1) | copy-start | bytes 1769476
  132.9 55.0 %collective-permute-start.9 = (bf16[160,2048]{1,0:T(8,128)(2,1)S(1)}, bf16[160,2048]{1,0:T(8,128)(2,1)S(1)}, u32[]{:S(2)}, u32[]{:S(2)}) collective-permute-start(bf16[160,2048]{1,0:T(8,128)(2,1)S(1)} %get-tuple-element.50), channel_id=1, source_target_pairs={{0,2},{6,4},{1,3},{7,5},{8,10},{14,12},{9,11},{15,13},{16,18},{22,... | collective-permute-start | bytes 1966088 | tf_op jit(solution)/shard_map/ppermute | solution.py:33
  136.3 13.5 %collective-permute-start.16 = (bf16[144,2048]{1,0:T(8,128)(2,1)S(1)}, bf16[144,2048]{1,0:T(8,128)(2,1)S(1)}, u32[]{:S(2)}, u32[]{:S(2)}) collective-permute-start(bf16[144,2048]{1,0:T(8,128)(2,1)S(1)} %collective-permute-done.5), channel_id=1, source_target_pairs={{2,0},{3,1},{10,8},{11,9},{18,16},{19,17},{26,24},{27,25},{34,32},... | collective-permute-start | bytes 1769480 | tf_op jit(solution)/shard_map/ppermute | solution.py:33
  137.6 13.5 %collective-permute-start.17 = (bf16[144,2048]{1,0:T(8,128)(2,1)S(1)}, bf16[144,2048]{1,0:T(8,128)(2,1)S(1)}, u32[]{:S(2)}, u32[]{:S(2)}) collective-permute-start(bf16[144,2048]{1,0:T(8,128)(2,1)S(1)} %collective-permute-done.6), channel_id=1, source_target_pairs={{4,6},{5,7},{12,14},{13,15},{20,22},{21,23},{28,30},{29,31},{36,38... | collective-permute-start | bytes 1769480 | tf_op jit(solution)/shard_map/ppermute | solution.py:33
  142.7 9.7 %collective-permute-start.14 = (bf16[160,2048]{1,0:T(8,128)(2,1)S(1)}, bf16[160,2048]{1,0:T(8,128)(2,1)S(1)}, u32[]{:S(2)}, u32[]{:S(2)}) collective-permute-start(bf16[160,2048]{1,0:T(8,128)(2,1)S(1)} %get-tuple-element.56), channel_id=1, source_target_pairs={{6,4},{4,2},{7,5},{5,3},{14,12},{12,10},{15,13},{13,11},{22,20},{2... | collective-permute-start | bytes 1966088 | tf_op jit(solution)/shard_map/ppermute | solution.py:33
  143.4 20.9 %collective-permute-start.12 = (bf16[160,2048]{1,0:T(8,128)(2,1)S(1)}, bf16[160,2048]{1,0:T(8,128)(2,1)S(1)}, u32[]{:S(2)}, u32[]{:S(2)}) collective-permute-start(bf16[160,2048]{1,0:T(8,128)(2,1)S(1)} %get-tuple-element.56), channel_id=1, source_target_pairs={{0,2},{2,4},{1,3},{3,5},{8,10},{10,12},{9,11},{11,13},{16,18},{18,... | collective-permute-start | bytes 1966088 | tf_op jit(solution)/shard_map/ppermute | solution.py:33
  149.8 17.2 %collective-permute-start.18 = (bf16[144,2048]{1,0:T(8,128)(2,1)S(1)}, bf16[144,2048]{1,0:T(8,128)(2,1)S(1)}, u32[]{:S(2)}, u32[]{:S(2)}) collective-permute-start(bf16[144,2048]{1,0:T(8,128)(2,1)S(1)} %collective-permute-done.10), channel_id=1, source_target_pairs={{2,0},{3,1},{10,8},{11,9},{18,16},{19,17},{26,24},{27,25},{34,32},... | collective-permute-start | bytes 1769480 | tf_op jit(solution)/shard_map/ppermute | solution.py:33
  151.1 15.9 %collective-permute-start.19 = (bf16[144,2048]{1,0:T(8,128)(2,1)S(1)}, bf16[144,2048]{1,0:T(8,128)(2,1)S(1)}, u32[]{:S(2)}, u32[]{:S(2)}) collective-permute-start(bf16[144,2048]{1,0:T(8,128)(2,1)S(1)} %collective-permute-done.11), channel_id=1, source_target_pairs={{4,6},{5,7},{12,14},{13,15},{20,22},{21,23},{28,30},{29,31},{36,38... | collective-permute-start | bytes 1769480 | tf_op jit(solution)/shard_map/ppermute | solution.py:33
  164.8 31.7 %collective-permute-start.15 = (bf16[160,2048]{1,0:T(8,128)(2,1)S(1)}, bf16[160,2048]{1,0:T(8,128)(2,1)S(1)}, u32[]{:S(2)}, u32[]{:S(2)}) collective-permute-start(bf16[160,2048]{1,0:T(8,128)(2,1)S(1)} %get-tuple-element.78), channel_id=1, source_target_pairs={{4,2},{2,0},{5,3},{3,1},{12,10},{10,8},{13,11},{11,9},{20,18},{18,... | collective-permute-start | bytes 1966088 | tf_op jit(solution)/shard_map/ppermute | solution.py:33
  166.1 30.4 %collective-permute-start.13 = (bf16[160,2048]{1,0:T(8,128)(2,1)S(1)}, bf16[160,2048]{1,0:T(8,128)(2,1)S(1)}, u32[]{:S(2)}, u32[]{:S(2)}) collective-permute-start(bf16[160,2048]{1,0:T(8,128)(2,1)S(1)} %get-tuple-element.79), channel_id=1, source_target_pairs={{2,4},{4,6},{3,5},{5,7},{10,12},{12,14},{11,13},{13,15},{18,20},{2... | collective-permute-start | bytes 1966088 | tf_op jit(solution)/shard_map/ppermute | solution.py:33
  169.0 18.8 %collective-permute-start.20 = (bf16[160,2048]{1,0:T(8,128)(2,1)S(1)}, bf16[160,2048]{1,0:T(8,128)(2,1)S(1)}, u32[]{:S(2)}, u32[]{:S(2)}) collective-permute-start(bf16[160,2048]{1,0:T(8,128)(2,1)S(1)} %get-tuple-element.61), channel_id=1, source_target_pairs={{0,6},{6,0},{1,7},{7,1},{8,14},{14,8},{9,15},{15,9},{16,22},{22,16... | collective-permute-start | bytes 1966088 | tf_op jit(solution)/shard_map/ppermute | solution.py:33
  196.4 51.4 %copy-start.3 = (bf16[144,2048]{1,0:T(8,128)(2,1)S(1)}, bf16[144,2048]{1,0:T(8,128)(2,1)}, u32[]{:S(2)}) copy-start(bf16[144,2048]{1,0:T(8,128)(2,1)} %copy-done.1) | copy-start | bytes 1769476
  196.4 51.4 %copy-start.5 = (bf16[144,2048]{1,0:T(8,128)(2,1)S(1)}, bf16[144,2048]{1,0:T(8,128)(2,1)}, u32[]{:S(2)}) copy-start(bf16[144,2048]{1,0:T(8,128)(2,1)} %copy-done.4) | copy-start | bytes 1769476
  196.4 51.4 %copy-start.7 = (bf16[144,2048]{1,0:T(8,128)(2,1)S(1)}, bf16[144,2048]{1,0:T(8,128)(2,1)}, u32[]{:S(2)}) copy-start(bf16[144,2048]{1,0:T(8,128)(2,1)} %copy-done.6) | copy-start | bytes 1769476
  196.5 51.4 %copy-start.20 = (bf16[576,256]{1,0:T(8,128)(2,1)S(1)}, bf16[576,256]{1,0:T(8,128)(2,1)}, u32[]{:S(2)}) copy-start(bf16[576,256]{1,0:T(8,128)(2,1)} %copy-done.19) | copy-start | bytes 884740
  197.8 54.7 %all-to-all-start.2 = ((bf16[4,40,2048]{2,1,0:T(8,128)(2,1)}), bf16[4,40,2048]{2,1,0:T(8,128)(2,1)}, u32[]{:S(2)}, u32[]{:S(2)}) async-start(bf16[4,40,2048]{2,1,0:T(8,128)(2,1)} %bitcast.29), calls=%async_computation.2 | async-start | bytes 1310720 | tf_op jit(solution)/shard_map/all_to_all | solution.py:185
  208.8 40.5 %collective-permute-start.21 = (bf16[2048,256]{1,0:T(8,128)(2,1)}, bf16[2048,256]{1,0:T(8,128)(2,1)S(1)}, u32[]{:S(2)}, u32[]{:S(2)}) collective-permute-start(bf16[2048,256]{1,0:T(8,128)(2,1)} %convolution_convert_fusion), channel_id=1, source_target_pairs={{0,1},{1,0},{2,3},{3,2},{4,5},{5,4},{6,7},{7,6},{8,9},{9,8},{10,11... | collective-permute-start | bytes 3145736 | tf_op jit(solution)/shard_map/ppermute | solution.py:37
  212.4 35.5 %collective-permute-start.22 = (bf16[128,2048]{1,0:T(8,128)(2,1)}, bf16[128,2048]{1,0:T(8,128)(2,1)S(1)}, u32[]{:S(2)}, u32[]{:S(2)}) collective-permute-start(bf16[128,2048]{1,0:T(8,128)(2,1)} %convolution_convert_fusion.3), channel_id=1, source_target_pairs={{0,1},{1,0},{2,3},{3,2},{4,5},{5,4},{6,7},{7,6},{8,9},{9,8},{10,11... | collective-permute-start | bytes 1572872 | tf_op jit(solution)/shard_map/ppermute | solution.py:37
  (18 other events, 292.6 us)

commit v5 on v4

--- a/solution.py
+++ b/solution.py
@@ -118,6 +118,7 @@
     earlier = (jnp.arange(tok)[:, None] > jnp.arange(tok)[None, :]).astype(F32)
     before = dot(earlier, onehot, 1, 0)
     slot = jnp.sum(before * onehot, axis=1).astype(jnp.int32)
+    rel = (ids - zb) % EXPERTS
     weight = combine.astype(F32)
     scaled = (weight * out_grad.astype(F32)).astype(BF)
     place = (
@@ -125,10 +126,11 @@
         == (ids * cap + slot)[None, :]
     ).astype(BF)
 
-    def to_blocks(a):
-        sent = dot(place, a, 1, 0).astype(BF).reshape(EXPERTS, cap, width)
-        unit = lax.all_to_all(sent, "zb", 0, 0, tiled=True)
-        return unit.reshape(EXPERTS * cap, width)
+    def dispatch(a):
+        return dot(place, a, 1, 0).astype(BF).reshape(EXPERTS, cap, width)
+
+    def block(a, k):
+        return lax.ppermute(a, "zb", [(i, (i + k) % EXPERTS) for i in range(EXPERTS)])
 
     where = jnp.where
     first, last, odd = zo == 0, zo == 3, (zo % 2) == 1
@@ -141,10 +143,16 @@
         whole = lambda *others: where(
             first, after(l3, *others), where(last, after(r3, *others), early)
         )
-        return [unit, where(odd, r1, l1), early, where(zo < 2, l2, r2)], whole
-
-    unit_x = to_blocks(tokens)
-    unit_g = to_blocks(scaled)
+        units = [unit, where(odd, r1, l1), early, where(zo < 2, l2, r2)]
+        return units, whole
+
+    from_block = (zb - jnp.arange(EXPERTS)) % EXPERTS
+
+    def to_blocks(a):
+        units = lax.all_to_all(dispatch(a), "zb", 0, 0, tiled=True)
+        return units[from_block].reshape(-1, width)
+
+    unit_x, unit_g = to_blocks(tokens), to_blocks(scaled)
     wgu_other, wdown_other = across(wgu), across(wdown)
     unit_x, wgu_other = lax.optimization_barrier((unit_x, wgu_other))
     unit_g, wdown_other = lax.optimization_barrier((unit_g, wdown_other))
@@ -159,7 +167,7 @@
     x3 = x3(*gus)
     gus.append(forward(after(xs[3], gs[1])))
     gu3 = forward(x3)
-    early = (xs[3], xs[3], xs[3], gs[3])
+    early = (x3, x3, x3, gs[3])
     done = [expert(gu, after(g, e)) for gu, g, e in zip(gus, gs, early)]
 
     add = lambda *terms: sum(a.astype(F32) for a in terms).astype(BF)
@@ -180,10 +188,12 @@
     other_gu = dot(x_all, cat(other), 0, 0).astype(BF)
     other_down = dot(hid_all[:, hidden:], g_all, 0, 0).astype(BF)
 
+    other_down = across(other_down)
     dx = add(d0, near, r1, l1, after(far, other_gu, other_down))
     dx = dx.reshape(EXPERTS, pitch, width)
-    back = lax.all_to_all(dx, "zb", 0, 0, tiled=True).reshape(-1, width)
-    other_gu, other_down = across(other_gu), across(other_down)
+    far, up1, down1 = (block(dx[k], -k) for k in (2, 1, 3))
+    back = jnp.concatenate([dx[0], up1, far, down1], axis=0)
+    other_gu = across(other_gu)
     grad_gu = (dot(x_all, cat(own), 0, 0) + other_gu.astype(F32)).astype(BF)
     grad_down = dot(hid_all[:, :hidden], g_all, 0, 0) + other_down.astype(F32)
     grad_down = grad_down.astype(BF)
@@ -191,14 +201,14 @@
 
     put = (
         jnp.arange(EXPERTS * pitch, dtype=jnp.int32)[:, None]
-        == (ids * pitch + slot)[None, :]
+        == (rel * pitch + slot)[None, :]
     ).astype(BF)
     moe = dot(put, back, 0, 0)
     input_grad = (out_grad.astype(F32) + moe).astype(BF)
     dp = back.reshape(EXPERTS, pitch, width)[:, cap, : LINE * LANES].astype(F32)
     dp = jnp.sum(dp.reshape(EXPERTS, LINE, LANES), axis=1)
-    pick = (ids[:, None] == jnp.arange(EXPERTS)[None, :])[:, :, None] & (
-        (zb * cap + slot)[:, None] == jnp.arange(LANES)[None, :]
+    pick = (rel[:, None] == jnp.arange(EXPERTS)[None, :])[:, :, None] & (
+        (rel * cap + slot)[:, None] == jnp.arange(LANES)[None, :]
     )[:, None, :]
     dp = jnp.sum(jnp.where(pick, dp[None], 0.0), axis=(1, 2))
     combine_grad = (dp[:, None] / weight).astype(BF)

time: 260 us -> 241 us (0.927)
  waiting for transfers between devices: 119 us -> 97 us
  starting transfers between devices: 95.4 us -> 101 us
  matrix products: 16.5 us -> 13.5 us
    ppermute x4, waiting for transfers between devices: 31.5 us -> 6.02 us  [across(): return lax.ppermute(a, 'yh', [(0, 1), (1, 0)])]
    ppermute x10, waiting for transfers between devices: 32.3 us -> 6.94 us  [line(): return lax.ppermute(a, 'zo', pairs)]
    ppermute x0 -> x3, starting transfers between devices: none -> 19.8 us  [block(): lax.ppermute(a, 'zb', [(i, (i + k) % EXPERTS) for i in range(EXPERTS)])]
    ppermute x0 -> x3, waiting for transfers between devices: none -> 18.2 us  [block(): lax.ppermute(a, 'zb', [(i, (i + k) % EXPERTS) for i in range(EXPERTS)])]
    all_to_all x3 -> x2, starting transfers between devices: 30.2 us -> 18.6 us  [to_blocks(): units = lax.all_to_all(dispatch(a), 'zb', 0, 0, tiled=True)]
    ppermute x4, waiting for transfers between devices: 5.32 us -> 16.7 us  [down(): lax.ppermute(a, ('zb', 'zo'), [((i + 1) % RING, i) for i in range(RING)])]
    ppermute x4, starting transfers between devices: 20.8 us -> 13.7 us  [down(): lax.ppermute(a, ('zb', 'zo'), [((i + 1) % RING, i) for i in range(RING)])]
    all_to_all x3 -> x2, waiting for transfers between devices: 41.3 us -> 47.8 us  [to_blocks(): units = lax.all_to_all(dispatch(a), 'zb', 0, 0, tiled=True)]
  transfers between devices with their start and end apart: 26 -> 28, of which waited for: 12 -> 12; matrix products, arithmetic and copies ran while one was open for 9% -> 9% of each run, Pallas kernels for 4% -> 4%
where the time goes in v5:
time: 241 us; the launch traced here: 237 us
  starting transfers between devices  101 us (42%)
  waiting for transfers between devices  97 us (40%)
  matrix products  13.5 us (6%)
  local copies, waits for them, and re-layouts  9.72 us (4%)
  Pallas kernels  9.48 us (4%)
  other arithmetic  5.94 us (2%)
    all_to_all x2, waiting for transfers between devices, to_blocks(): units = lax.all_to_all(dispatch(a), 'zb', 0, 0, tiled=True)  47.8 us
    ppermute x3, starting transfers between devices, block(): lax.ppermute(a, 'zb', [(i, (i + k) % EXPERTS) for i in range(EXPERTS)])  19.8 us
    all_to_all x2, starting transfers between devices, to_blocks(): units = lax.all_to_all(dispatch(a), 'zb', 0, 0, tiled=True)  18.6 us
    ppermute x3, waiting for transfers between devices, block(): lax.ppermute(a, 'zb', [(i, (i + k) % EXPERTS) for i in range(EXPERTS)])  18.2 us
    ppermute x4, starting transfers between devices, across(): return lax.ppermute(a, 'yh', [(0, 1), (1, 0)])  17.5 us
    ppermute x4, waiting for transfers between devices, down(): lax.ppermute(a, ('zb', 'zo'), [((i + 1) % RING, i) for i in range(RING)])  16.7 us
    ppermute x10, starting transfers between devices, line(): return lax.ppermute(a, 'zo', pairs)  16.6 us
    ppermute x4, starting transfers between devices, down(): lax.ppermute(a, ('zb', 'zo'), [((i + 1) % RING, i) for i in range(RING)])  13.7 us
  transfers between devices with their start and end apart: 28, of which 12 were waited for; matrix products, arithmetic and copies ran while one was open for 9% of the time, Pallas kernels for 4%

profile of v5, /device:TPU:6, one launch (start us, length us, event | category | flops | bytes accessed | tf_op | source)
XLA Modules:
  0.0 237.5 jit_solution(9918876879456242676)
XLA Ops:
  3.5 15.1 %all-to-all-start = ((bf16[4,36,2048]{2,1,0:T(8,128)(2,1)}), bf16[4,36,2048]{2,1,0:T(8,128)(2,1)S(1)}, u32[]{:S(2)}, u32[]{:S(2)}) async-start(bf16[4,36,2048]{2,1,0:T(8,128)(2,1)} %reshape.163), calls=%async_computation | async-start | bytes 1310720 | tf_op jit(solution)/shard_map/all_to_all | solution.py:152
  18.6 2.0 collective-permute-start
  20.7 5.1 %collective-permute-start.1 = (bf16[2048,256]{1,0:T(8,128)(2,1)}, bf16[2048,256]{1,0:T(8,128)(2,1)}, u32[]{:S(2)}, u32[]{:S(2)}) collective-permute-start(bf16[2048,256]{1,0:T(8,128)(2,1)} %bitcast.3), channel_id=1, source_target_pairs={{0,1},{1,0},{2,3},{3,2},{4,5},{5,4},{6,7},{7,6},{8,9},{9,8},{10,11... | collective-permute-start | bytes 3145736 | tf_op jit(solution)/shard_map/ppermute | solution.py:37
  25.8 2.2 collective-permute-start.4
  29.5 27.0 %all-to-all-done = bf16[4,36,2048]{2,1,0:T(8,128)(2,1)S(1)} async-done(((bf16[4,36,2048]{2,1,0:T(8,128)(2,1)}), bf16[4,36,2048]{2,1,0:T(8,128)(2,1)S(1)}, u32[]{:S(2)}, u32[]{:S(2)}) %all-to-all-start) | async-done | bytes 589856 | tf_op jit(solution)/shard_map/all_to_all | solution.py:152
  56.5 3.5 %all-to-all-start.1 = ((bf16[4,36,2048]{2,1,0:T(8,128)(2,1)}), bf16[4,36,2048]{2,1,0:T(8,128)(2,1)S(1)}, u32[]{:S(2)}, u32[]{:S(2)}) async-start(bf16[4,36,2048]{2,1,0:T(8,128)(2,1)} %reshape.165), calls=%async_computation.1 | async-start | bytes 1310720 | tf_op jit(solution)/shard_map/all_to_all | solution.py:152
  60.1 2.2 fusion.40
  63.9 6.5 %collective-permute-start.3 = (bf16[144,2048]{1,0:T(8,128)(2,1)}, bf16[144,2048]{1,0:T(8,128)(2,1)}, u32[]{:S(2)}, u32[]{:S(2)}) collective-permute-start(bf16[144,2048]{1,0:T(8,128)(2,1)} %reshape.164), channel_id=1, source_target_pairs={{2,0},{4,2},{6,4},{8,6},{10,8},{12,10},{14,12},{16,14},{18,16},{20... | collective-permute-start | bytes 1769480 | tf_op jit(solution)/shard_map/ppermute | solution.py:29
  70.5 1.9 collective-permute-start.2
  73.9 20.8 %all-to-all-done.1 = bf16[4,36,2048]{2,1,0:T(8,128)(2,1)S(1)} async-done(((bf16[4,36,2048]{2,1,0:T(8,128)(2,1)}), bf16[4,36,2048]{2,1,0:T(8,128)(2,1)S(1)}, u32[]{:S(2)}, u32[]{:S(2)}) %all-to-all-start.1) | async-done | bytes 589856 | tf_op jit(solution)/shard_map/all_to_all | solution.py:152
  99.3 3.9 %collective-permute-start.9 = (bf16[144,2048]{1,0:T(8,128)(2,1)S(1)}, bf16[144,2048]{1,0:T(8,128)(2,1)S(1)}, u32[]{:S(2)}, u32[]{:S(2)}) collective-permute-start(bf16[144,2048]{1,0:T(8,128)(2,1)S(1)} %reshape.166.g_ref), channel_id=1, source_target_pairs={{0,2},{2,4},{4,6},{6,8},{8,10},{10,12},{12,14},{14,16},{16,18},{18... | collective-permute-start | bytes 1769480 | tf_op jit(solution)/shard_map/ppermute | solution.py:25
  105.9 3.1 %collective-permute-start.5 = (bf16[144,2048]{1,0:T(8,128)(2,1)}, bf16[144,2048]{1,0:T(8,128)(2,1)S(1)}, u32[]{:S(2)}, u32[]{:S(2)}) collective-permute-start(bf16[144,2048]{1,0:T(8,128)(2,1)} %collective-permute-done.3), channel_id=1, source_target_pairs={{2,0},{4,2},{6,4},{8,6},{10,8},{12,10},{14,12},{16,14},{18,16},{20... | collective-permute-start | bytes 1769480 | tf_op jit(solution)/shard_map/ppermute | solution.py:29
  109.0 2.7 %collective-permute-start.7 = (bf16[144,2048]{1,0:T(8,128)(2,1)}, bf16[144,2048]{1,0:T(8,128)(2,1)S(1)}, u32[]{:S(2)}, u32[]{:S(2)}) collective-permute-start(bf16[144,2048]{1,0:T(8,128)(2,1)} %collective-permute-done.2), channel_id=1, source_target_pairs={{0,2},{2,4},{4,6},{6,8},{8,10},{10,12},{12,14},{14,16},{16,18},{18... | collective-permute-start | bytes 1769480 | tf_op jit(solution)/shard_map/ppermute | solution.py:25
  113.2 2.2 collective-permute-done.10
  115.5 2.1 collective-permute-start.12
  117.6 3.7 %collective-permute-start.13 = (bf16[144,2048]{1,0:T(8,128)(2,1)S(1)}, bf16[144,2048]{1,0:T(8,128)(2,1)S(1)}, u32[]{:S(2)}, u32[]{:S(2)}) collective-permute-start(bf16[144,2048]{1,0:T(8,128)(2,1)S(1)} %collective-permute-done.9), channel_id=1, source_target_pairs={{0,2},{2,4},{4,6},{6,8},{8,10},{10,12},{12,14},{14,16},{16,18},{18... | collective-permute-start | bytes 1769480 | tf_op jit(solution)/shard_map/ppermute | solution.py:25
  121.4 6.7 %collective-permute-done.5 = bf16[144,2048]{1,0:T(8,128)(2,1)S(1)} collective-permute-done((bf16[144,2048]{1,0:T(8,128)(2,1)}, bf16[144,2048]{1,0:T(8,128)(2,1)S(1)}, u32[]{:S(2)}, u32[]{:S(2)}) %collective-permute-start.5) | collective-permute-done | bytes 589856 | tf_op jit(solution)/shard_map/ppermute | solution.py:29
  133.0 7.7 %collective-permute-done.12 = bf16[144,2048]{1,0:T(8,128)(2,1)S(1)} collective-permute-done((bf16[144,2048]{1,0:T(8,128)(2,1)S(1)}, bf16[144,2048]{1,0:T(8,128)(2,1)S(1)}, u32[]{:S(2)}, u32[]{:S(2)}) %collective-permute-start.12) | collective-permute-done | bytes 589856 | tf_op jit(solution)/shard_map/ppermute | solution.py:29
  143.5 2.1 collective-permute-start.14
  146.8 6.0 %collective-permute-done.6 = bf16[144,2048]{1,0:T(8,128)(2,1)S(1)} collective-permute-done((bf16[144,2048]{1,0:T(8,128)(2,1)S(1)}, bf16[144,2048]{1,0:T(8,128)(2,1)S(1)}, u32[]{:S(2)}, u32[]{:S(2)}) %collective-permute-start.6) | collective-permute-done | bytes 589856 | tf_op jit(solution)/shard_map/ppermute | solution.py:33
  167.0 6.2 %collective-permute-start.20 = (bf16[160,2048]{1,0:T(8,128)(2,1)S(1)}, bf16[160,2048]{1,0:T(8,128)(2,1)S(1)}, u32[]{:S(2)}, u32[]{:S(2)}) collective-permute-start(bf16[160,2048]{1,0:T(8,128)(2,1)S(1)} %get-tuple-element.61), channel_id=1, source_target_pairs={{0,6},{6,0},{1,7},{7,1},{8,14},{14,8},{9,15},{15,9},{16,22},{22,16... | collective-permute-start | bytes 1966088 | tf_op jit(solution)/shard_map/ppermute | solution.py:33
  173.8 5.1 %collective-permute-start.21 = (bf16[128,2048]{1,0:T(8,128)(2,1)S(1)}, bf16[128,2048]{1,0:T(8,128)(2,1)S(1)}, u32[]{:S(2)}, u32[]{:S(2)}) collective-permute-start(bf16[128,2048]{1,0:T(8,128)(2,1)S(1)} %convolution_convert_fusion.3), channel_id=1, source_target_pairs={{0,1},{1,0},{2,3},{3,2},{4,5},{5,4},{6,7},{7,6},{8,9},{9,8},{10,11... | collective-permute-start | bytes 1572872 | tf_op jit(solution)/shard_map/ppermute | solution.py:37
  178.9 2.1 convolution_convert_fusion
  181.1 6.0 %collective-permute-done.21 = bf16[128,2048]{1,0:T(8,128)(2,1)S(1)} collective-permute-done((bf16[128,2048]{1,0:T(8,128)(2,1)S(1)}, bf16[128,2048]{1,0:T(8,128)(2,1)S(1)}, u32[]{:S(2)}, u32[]{:S(2)}) %collective-permute-start.21) | collective-permute-done | bytes 524320 | tf_op jit(solution)/shard_map/ppermute | solution.py:37
  187.1 5.1 %collective-permute-start.25 = (bf16[2048,256]{1,0:T(8,128)(2,1)S(1)}, bf16[2048,256]{1,0:T(8,128)(2,1)S(1)}, u32[]{:S(2)}, u32[]{:S(2)}) collective-permute-start(bf16[2048,256]{1,0:T(8,128)(2,1)S(1)} %convolution_convert_fusion), channel_id=1, source_target_pairs={{0,1},{1,0},{2,3},{3,2},{4,5},{5,4},{6,7},{7,6},{8,9},{9,8},{10,11... | collective-permute-start | bytes 3145736 | tf_op jit(solution)/shard_map/ppermute | solution.py:37
  192.8 6.7 %collective-permute-start.24 = (bf16[40,2048]{1,0:T(8,128)(2,1)S(1)}, bf16[40,2048]{1,0:T(8,128)(2,1)S(1)}, u32[]{:S(2)}, u32[]{:S(2)}) collective-permute-start(bf16[40,2048]{1,0:T(8,128)(2,1)S(1)} %get-tuple-element.91), channel_id=1, source_target_pairs={{0,8},{8,16},{16,24},{24,0},{1,9},{9,17},{17,25},{25,1},{2,10},{10... | collective-permute-start | bytes 491528 | tf_op jit(solution)/shard_map/ppermute | solution.py:133
  199.5 7.0 %collective-permute-start.23 = (bf16[40,2048]{1,0:T(8,128)(2,1)S(1)}, bf16[40,2048]{1,0:T(8,128)(2,1)S(1)}, u32[]{:S(2)}, u32[]{:S(2)}) collective-permute-start(bf16[40,2048]{1,0:T(8,128)(2,1)S(1)} %get-tuple-element.92), channel_id=1, source_target_pairs={{0,16},{8,24},{16,0},{24,8},{1,17},{9,25},{17,1},{25,9},{2,18},{10... | collective-permute-start | bytes 491528 | tf_op jit(solution)/shard_map/ppermute | solution.py:133
  206.5 6.0 %collective-permute-start.22 = (bf16[40,2048]{1,0:T(8,128)(2,1)S(1)}, bf16[40,2048]{1,0:T(8,128)(2,1)S(1)}, u32[]{:S(2)}, u32[]{:S(2)}) collective-permute-start(bf16[40,2048]{1,0:T(8,128)(2,1)S(1)} %get-tuple-element.93), channel_id=1, source_target_pairs={{0,24},{8,0},{16,8},{24,16},{1,25},{9,1},{17,9},{25,17},{2,26},{10... | collective-permute-start | bytes 491528 | tf_op jit(solution)/shard_map/ppermute | solution.py:133
  214.0 6.0 %collective-permute-done.24 = bf16[40,2048]{1,0:T(8,128)(2,1)S(1)} collective-permute-done((bf16[40,2048]{1,0:T(8,128)(2,1)S(1)}, bf16[40,2048]{1,0:T(8,128)(2,1)S(1)}, u32[]{:S(2)}, u32[]{:S(2)}) %collective-permute-start.24) | collective-permute-done | bytes 163872 | tf_op jit(solution)/shard_map/ppermute | solution.py:133
  220.0 8.6 %collective-permute-done.23 = bf16[40,2048]{1,0:T(8,128)(2,1)S(1)} collective-permute-done((bf16[40,2048]{1,0:T(8,128)(2,1)S(1)}, bf16[40,2048]{1,0:T(8,128)(2,1)S(1)}, u32[]{:S(2)}, u32[]{:S(2)}) %collective-permute-start.23) | collective-permute-done | bytes 163872 | tf_op jit(solution)/shard_map/ppermute | solution.py:133
  228.7 3.5 %collective-permute-done.22 = bf16[40,2048]{1,0:T(8,128)(2,1)S(1)} collective-permute-done((bf16[40,2048]{1,0:T(8,128)(2,1)S(1)}, bf16[40,2048]{1,0:T(8,128)(2,1)S(1)}, u32[]{:S(2)}, u32[]{:S(2)}) %collective-permute-start.22) | collective-permute-done | bytes 163872 | tf_op jit(solution)/shard_map/ppermute | solution.py:133
  232.3 3.2 %fusion = bf16[2048,256]{1,0:T(8,128)(2,1)} fusion(bf16[2048,256]{1,0:T(8,128)(2,1)S(1)} %collective-permute-done.25, bf16[144,2048]{1,0:T(8,128)(2,1)S(1)} %select_select_fusion.1, bf16[144,2048]{1,0:T(8,128)(2,1)S(1)} %broadcast_select_fusion.1, bf16[144,2048]{1,0:T(8,128)(2,1)S(1)} %get-tuple-element.45, bf16[144,2048]{1,0:T(8,128)(2,1)} %reshape.164, ...), kind=kOutput, calls=%fused_computation.4 | convolution fusion | flops 616169472 | bytes 4751360 | tf_op jit(solution)/shard_map/dot_general | solution.py:21
  (94 shorter events, 43.8 us)
Async XLA Ops:
  0.6 18.0 %copy-start.6 = (bf16[128,2048]{1,0:T(8,128)(2,1)S(1)}, bf16[128,2048]{1,0:T(8,128)(2,1)}, u32[]{:S(2)}) copy-start(bf16[128,2048]{1,0:T(8,128)(2,1)} %param.7) | copy-start | bytes 1572868
  0.7 27.4 %copy-start.7 = (bf16[128,1]{0,1:T(2,128)(2,1)S(1)}, bf16[128,1]{0,1:T(2,128)(2,1)}, u32[]{:S(2)}) copy-start(bf16[128,1]{0,1:T(2,128)(2,1)} %param.9) | copy-start | bytes 772
  3.5 53.0 %all-to-all-start = ((bf16[4,36,2048]{2,1,0:T(8,128)(2,1)}), bf16[4,36,2048]{2,1,0:T(8,128)(2,1)S(1)}, u32[]{:S(2)}, u32[]{:S(2)}) async-start(bf16[4,36,2048]{2,1,0:T(8,128)(2,1)} %reshape.163), calls=%async_computation | async-start | bytes 1310720 | tf_op jit(solution)/shard_map/all_to_all | solution.py:152
  18.6 41.4 %copy-start.5 = (s32[128,1]{0,1:T(1,128)S(1)}, s32[128,1]{0,1:T(1,128)}, u32[]{:S(2)}) copy-start(s32[128,1]{0,1:T(1,128)} %param.8) | copy-start | bytes 1540
  18.6 9.5 %collective-permute-start = (bf16[128,2048]{1,0:T(8,128)(2,1)S(1)}, bf16[128,2048]{1,0:T(8,128)(2,1)S(1)}, u32[]{:S(2)}, u32[]{:S(2)}) collective-permute-start(bf16[128,2048]{1,0:T(8,128)(2,1)S(1)} %copy-done.6), channel_id=1, source_target_pairs={{0,480},{32,0},{64,32},{96,64},{128,96},{160,128},{192,160},{224,1... | collective-permute-start | bytes 1572872 | tf_op jit(solution)/shard_map/ppermute | solution.py:112
  20.7 43.2 %collective-permute-start.1 = (bf16[2048,256]{1,0:T(8,128)(2,1)}, bf16[2048,256]{1,0:T(8,128)(2,1)}, u32[]{:S(2)}, u32[]{:S(2)}) collective-permute-start(bf16[2048,256]{1,0:T(8,128)(2,1)} %bitcast.3), channel_id=1, source_target_pairs={{0,1},{1,0},{2,3},{3,2},{4,5},{5,4},{6,7},{7,6},{8,9},{9,8},{10,11... | collective-permute-start | bytes 3145736 | tf_op jit(solution)/shard_map/ppermute | solution.py:37
  25.8 71.5 %collective-permute-start.4 = (bf16[128,2048]{1,0:T(8,128)(2,1)}, bf16[128,2048]{1,0:T(8,128)(2,1)}, u32[]{:S(2)}, u32[]{:S(2)}) collective-permute-start(bf16[128,2048]{1,0:T(8,128)(2,1)} %bitcast.5), channel_id=1, source_target_pairs={{0,1},{1,0},{2,3},{3,2},{4,5},{5,4},{6,7},{7,6},{8,9},{9,8},{10,11... | collective-permute-start | bytes 1572872 | tf_op jit(solution)/shard_map/ppermute | solution.py:37
  28.1 32.0 %copy-start.1 = (bf16[128,2048]{1,0:T(8,128)(2,1)}, bf16[128,2048]{1,0:T(8,128)(2,1)S(1)}, u32[]{:S(2)}) copy-start(bf16[128,2048]{1,0:T(8,128)(2,1)S(1)} %collective-permute-done) | copy-start | bytes 1572868
  56.5 38.2 %all-to-all-start.1 = ((bf16[4,36,2048]{2,1,0:T(8,128)(2,1)}), bf16[4,36,2048]{2,1,0:T(8,128)(2,1)S(1)}, u32[]{:S(2)}, u32[]{:S(2)}) async-start(bf16[4,36,2048]{2,1,0:T(8,128)(2,1)} %reshape.165), calls=%async_computation.1 | async-start | bytes 1310720 | tf_op jit(solution)/shard_map/all_to_all | solution.py:152
  63.9 40.6 %collective-permute-start.3 = (bf16[144,2048]{1,0:T(8,128)(2,1)}, bf16[144,2048]{1,0:T(8,128)(2,1)}, u32[]{:S(2)}, u32[]{:S(2)}) collective-permute-start(bf16[144,2048]{1,0:T(8,128)(2,1)} %reshape.164), channel_id=1, source_target_pairs={{2,0},{4,2},{6,4},{8,6},{10,8},{12,10},{14,12},{16,14},{18,16},{20... | collective-permute-start | bytes 1769480 | tf_op jit(solution)/shard_map/ppermute | solution.py:29
  70.5 34.1 %collective-permute-start.2 = (bf16[144,2048]{1,0:T(8,128)(2,1)}, bf16[144,2048]{1,0:T(8,128)(2,1)}, u32[]{:S(2)}, u32[]{:S(2)}) collective-permute-start(bf16[144,2048]{1,0:T(8,128)(2,1)} %reshape.164), channel_id=1, source_target_pairs={{0,2},{2,4},{4,6},{6,8},{8,10},{10,12},{12,14},{14,16},{16,18},{18... | collective-permute-start | bytes 1769480 | tf_op jit(solution)/shard_map/ppermute | solution.py:25
  97.3 18.2 %collective-permute-start.10 = (bf16[144,2048]{1,0:T(8,128)(2,1)S(1)}, bf16[144,2048]{1,0:T(8,128)(2,1)S(1)}, u32[]{:S(2)}, u32[]{:S(2)}) collective-permute-start(bf16[144,2048]{1,0:T(8,128)(2,1)S(1)} %reshape.166.g_ref), channel_id=1, source_target_pairs={{2,0},{4,2},{6,4},{8,6},{10,8},{12,10},{14,12},{16,14},{18,16},{20... | collective-permute-start | bytes 1769480 | tf_op jit(solution)/shard_map/ppermute | solution.py:29
  99.3 18.3 %collective-permute-start.9 = (bf16[144,2048]{1,0:T(8,128)(2,1)S(1)}, bf16[144,2048]{1,0:T(8,128)(2,1)S(1)}, u32[]{:S(2)}, u32[]{:S(2)}) collective-permute-start(bf16[144,2048]{1,0:T(8,128)(2,1)S(1)} %reshape.166.g_ref), channel_id=1, source_target_pairs={{0,2},{2,4},{4,6},{6,8},{8,10},{10,12},{12,14},{14,16},{16,18},{18... | collective-permute-start | bytes 1769480 | tf_op jit(solution)/shard_map/ppermute | solution.py:25
  105.9 22.3 %collective-permute-start.5 = (bf16[144,2048]{1,0:T(8,128)(2,1)}, bf16[144,2048]{1,0:T(8,128)(2,1)S(1)}, u32[]{:S(2)}, u32[]{:S(2)}) collective-permute-start(bf16[144,2048]{1,0:T(8,128)(2,1)} %collective-permute-done.3), channel_id=1, source_target_pairs={{2,0},{4,2},{6,4},{8,6},{10,8},{12,10},{14,12},{16,14},{18,16},{20... | collective-permute-start | bytes 1769480 | tf_op jit(solution)/shard_map/ppermute | solution.py:29
  109.0 20.5 %collective-permute-start.7 = (bf16[144,2048]{1,0:T(8,128)(2,1)}, bf16[144,2048]{1,0:T(8,128)(2,1)S(1)}, u32[]{:S(2)}, u32[]{:S(2)}) collective-permute-start(bf16[144,2048]{1,0:T(8,128)(2,1)} %collective-permute-done.2), channel_id=1, source_target_pairs={{0,2},{2,4},{4,6},{6,8},{8,10},{10,12},{12,14},{14,16},{16,18},{18... | collective-permute-start | bytes 1769480 | tf_op jit(solution)/shard_map/ppermute | solution.py:25
  115.5 25.3 %collective-permute-start.12 = (bf16[144,2048]{1,0:T(8,128)(2,1)S(1)}, bf16[144,2048]{1,0:T(8,128)(2,1)S(1)}, u32[]{:S(2)}, u32[]{:S(2)}) collective-permute-start(bf16[144,2048]{1,0:T(8,128)(2,1)S(1)} %collective-permute-done.10), channel_id=1, source_target_pairs={{2,0},{4,2},{6,4},{8,6},{10,8},{12,10},{14,12},{16,14},{18,16},{20... | collective-permute-start | bytes 1769480 | tf_op jit(solution)/shard_map/ppermute | solution.py:29
  117.6 23.2 %collective-permute-start.13 = (bf16[144,2048]{1,0:T(8,128)(2,1)S(1)}, bf16[144,2048]{1,0:T(8,128)(2,1)S(1)}, u32[]{:S(2)}, u32[]{:S(2)}) collective-permute-start(bf16[144,2048]{1,0:T(8,128)(2,1)S(1)} %collective-permute-done.9), channel_id=1, source_target_pairs={{0,2},{2,4},{4,6},{6,8},{8,10},{10,12},{12,14},{14,16},{16,18},{18... | collective-permute-start | bytes 1769480 | tf_op jit(solution)/shard_map/ppermute | solution.py:25
  130.1 22.8 %collective-permute-start.6 = (bf16[144,2048]{1,0:T(8,128)(2,1)S(1)}, bf16[144,2048]{1,0:T(8,128)(2,1)S(1)}, u32[]{:S(2)}, u32[]{:S(2)}) collective-permute-start(bf16[144,2048]{1,0:T(8,128)(2,1)S(1)} %collective-permute-done.5), channel_id=1, source_target_pairs={{2,0},{3,1},{10,8},{11,9},{18,16},{19,17},{26,24},{27,25},{34,32},... | collective-permute-start | bytes 1769480 | tf_op jit(solution)/shard_map/ppermute | solution.py:33
  131.4 22.2 %collective-permute-start.8 = (bf16[144,2048]{1,0:T(8,128)(2,1)S(1)}, bf16[144,2048]{1,0:T(8,128)(2,1)S(1)}, u32[]{:S(2)}, u32[]{:S(2)}) collective-permute-start(bf16[144,2048]{1,0:T(8,128)(2,1)S(1)} %collective-permute-done.7), channel_id=1, source_target_pairs={{4,6},{5,7},{12,14},{13,15},{20,22},{21,23},{28,30},{29,31},{36,38... | collective-permute-start | bytes 1769480 | tf_op jit(solution)/shard_map/ppermute | solution.py:33
  142.8 18.6 %collective-permute-start.16 = (bf16[160,2048]{1,0:T(8,128)(2,1)S(1)}, bf16[160,2048]{1,0:T(8,128)(2,1)S(1)}, u32[]{:S(2)}, u32[]{:S(2)}) collective-permute-start(bf16[160,2048]{1,0:T(8,128)(2,1)S(1)} %get-tuple-element.58), channel_id=1, source_target_pairs={{6,4},{4,2},{7,5},{5,3},{14,12},{12,10},{15,13},{13,11},{22,20},{2... | collective-permute-start | bytes 1966088 | tf_op jit(solution)/shard_map/ppermute | solution.py:33
  143.5 17.9 %collective-permute-start.14 = (bf16[160,2048]{1,0:T(8,128)(2,1)S(1)}, bf16[160,2048]{1,0:T(8,128)(2,1)S(1)}, u32[]{:S(2)}, u32[]{:S(2)}) collective-permute-start(bf16[160,2048]{1,0:T(8,128)(2,1)S(1)} %get-tuple-element.58), channel_id=1, source_target_pairs={{0,2},{2,4},{1,3},{3,5},{8,10},{10,12},{9,11},{11,13},{16,18},{18,... | collective-permute-start | bytes 1966088 | tf_op jit(solution)/shard_map/ppermute | solution.py:33
  145.5 19.4 %collective-permute-start.18 = (bf16[144,2048]{1,0:T(8,128)(2,1)S(1)}, bf16[144,2048]{1,0:T(8,128)(2,1)S(1)}, u32[]{:S(2)}, u32[]{:S(2)}) collective-permute-start(bf16[144,2048]{1,0:T(8,128)(2,1)S(1)} %collective-permute-done.12), channel_id=1, source_target_pairs={{2,0},{3,1},{10,8},{11,9},{18,16},{19,17},{26,24},{27,25},{34,32},... | collective-permute-start | bytes 1769480 | tf_op jit(solution)/shard_map/ppermute | solution.py:33
  152.8 12.2 %collective-permute-start.19 = (bf16[144,2048]{1,0:T(8,128)(2,1)S(1)}, bf16[144,2048]{1,0:T(8,128)(2,1)S(1)}, u32[]{:S(2)}, u32[]{:S(2)}) collective-permute-start(bf16[144,2048]{1,0:T(8,128)(2,1)S(1)} %collective-permute-done.13), channel_id=1, source_target_pairs={{4,6},{5,7},{12,14},{13,15},{20,22},{21,23},{28,30},{29,31},{36,38... | collective-permute-start | bytes 1769480 | tf_op jit(solution)/shard_map/ppermute | solution.py:33
  157.4 34.8 %collective-permute-start.11 = (bf16[160,2048]{1,0:T(8,128)(2,1)S(1)}, bf16[160,2048]{1,0:T(8,128)(2,1)S(1)}, u32[]{:S(2)}, u32[]{:S(2)}) collective-permute-start(bf16[160,2048]{1,0:T(8,128)(2,1)S(1)} %get-tuple-element.53), channel_id=1, source_target_pairs={{0,2},{6,4},{1,3},{7,5},{8,10},{14,12},{9,11},{15,13},{16,18},{22,... | collective-permute-start | bytes 1966088 | tf_op jit(solution)/shard_map/ppermute | solution.py:33
  161.8 30.3 %collective-permute-start.17 = (bf16[160,2048]{1,0:T(8,128)(2,1)S(1)}, bf16[160,2048]{1,0:T(8,128)(2,1)S(1)}, u32[]{:S(2)}, u32[]{:S(2)}) collective-permute-start(bf16[160,2048]{1,0:T(8,128)(2,1)S(1)} %get-tuple-element.80), channel_id=1, source_target_pairs={{4,2},{2,0},{5,3},{3,1},{12,10},{10,8},{13,11},{11,9},{20,18},{18,... | collective-permute-start | bytes 1966088 | tf_op jit(solution)/shard_map/ppermute | solution.py:33
  163.3 28.9 %collective-permute-start.15 = (bf16[160,2048]{1,0:T(8,128)(2,1)S(1)}, bf16[160,2048]{1,0:T(8,128)(2,1)S(1)}, u32[]{:S(2)}, u32[]{:S(2)}) collective-permute-start(bf16[160,2048]{1,0:T(8,128)(2,1)S(1)} %get-tuple-element.81), channel_id=1, source_target_pairs={{2,4},{4,6},{3,5},{5,7},{10,12},{12,14},{11,13},{13,15},{18,20},{2... | collective-permute-start | bytes 1966088 | tf_op jit(solution)/shard_map/ppermute | solution.py:33
  167.0 25.2 %collective-permute-start.20 = (bf16[160,2048]{1,0:T(8,128)(2,1)S(1)}, bf16[160,2048]{1,0:T(8,128)(2,1)S(1)}, u32[]{:S(2)}, u32[]{:S(2)}) collective-permute-start(bf16[160,2048]{1,0:T(8,128)(2,1)S(1)} %get-tuple-element.61), channel_id=1, source_target_pairs={{0,6},{6,0},{1,7},{7,1},{8,14},{14,8},{9,15},{15,9},{16,22},{22,16... | collective-permute-start | bytes 1966088 | tf_op jit(solution)/shard_map/ppermute | solution.py:33
  173.8 13.3 %collective-permute-start.21 = (bf16[128,2048]{1,0:T(8,128)(2,1)S(1)}, bf16[128,2048]{1,0:T(8,128)(2,1)S(1)}, u32[]{:S(2)}, u32[]{:S(2)}) collective-permute-start(bf16[128,2048]{1,0:T(8,128)(2,1)S(1)} %convolution_convert_fusion.3), channel_id=1, source_target_pairs={{0,1},{1,0},{2,3},{3,2},{4,5},{5,4},{6,7},{7,6},{8,9},{9,8},{10,11... | collective-permute-start | bytes 1572872 | tf_op jit(solution)/shard_map/ppermute | solution.py:37
  187.1 45.2 %collective-permute-start.25 = (bf16[2048,256]{1,0:T(8,128)(2,1)S(1)}, bf16[2048,256]{1,0:T(8,128)(2,1)S(1)}, u32[]{:S(2)}, u32[]{:S(2)}) collective-permute-start(bf16[2048,256]{1,0:T(8,128)(2,1)S(1)} %convolution_convert_fusion), channel_id=1, source_target_pairs={{0,1},{1,0},{2,3},{3,2},{4,5},{5,4},{6,7},{7,6},{8,9},{9,8},{10,11... | collective-permute-start | bytes 3145736 | tf_op jit(solution)/shard_map/ppermute | solution.py:37
  192.8 27.2 %collective-permute-start.24 = (bf16[40,2048]{1,0:T(8,128)(2,1)S(1)}, bf16[40,2048]{1,0:T(8,128)(2,1)S(1)}, u32[]{:S(2)}, u32[]{:S(2)}) collective-permute-start(bf16[40,2048]{1,0:T(8,128)(2,1)S(1)} %get-tuple-element.91), channel_id=1, source_target_pairs={{0,8},{8,16},{16,24},{24,0},{1,9},{9,17},{17,25},{25,1},{2,10},{10... | collective-permute-start | bytes 491528 | tf_op jit(solution)/shard_map/ppermute | solution.py:133
  199.5 29.1 %collective-permute-start.23 = (bf16[40,2048]{1,0:T(8,128)(2,1)S(1)}, bf16[40,2048]{1,0:T(8,128)(2,1)S(1)}, u32[]{:S(2)}, u32[]{:S(2)}) collective-permute-start(bf16[40,2048]{1,0:T(8,128)(2,1)S(1)} %get-tuple-element.92), channel_id=1, source_target_pairs={{0,16},{8,24},{16,0},{24,8},{1,17},{9,25},{17,1},{25,9},{2,18},{10... | collective-permute-start | bytes 491528 | tf_op jit(solution)/shard_map/ppermute | solution.py:133
  206.5 25.7 %collective-permute-start.22 = (bf16[40,2048]{1,0:T(8,128)(2,1)S(1)}, bf16[40,2048]{1,0:T(8,128)(2,1)S(1)}, u32[]{:S(2)}, u32[]{:S(2)}) collective-permute-start(bf16[40,2048]{1,0:T(8,128)(2,1)S(1)} %get-tuple-element.93), channel_id=1, source_target_pairs={{0,24},{8,0},{16,8},{24,16},{1,25},{9,1},{17,9},{25,17},{2,26},{10... | collective-permute-start | bytes 491528 | tf_op jit(solution)/shard_map/ppermute | solution.py:133
  (4 other events, 25.2 us)

commit v6 on v5

--- a/solution.py
+++ b/solution.py
@@ -41,7 +41,7 @@
     return lax.optimization_barrier((a, *others))[0]
 
 
-def slice_kernel(cap, zo_ref, gu_ref, g_ref, w_ref, wd_ref, own_ref, other_ref, h_ref, dx_ref):
+def slice_kernel(cap, at_ref, gu_ref, g_ref, w_ref, wd_ref, own_ref, other_ref, h_ref, dx_ref):
     rows, hid2 = h_ref.shape
     hidden = hid2 // 2
     padded, width = dx_ref.shape
@@ -60,7 +60,8 @@
     other_ref[:, hidden:] = dupper[:, hidden:]
     to = lax.broadcasted_iota(jnp.int32, (padded, rows), 0)
     of = lax.broadcasted_iota(jnp.int32, (padded, rows), 1)
-    pick = ((to // pitch * cap + to % pitch == of) & (to % pitch < cap)).astype(BF)
+    group = (at_ref[1] + EXPERTS - to // pitch) % EXPERTS
+    pick = ((group * cap + to % pitch == of) & (to % pitch < cap)).astype(BF)
     dgu = jnp.concatenate([dgate, dupper], axis=1)
     dgu = dot(pick, dgu, 1, 0).astype(BF)
     dx = dot(dgu, w_ref[...], 1, 1)
@@ -74,12 +75,12 @@
     line = jnp.concatenate([line, jnp.zeros((8, LANES - rows), F32)], axis=1)
     line = jnp.concatenate([line] * (width // LANES), axis=1)[:1]
     lane = lax.broadcasted_iota(jnp.int32, (1, width), 1)
-    line = jnp.where(lane // LANES == zo_ref[0], line, 0.0)
+    line = jnp.where(lane // LANES == at_ref[0], line, 0.0)
     row = lax.broadcasted_iota(jnp.int32, (padded, width), 0)
     dx_ref[...] = jnp.where(row % pitch == cap, line, dx).astype(BF)
 
 
-def slice_backward(cap, zo, gu, g, w, wd):
+def slice_backward(cap, at, gu, g, w, wd):
     rows, width = g.shape
     hid2 = wd.shape[0]
     whole = pl.BlockSpec(memory_space=pltpu.VMEM)
@@ -97,7 +98,7 @@
         cost_estimate=pl.CostEstimate(
             flops=2 * rows * width * 3 * hid2, bytes_accessed=5 * 2**20, transcendentals=0
         ),
-    )(zo, gu, g, w, wd)
+    )(at, gu, g, w, wd)
 
 
 def per_device(tokens, upstream, expert_ids, combine, w_gate_up, w_down):
@@ -121,12 +122,10 @@
     rel = (ids - zb) % EXPERTS
     weight = combine.astype(F32)
     scaled = (weight * out_grad.astype(F32)).astype(BF)
-    place = (
-        jnp.arange(EXPERTS * cap, dtype=jnp.int32)[:, None]
-        == (ids * cap + slot)[None, :]
-    ).astype(BF)
-
-    def dispatch(a):
+    row = jnp.arange(EXPERTS * cap, dtype=jnp.int32)[:, None]
+
+    def dispatch(a, expert):
+        place = (row == (expert * cap + slot)[None, :]).astype(BF)
         return dot(place, a, 1, 0).astype(BF).reshape(EXPERTS, cap, width)
 
     def block(a, k):
@@ -146,13 +145,12 @@
         units = [unit, where(odd, r1, l1), early, where(zo < 2, l2, r2)]
         return units, whole
 
-    from_block = (zb - jnp.arange(EXPERTS)) % EXPERTS
-
-    def to_blocks(a):
-        units = lax.all_to_all(dispatch(a), "zb", 0, 0, tiled=True)
-        return units[from_block].reshape(-1, width)
-
-    unit_x, unit_g = to_blocks(tokens), to_blocks(scaled)
+    unit_x = lax.all_to_all(dispatch(tokens, ids), "zb", 0, 0, tiled=True)
+    unit_x = unit_x[(zb - jnp.arange(EXPERTS)) % EXPERTS].reshape(-1, width)
+    sent = dispatch(scaled, rel)
+    came = [block(sent[k], k) for k in (2, 1, 3)]
+    g2, g1, g3, _ = lax.optimization_barrier((*came, unit_x))
+    unit_g = jnp.concatenate([sent[0], g1, g2, g3], axis=0)
     wgu_other, wdown_other = across(wgu), across(wdown)
     unit_x, wgu_other = lax.optimization_barrier((unit_x, wgu_other))
     unit_g, wdown_other = lax.optimization_barrier((unit_g, wdown_other))
@@ -162,24 +160,26 @@
     (xs, x3), (gs, g3) = relay(unit_x), relay(unit_g)
 
     forward = lambda x: dot(x, wgu_all, 1, 0)
-    expert = lambda gu, g: slice_backward(cap, zo[None], gu, g, wgu_all, wdown_all)
+    at = jnp.stack([zo, zb]).astype(jnp.int32)
+    expert = lambda gu, g: slice_backward(cap, at, gu, g, wgu_all, wdown_all)
     gus = [forward(after(xs[k], xs[l])) for k, l in ((0, 1), (1, 3), (2, 3))]
     x3 = x3(*gus)
     gus.append(forward(after(xs[3], gs[1])))
     gu3 = forward(x3)
-    early = (x3, x3, x3, gs[3])
+    early = (x3, x3, x3, x3)
     done = [expert(gu, after(g, e)) for gu, g, e in zip(gus, gs, early)]
 
     add = lambda *terms: sum(a.astype(F32) for a in terms).astype(BF)
     d0, d1, d3_early, d2 = (d[3] for d in done)
-    near = line(d1, (0, 1), (3, 2))
     r2, l2 = line(d2, (0, 1), (1, 2)), line(d2, (3, 2), (2, 1))
     to_r1 = add(where(zo == 1, d3_early, d1), r2)
     to_l1 = add(where(zo == 2, d3_early, d1), l2)
-    r1, l1 = line(to_r1, (1, 2), (2, 3)), line(to_l1, (2, 1), (1, 0))
-    g3 = g3(to_r1, to_l1, gu3)
+    g3 = g3(gu3, d0, d2, d3_early)
     done[2] = expert(gu3, g3)
     far = line(done[2][3], (0, 3), (3, 0))
+    to_r1, to_l1, _ = lax.optimization_barrier((to_r1, to_l1, done[2][3]))
+    r1 = line(to_r1, (0, 1), (1, 2), (2, 3))
+    l1 = line(to_l1, (3, 2), (2, 1), (1, 0))
     own, other, hids, _ = zip(*(done[k] for k in (0, 1, 3, 2)))
 
     cat = lambda arrays: jnp.concatenate(arrays, axis=0)
@@ -189,25 +189,24 @@
     other_down = dot(hid_all[:, hidden:], g_all, 0, 0).astype(BF)
 
     other_down = across(other_down)
-    dx = add(d0, near, r1, l1, after(far, other_gu, other_down))
-    dx = dx.reshape(EXPERTS, pitch, width)
-    far, up1, down1 = (block(dx[k], -k) for k in (2, 1, 3))
-    back = jnp.concatenate([dx[0], up1, far, down1], axis=0)
+    dx = add(d0, r1, l1, after(far, other_gu, other_down)).reshape(EXPERTS, pitch, width)
+    back = lax.all_to_all(dx, "zb", 0, 0, tiled=True).reshape(-1, width)
     other_gu = across(other_gu)
-    grad_gu = (dot(x_all, cat(own), 0, 0) + other_gu.astype(F32)).astype(BF)
+    own_gu = lax.optimization_barrier(dot(x_all, cat(own), 0, 0))
+    grad_gu = (own_gu + other_gu.astype(F32)).astype(BF)
     grad_down = dot(hid_all[:, :hidden], g_all, 0, 0) + other_down.astype(F32)
     grad_down = grad_down.astype(BF)
     back, grad_gu, grad_down = lax.optimization_barrier((back, grad_gu, grad_down))
 
     put = (
         jnp.arange(EXPERTS * pitch, dtype=jnp.int32)[:, None]
-        == (rel * pitch + slot)[None, :]
+        == (ids * pitch + slot)[None, :]
     ).astype(BF)
     moe = dot(put, back, 0, 0)
     input_grad = (out_grad.astype(F32) + moe).astype(BF)
     dp = back.reshape(EXPERTS, pitch, width)[:, cap, : LINE * LANES].astype(F32)
     dp = jnp.sum(dp.reshape(EXPERTS, LINE, LANES), axis=1)
-    pick = (rel[:, None] == jnp.arange(EXPERTS)[None, :])[:, :, None] & (
+    pick = (ids[:, None] == jnp.arange(EXPERTS)[None, :])[:, :, None] & (
         (rel * cap + slot)[:, None] == jnp.arange(LANES)[None, :]
     )[:, None, :]
     dp = jnp.sum(jnp.where(pick, dp[None], 0.0), axis=(1, 2))

time: 241 us -> 245 us (1.017)
  the two profiles are of different devices: /device:TPU:6 before, /device:TPU:50 now
where the time goes in v6:
time: 245 us; the launch traced here: 244 us
  starting transfers between devices  116 us (47%)
  waiting for transfers between devices  86 us (35%)
  matrix products  12.9 us (5%)
  Pallas kernels  12.3 us (5%)
  other arithmetic  8.9 us (4%)
  local copies, waits for them, and re-layouts  6.5 us (3%)
    ppermute x4, waiting for transfers between devices, across(): return lax.ppermute(a, 'yh', [(0, 1), (1, 0)])  28.1 us
    ppermute x4, starting transfers between devices, down(): lax.ppermute(a, ('zb', 'zo'), [((i + 1) % RING, i) for i in range(RING)])  24.2 us
    ppermute x3, starting transfers between devices, block(): lax.ppermute(a, 'zb', [(i, (i + k) % EXPERTS) for i in range(EXPERTS)])  22.4 us
    ppermute x9, starting transfers between devices, line(): return lax.ppermute(a, 'zo', pairs)  21.5 us
    ppermute x9, waiting for transfers between devices, line(): return lax.ppermute(a, 'zo', pairs)  19.9 us
    all_to_all x1, starting transfers between devices, per_device(): unit_x = lax.all_to_all(dispatch(tokens, ids), 'zb', 0, 0, tiled=True)  14.2 us
    dot_general x13, matrix products, dot(): lax.dot_general(a, b, (((ca,), (cb,)), ((), ())), preferred_element_type=...  12.9 us
    pallas_call x5, Pallas kernels, slice_backward(): pl.pallas_call(functools.partial(slice_kernel, cap), out_shape=(jax.Shape...  12.3 us
  transfers between devices with their start and end apart: 27, of which 16 were waited for; matrix products, arithmetic and copies ran while one was open for 8% of the time, Pallas kernels for 5%

profile of v6, /device:TPU:50, one launch (start us, length us, event | category | flops | bytes accessed | tf_op | source)
XLA Modules:
  0.0 244.2 jit_solution(16940275282170448169)
XLA Ops:
  3.5 14.2 %all-to-all-start = ((bf16[4,36,2048]{2,1,0:T(8,128)(2,1)}), bf16[4,36,2048]{2,1,0:T(8,128)(2,1)S(1)}, u32[]{:S(2)}, u32[]{:S(2)}) async-start(bf16[4,36,2048]{2,1,0:T(8,128)(2,1)} %reshape.171), calls=%async_computation | async-start | bytes 1310720 | tf_op jit(solution)/shard_map/all_to_all | solution.py:148
  17.7 2.2 collective-permute-start.1
  21.9 5.1 %collective-permute-start.7 = (bf16[128,2048]{1,0:T(8,128)(2,1)}, bf16[128,2048]{1,0:T(8,128)(2,1)}, u32[]{:S(2)}, u32[]{:S(2)}) collective-permute-start(bf16[128,2048]{1,0:T(8,128)(2,1)} %bitcast.6), channel_id=1, source_target_pairs={{0,1},{1,0},{2,3},{3,2},{4,5},{5,4},{6,7},{7,6},{8,9},{9,8},{10,11... | collective-permute-start | bytes 1572872 | tf_op jit(solution)/shard_map/ppermute | solution.py:37
  30.1 12.6 %collective-permute-start.4 = (bf16[36,2048]{1,0:T(8,128)(2,1)}, bf16[36,2048]{1,0:T(8,128)(2,1)S(1)}, u32[]{:S(2)}, u32[]{:S(2)}) collective-permute-start(bf16[36,2048]{1,0:T(8,128)(2,1)} %get-tuple-element.101), channel_id=1, source_target_pairs={{0,16},{8,24},{16,0},{24,8},{1,17},{9,25},{17,1},{25,9},{2,18},{10... | collective-permute-start | bytes 442376 | tf_op jit(solution)/shard_map/ppermute | solution.py:132
  42.8 2.5 %collective-permute-start.5 = (bf16[36,2048]{1,0:T(8,128)(2,1)}, bf16[36,2048]{1,0:T(8,128)(2,1)S(1)}, u32[]{:S(2)}, u32[]{:S(2)}) collective-permute-start(bf16[36,2048]{1,0:T(8,128)(2,1)} %get-tuple-element.100), channel_id=1, source_target_pairs={{0,8},{8,16},{16,24},{24,0},{1,9},{9,17},{17,25},{25,1},{2,10},{10... | collective-permute-start | bytes 442376 | tf_op jit(solution)/shard_map/ppermute | solution.py:132
  45.3 7.3 %collective-permute-start.6 = (bf16[36,2048]{1,0:T(8,128)(2,1)}, bf16[36,2048]{1,0:T(8,128)(2,1)S(1)}, u32[]{:S(2)}, u32[]{:S(2)}) collective-permute-start(bf16[36,2048]{1,0:T(8,128)(2,1)} %get-tuple-element.99), channel_id=1, source_target_pairs={{0,24},{8,0},{16,8},{24,16},{1,25},{9,1},{17,9},{25,17},{2,26},{10... | collective-permute-start | bytes 442376 | tf_op jit(solution)/shard_map/ppermute | solution.py:132
  52.6 5.6 %all-to-all-done = bf16[4,36,2048]{2,1,0:T(8,128)(2,1)S(1)} async-done(((bf16[4,36,2048]{2,1,0:T(8,128)(2,1)}), bf16[4,36,2048]{2,1,0:T(8,128)(2,1)S(1)}, u32[]{:S(2)}, u32[]{:S(2)}) %all-to-all-start) | async-done | bytes 589856 | tf_op jit(solution)/shard_map/all_to_all | solution.py:148
  59.0 17.8 %collective-permute-start.3 = (bf16[144,2048]{1,0:T(8,128)(2,1)S(1)}, bf16[144,2048]{1,0:T(8,128)(2,1)S(1)}, u32[]{:S(2)}, u32[]{:S(2)}) collective-permute-start(bf16[144,2048]{1,0:T(8,128)(2,1)S(1)} %reshape.172), channel_id=1, source_target_pairs={{2,0},{4,2},{6,4},{8,6},{10,8},{12,10},{14,12},{16,14},{18,16},{20... | collective-permute-start | bytes 1769480 | tf_op jit(solution)/shard_map/ppermute | solution.py:29
  78.8 5.3 %collective-permute-done.5 = bf16[36,2048]{1,0:T(8,128)(2,1)S(1)} collective-permute-done((bf16[36,2048]{1,0:T(8,128)(2,1)}, bf16[36,2048]{1,0:T(8,128)(2,1)S(1)}, u32[]{:S(2)}, u32[]{:S(2)}) %collective-permute-start.5) | collective-permute-done | bytes 147488 | tf_op jit(solution)/shard_map/ppermute | solution.py:132
  88.6 3.9 %collective-permute-start.13 = (bf16[144,2048]{1,0:T(8,128)(2,1)S(1)}, bf16[144,2048]{1,0:T(8,128)(2,1)S(1)}, u32[]{:S(2)}, u32[]{:S(2)}) collective-permute-start(bf16[144,2048]{1,0:T(8,128)(2,1)S(1)} %pad_maximum_fusion.4.g_ref), channel_id=1, source_target_pairs={{0,2},{2,4},{4,6},{6,8},{8,10},{10,12},{12,14},{14,16},{16,18},{18... | collective-permute-start | bytes 1769480 | tf_op jit(solution)/shard_map/ppermute | solution.py:25
  96.8 2.5 %collective-permute-start.8 = (bf16[144,2048]{1,0:T(8,128)(2,1)S(1)}, bf16[144,2048]{1,0:T(8,128)(2,1)S(1)}, u32[]{:S(2)}, u32[]{:S(2)}) collective-permute-start(bf16[144,2048]{1,0:T(8,128)(2,1)S(1)} %collective-permute-done.3), channel_id=1, source_target_pairs={{2,0},{4,2},{6,4},{8,6},{10,8},{12,10},{14,12},{16,14},{18,16},{20... | collective-permute-start | bytes 1769480 | tf_op jit(solution)/shard_map/ppermute | solution.py:29
  99.3 3.3 %collective-permute-start.10 = (bf16[144,2048]{1,0:T(8,128)(2,1)S(1)}, bf16[144,2048]{1,0:T(8,128)(2,1)S(1)}, u32[]{:S(2)}, u32[]{:S(2)}) collective-permute-start(bf16[144,2048]{1,0:T(8,128)(2,1)S(1)} %collective-permute-done.2), channel_id=1, source_target_pairs={{0,2},{2,4},{4,6},{6,8},{8,10},{10,12},{12,14},{14,16},{16,18},{18... | collective-permute-start | bytes 1769480 | tf_op jit(solution)/shard_map/ppermute | solution.py:25
  106.8 2.5 %collective-permute-done.13 = bf16[144,2048]{1,0:T(8,128)(2,1)S(1)} collective-permute-done((bf16[144,2048]{1,0:T(8,128)(2,1)S(1)}, bf16[144,2048]{1,0:T(8,128)(2,1)S(1)}, u32[]{:S(2)}, u32[]{:S(2)}) %collective-permute-start.13) | collective-permute-done | bytes 589856 | tf_op jit(solution)/shard_map/ppermute | solution.py:25
  111.3 6.2 %collective-permute-done.8 = bf16[144,2048]{1,0:T(8,128)(2,1)S(1)} collective-permute-done((bf16[144,2048]{1,0:T(8,128)(2,1)S(1)}, bf16[144,2048]{1,0:T(8,128)(2,1)S(1)}, u32[]{:S(2)}, u32[]{:S(2)}) %collective-permute-start.8) | collective-permute-done | bytes 589856 | tf_op jit(solution)/shard_map/ppermute | solution.py:29
  117.6 4.4 %collective-permute-done.10 = bf16[144,2048]{1,0:T(8,128)(2,1)S(1)} collective-permute-done((bf16[144,2048]{1,0:T(8,128)(2,1)S(1)}, bf16[144,2048]{1,0:T(8,128)(2,1)S(1)}, u32[]{:S(2)}, u32[]{:S(2)}) %collective-permute-start.10) | collective-permute-done | bytes 589856 | tf_op jit(solution)/shard_map/ppermute | solution.py:25
  122.5 2.5 %collective-permute-start.9 = (bf16[144,2048]{1,0:T(8,128)(2,1)S(1)}, bf16[144,2048]{1,0:T(8,128)(2,1)S(1)}, u32[]{:S(2)}, u32[]{:S(2)}) collective-permute-start(bf16[144,2048]{1,0:T(8,128)(2,1)S(1)} %collective-permute-done.8), channel_id=1, source_target_pairs={{2,0},{3,1},{10,8},{11,9},{18,16},{19,17},{26,24},{27,25},{34,32},... | collective-permute-start | bytes 1769480 | tf_op jit(solution)/shard_map/ppermute | solution.py:33
  126.7 3.5 %collective-permute-done.14 = bf16[144,2048]{1,0:T(8,128)(2,1)S(1)} collective-permute-done((bf16[144,2048]{1,0:T(8,128)(2,1)S(1)}, bf16[144,2048]{1,0:T(8,128)(2,1)S(1)}, u32[]{:S(2)}, u32[]{:S(2)}) %collective-permute-start.14) | collective-permute-done | bytes 589856 | tf_op jit(solution)/shard_map/ppermute | solution.py:29
  131.9 2.5 %collective-permute-done.15 = bf16[144,2048]{1,0:T(8,128)(2,1)S(1)} collective-permute-done((bf16[144,2048]{1,0:T(8,128)(2,1)S(1)}, bf16[144,2048]{1,0:T(8,128)(2,1)S(1)}, u32[]{:S(2)}, u32[]{:S(2)}) %collective-permute-start.15) | collective-permute-done | bytes 589856 | tf_op jit(solution)/shard_map/ppermute | solution.py:25
  135.2 5.0 %collective-permute-done.9 = bf16[144,2048]{1,0:T(8,128)(2,1)S(1)} collective-permute-done((bf16[144,2048]{1,0:T(8,128)(2,1)S(1)}, bf16[144,2048]{1,0:T(8,128)(2,1)S(1)}, u32[]{:S(2)}, u32[]{:S(2)}) %collective-permute-start.9) | collective-permute-done | bytes 589856 | tf_op jit(solution)/shard_map/ppermute | solution.py:33
  140.3 2.5 %shard_map.96 = (bf16[144,256]{1,0:T(8,128)(2,1)S(1)}, bf16[144,256]{1,0:T(8,128)(2,1)S(1)}, bf16[144,256]{1,0:T(8,128)(2,1)S(1)}, bf16[160,2048]{1,0:T(8,128)(2,1)S(1)}) custom-call(s32[2]{0:T(128)S(1)} %pad_add_fusion.at_ref, f32[144,512]{1,0:T(8,128)S(1)} %fusion.47.gu_ref, bf16[144,2048]{1,0:T(8,128)(2,1)S(1)} %broadcast_select_fusion.g_ref, ...), custom_call_target="tpu_custom_call" | custom-call | flops 452984832 | bytes 5242880 | tf_op jit(solution)/shard_map/pallas_call | solution.py:87
  144.0 6.7 %collective-permute-start.16 = (bf16[160,2048]{1,0:T(8,128)(2,1)S(1)}, bf16[160,2048]{1,0:T(8,128)(2,1)S(1)}, u32[]{:S(2)}, u32[]{:S(2)}) collective-permute-start(bf16[160,2048]{1,0:T(8,128)(2,1)S(1)} %get-tuple-element.66), channel_id=1, source_target_pairs={{0,2},{2,4},{1,3},{3,5},{8,10},{10,12},{9,11},{11,13},{16,18},{18,... | collective-permute-start | bytes 1966088 | tf_op jit(solution)/shard_map/ppermute | solution.py:33
  150.7 2.5 %shard_map.93 = (bf16[144,256]{1,0:T(8,128)(2,1)S(1)}, bf16[144,256]{1,0:T(8,128)(2,1)S(1)}, bf16[144,256]{1,0:T(8,128)(2,1)S(1)}, bf16[160,2048]{1,0:T(8,128)(2,1)S(1)}) custom-call(s32[2]{0:T(128)S(1)} %pad_add_fusion.at_ref, f32[144,512]{1,0:T(8,128)S(1)} %fusion.44.gu_ref, bf16[144,2048]{1,0:T(8,128)(2,1)S(1)} %pad_maximum_fusion.4.g_ref, ...), custom_call_target="tpu_custom_call" | custom-call | flops 452984832 | bytes 5242880 | tf_op jit(solution)/shard_map/pallas_call | solution.py:87
  153.2 2.5 %shard_map.94 = (bf16[144,256]{1,0:T(8,128)(2,1)}, bf16[144,256]{1,0:T(8,128)(2,1)}, bf16[144,256]{1,0:T(8,128)(2,1)}, bf16[160,2048]{1,0:T(8,128)(2,1)S(1)}) custom-call(s32[2]{0:T(128)S(1)} %pad_add_fusion.at_ref, f32[144,512]{1,0:T(8,128)S(1)} %fusion.46.gu_ref, bf16[144,2048]{1,0:T(8,128)(2,1)S(1)} %get-tuple-element.60.g_ref, ...), custom_call_target="tpu_custom_call" | custom-call | flops 452984832 | bytes 5242880 | tf_op jit(solution)/shard_map/pallas_call | solution.py:87
  156.3 2.5 %shard_map.97 = (bf16[144,256]{1,0:T(8,128)(2,1)S(1)}, bf16[144,256]{1,0:T(8,128)(2,1)S(1)}, bf16[144,256]{1,0:T(8,128)(2,1)S(1)}, bf16[160,2048]{1,0:T(8,128)(2,1)S(1)}) custom-call(s32[2]{0:T(128)S(1)} %pad_add_fusion.at_ref, f32[144,512]{1,0:T(8,128)S(1)} %fusion.48.gu_ref, bf16[144,2048]{1,0:T(8,128)(2,1)S(1)} %select_select_fusion.g_ref, ...), custom_call_target="tpu_custom_call" | custom-call | flops 452984832 | bytes 5242880 | tf_op jit(solution)/shard_map/pallas_call | solution.py:87
  159.6 2.5 %shard_map.95 = (bf16[144,256]{1,0:T(8,128)(2,1)S(1)}, bf16[144,256]{1,0:T(8,128)(2,1)S(1)}, bf16[144,256]{1,0:T(8,128)(2,1)S(1)}, bf16[160,2048]{1,0:T(8,128)(2,1)S(1)}) custom-call(s32[2]{0:T(128)S(1)} %pad_add_fusion.at_ref, f32[144,512]{1,0:T(8,128)S(1)} %fusion.45.gu_ref, bf16[144,2048]{1,0:T(8,128)(2,1)S(1)} %get-tuple-element.62.g_ref, ...), custom_call_target="tpu_custom_call" | custom-call | flops 452984832 | bytes 5242880 | tf_op jit(solution)/shard_map/pallas_call | solution.py:87
  162.6 14.4 %collective-permute-done.16 = bf16[160,2048]{1,0:T(8,128)(2,1)S(1)} collective-permute-done((bf16[160,2048]{1,0:T(8,128)(2,1)S(1)}, bf16[160,2048]{1,0:T(8,128)(2,1)S(1)}, u32[]{:S(2)}, u32[]{:S(2)}) %collective-permute-start.16) | collective-permute-done | bytes 655392 | tf_op jit(solution)/shard_map/ppermute | solution.py:33
  179.6 4.9 %collective-permute-start.20 = (bf16[160,2048]{1,0:T(8,128)(2,1)S(1)}, bf16[160,2048]{1,0:T(8,128)(2,1)S(1)}, u32[]{:S(2)}, u32[]{:S(2)}) collective-permute-start(bf16[160,2048]{1,0:T(8,128)(2,1)S(1)} %get-tuple-element.70), channel_id=1, source_target_pairs={{0,2},{2,4},{4,6},{1,3},{3,5},{5,7},{8,10},{10,12},{12,14},{9,11},... | collective-permute-start | bytes 1966088 | tf_op jit(solution)/shard_map/ppermute | solution.py:33
  189.1 8.6 %collective-permute-done.23 = bf16[128,2048]{1,0:T(8,128)(2,1)S(1)} collective-permute-done((bf16[128,2048]{1,0:T(8,128)(2,1)S(1)}, bf16[128,2048]{1,0:T(8,128)(2,1)S(1)}, u32[]{:S(2)}, u32[]{:S(2)}) %collective-permute-start.23) | collective-permute-done | bytes 524320 | tf_op jit(solution)/shard_map/ppermute | solution.py:37
  199.0 9.6 %all-to-all-start.1 = ((bf16[4,40,2048]{2,1,0:T(8,128)(2,1)}), bf16[4,40,2048]{2,1,0:T(8,128)(2,1)}, u32[]{:S(2)}, u32[]{:S(2)}) async-start(bf16[4,40,2048]{2,1,0:T(8,128)(2,1)} %bitcast.39), calls=%async_computation.1 | async-start | bytes 1310720 | tf_op jit(solution)/shard_map/all_to_all | solution.py:193
  211.0 2.7 %fusion.6 = f32[2048,256]{1,0:T(8,128)S(1)} fusion(bf16[144,2048]{1,0:T(8,128)(2,1)} %copy-done.5, bf16[144,2048]{1,0:T(8,128)(2,1)} %copy-done.4, bf16[144,2048]{1,0:T(8,128)(2,1)} %copy-done.1, bf16[144,2048]{1,0:T(8,128)(2,1)} %copy-done.2, bf16[144,256]{1,0:T(8,128)(2,1)S(1)} %get-tuple-element.84, bf16[144,256]{1,0:T(8,128)(2,1)S(1)} %get-tuple-element.83, ...), kind=kOutput, calls=%fused_computation.32 | convolution fusion | flops 614596608 | bytes 4751360 | tf_op jit(solution)/shard_map/dot_general | solution.py:21
  215.1 19.5 %collective-permute-done.24 = bf16[2048,256]{1,0:T(8,128)(2,1)S(1)} collective-permute-done((bf16[2048,256]{1,0:T(8,128)(2,1)}, bf16[2048,256]{1,0:T(8,128)(2,1)S(1)}, u32[]{:S(2)}, u32[]{:S(2)}) %collective-permute-start.24) | collective-permute-done | bytes 1048608 | tf_op jit(solution)/shard_map/ppermute | solution.py:37
  235.9 4.3 %all-to-all-done.1 = bf16[4,40,2048]{2,1,0:T(8,128)(2,1)} async-done(((bf16[4,40,2048]{2,1,0:T(8,128)(2,1)}), bf16[4,40,2048]{2,1,0:T(8,128)(2,1)}, u32[]{:S(2)}, u32[]{:S(2)}) %all-to-all-start.1) | async-done | bytes 655392 | tf_op jit(solution)/shard_map/all_to_all | solution.py:193
  (105 shorter events, 50.8 us)
Async XLA Ops:
  3.5 54.7 %all-to-all-start = ((bf16[4,36,2048]{2,1,0:T(8,128)(2,1)}), bf16[4,36,2048]{2,1,0:T(8,128)(2,1)S(1)}, u32[]{:S(2)}, u32[]{:S(2)}) async-start(bf16[4,36,2048]{2,1,0:T(8,128)(2,1)} %reshape.171), calls=%async_computation | async-start | bytes 1310720 | tf_op jit(solution)/shard_map/all_to_all | solution.py:148
  17.7 41.3 %collective-permute-start.1 = (bf16[2048,256]{1,0:T(8,128)(2,1)}, bf16[2048,256]{1,0:T(8,128)(2,1)}, u32[]{:S(2)}, u32[]{:S(2)}) collective-permute-start(bf16[2048,256]{1,0:T(8,128)(2,1)} %bitcast.4), channel_id=1, source_target_pairs={{0,1},{1,0},{2,3},{3,2},{4,5},{5,4},{6,7},{7,6},{8,9},{9,8},{10,11... | collective-permute-start | bytes 3145736 | tf_op jit(solution)/shard_map/ppermute | solution.py:37
  19.9 8.9 %collective-permute-start = (bf16[128,2048]{1,0:T(8,128)(2,1)}, bf16[128,2048]{1,0:T(8,128)(2,1)S(1)}, u32[]{:S(2)}, u32[]{:S(2)}) collective-permute-start(bf16[128,2048]{1,0:T(8,128)(2,1)} %param.7), channel_id=1, source_target_pairs={{0,480},{32,0},{64,32},{96,64},{128,96},{160,128},{192,160},{224,1... | collective-permute-start | bytes 1572872 | tf_op jit(solution)/shard_map/ppermute | solution.py:113
  21.9 64.8 %collective-permute-start.7 = (bf16[128,2048]{1,0:T(8,128)(2,1)}, bf16[128,2048]{1,0:T(8,128)(2,1)}, u32[]{:S(2)}, u32[]{:S(2)}) collective-permute-start(bf16[128,2048]{1,0:T(8,128)(2,1)} %bitcast.6), channel_id=1, source_target_pairs={{0,1},{1,0},{2,3},{3,2},{4,5},{5,4},{6,7},{7,6},{8,9},{9,8},{10,11... | collective-permute-start | bytes 1572872 | tf_op jit(solution)/shard_map/ppermute | solution.py:37
  30.1 46.7 %collective-permute-start.4 = (bf16[36,2048]{1,0:T(8,128)(2,1)}, bf16[36,2048]{1,0:T(8,128)(2,1)S(1)}, u32[]{:S(2)}, u32[]{:S(2)}) collective-permute-start(bf16[36,2048]{1,0:T(8,128)(2,1)} %get-tuple-element.101), channel_id=1, source_target_pairs={{0,16},{8,24},{16,0},{24,8},{1,17},{9,25},{17,1},{25,9},{2,18},{10... | collective-permute-start | bytes 442376 | tf_op jit(solution)/shard_map/ppermute | solution.py:132
  42.8 41.3 %collective-permute-start.5 = (bf16[36,2048]{1,0:T(8,128)(2,1)}, bf16[36,2048]{1,0:T(8,128)(2,1)S(1)}, u32[]{:S(2)}, u32[]{:S(2)}) collective-permute-start(bf16[36,2048]{1,0:T(8,128)(2,1)} %get-tuple-element.100), channel_id=1, source_target_pairs={{0,8},{8,16},{16,24},{24,0},{1,9},{9,17},{17,25},{25,1},{2,10},{10... | collective-permute-start | bytes 442376 | tf_op jit(solution)/shard_map/ppermute | solution.py:132
  45.3 38.8 %collective-permute-start.6 = (bf16[36,2048]{1,0:T(8,128)(2,1)}, bf16[36,2048]{1,0:T(8,128)(2,1)S(1)}, u32[]{:S(2)}, u32[]{:S(2)}) collective-permute-start(bf16[36,2048]{1,0:T(8,128)(2,1)} %get-tuple-element.99), channel_id=1, source_target_pairs={{0,24},{8,0},{16,8},{24,16},{1,25},{9,1},{17,9},{25,17},{2,26},{10... | collective-permute-start | bytes 442376 | tf_op jit(solution)/shard_map/ppermute | solution.py:132
  59.0 43.6 %copy-start.2 = (bf16[144,2048]{1,0:T(8,128)(2,1)}, bf16[144,2048]{1,0:T(8,128)(2,1)S(1)}, u32[]{:S(2)}) copy-start(bf16[144,2048]{1,0:T(8,128)(2,1)S(1)} %reshape.172) | copy-start | bytes 1769476
  59.0 36.4 %collective-permute-start.3 = (bf16[144,2048]{1,0:T(8,128)(2,1)S(1)}, bf16[144,2048]{1,0:T(8,128)(2,1)S(1)}, u32[]{:S(2)}, u32[]{:S(2)}) collective-permute-start(bf16[144,2048]{1,0:T(8,128)(2,1)S(1)} %reshape.172), channel_id=1, source_target_pairs={{2,0},{4,2},{6,4},{8,6},{10,8},{12,10},{14,12},{16,14},{18,16},{20... | collective-permute-start | bytes 1769480 | tf_op jit(solution)/shard_map/ppermute | solution.py:29
  76.8 19.8 %collective-permute-start.2 = (bf16[144,2048]{1,0:T(8,128)(2,1)S(1)}, bf16[144,2048]{1,0:T(8,128)(2,1)S(1)}, u32[]{:S(2)}, u32[]{:S(2)}) collective-permute-start(bf16[144,2048]{1,0:T(8,128)(2,1)S(1)} %reshape.172), channel_id=1, source_target_pairs={{0,2},{2,4},{4,6},{6,8},{8,10},{10,12},{12,14},{14,16},{16,18},{18... | collective-permute-start | bytes 1769480 | tf_op jit(solution)/shard_map/ppermute | solution.py:25
  86.6 18.3 %collective-permute-start.12 = (bf16[144,2048]{1,0:T(8,128)(2,1)S(1)}, bf16[144,2048]{1,0:T(8,128)(2,1)S(1)}, u32[]{:S(2)}, u32[]{:S(2)}) collective-permute-start(bf16[144,2048]{1,0:T(8,128)(2,1)S(1)} %pad_maximum_fusion.4.g_ref), channel_id=1, source_target_pairs={{2,0},{4,2},{6,4},{8,6},{10,8},{12,10},{14,12},{16,14},{18,16},{20... | collective-permute-start | bytes 1769480 | tf_op jit(solution)/shard_map/ppermute | solution.py:29
  88.6 20.7 %collective-permute-start.13 = (bf16[144,2048]{1,0:T(8,128)(2,1)S(1)}, bf16[144,2048]{1,0:T(8,128)(2,1)S(1)}, u32[]{:S(2)}, u32[]{:S(2)}) collective-permute-start(bf16[144,2048]{1,0:T(8,128)(2,1)S(1)} %pad_maximum_fusion.4.g_ref), channel_id=1, source_target_pairs={{0,2},{2,4},{4,6},{6,8},{8,10},{10,12},{12,14},{14,16},{16,18},{18... | collective-permute-start | bytes 1769480 | tf_op jit(solution)/shard_map/ppermute | solution.py:25
  96.7 90.3 %copy-start.1 = (bf16[144,2048]{1,0:T(8,128)(2,1)}, bf16[144,2048]{1,0:T(8,128)(2,1)S(1)}, u32[]{:S(2)}) copy-start(bf16[144,2048]{1,0:T(8,128)(2,1)S(1)} %get-tuple-element.53) | copy-start | bytes 1769476
  96.8 20.8 %collective-permute-start.8 = (bf16[144,2048]{1,0:T(8,128)(2,1)S(1)}, bf16[144,2048]{1,0:T(8,128)(2,1)S(1)}, u32[]{:S(2)}, u32[]{:S(2)}) collective-permute-start(bf16[144,2048]{1,0:T(8,128)(2,1)S(1)} %collective-permute-done.3), channel_id=1, source_target_pairs={{2,0},{4,2},{6,4},{8,6},{10,8},{12,10},{14,12},{16,14},{18,16},{20... | collective-permute-start | bytes 1769480 | tf_op jit(solution)/shard_map/ppermute | solution.py:29
  99.3 22.7 %collective-permute-start.10 = (bf16[144,2048]{1,0:T(8,128)(2,1)S(1)}, bf16[144,2048]{1,0:T(8,128)(2,1)S(1)}, u32[]{:S(2)}, u32[]{:S(2)}) collective-permute-start(bf16[144,2048]{1,0:T(8,128)(2,1)S(1)} %collective-permute-done.2), channel_id=1, source_target_pairs={{0,2},{2,4},{4,6},{6,8},{8,10},{10,12},{12,14},{14,16},{16,18},{18... | collective-permute-start | bytes 1769480 | tf_op jit(solution)/shard_map/ppermute | solution.py:25
  104.9 25.3 %collective-permute-start.14 = (bf16[144,2048]{1,0:T(8,128)(2,1)S(1)}, bf16[144,2048]{1,0:T(8,128)(2,1)S(1)}, u32[]{:S(2)}, u32[]{:S(2)}) collective-permute-start(bf16[144,2048]{1,0:T(8,128)(2,1)S(1)} %collective-permute-done.12), channel_id=1, source_target_pairs={{2,0},{4,2},{6,4},{8,6},{10,8},{12,10},{14,12},{16,14},{18,16},{20... | collective-permute-start | bytes 1769480 | tf_op jit(solution)/shard_map/ppermute | solution.py:29
  109.3 25.1 %collective-permute-start.15 = (bf16[144,2048]{1,0:T(8,128)(2,1)S(1)}, bf16[144,2048]{1,0:T(8,128)(2,1)S(1)}, u32[]{:S(2)}, u32[]{:S(2)}) collective-permute-start(bf16[144,2048]{1,0:T(8,128)(2,1)S(1)} %collective-permute-done.13), channel_id=1, source_target_pairs={{0,2},{2,4},{4,6},{6,8},{8,10},{10,12},{12,14},{14,16},{16,18},{18... | collective-permute-start | bytes 1769480 | tf_op jit(solution)/shard_map/ppermute | solution.py:25
  122.0 65.0 %copy-start.4 = (bf16[144,2048]{1,0:T(8,128)(2,1)}, bf16[144,2048]{1,0:T(8,128)(2,1)S(1)}, u32[]{:S(2)}) copy-start(bf16[144,2048]{1,0:T(8,128)(2,1)S(1)} %broadcast_select_fusion.1) | copy-start | bytes 1769476
  122.5 17.7 %collective-permute-start.9 = (bf16[144,2048]{1,0:T(8,128)(2,1)S(1)}, bf16[144,2048]{1,0:T(8,128)(2,1)S(1)}, u32[]{:S(2)}, u32[]{:S(2)}) collective-permute-start(bf16[144,2048]{1,0:T(8,128)(2,1)S(1)} %collective-permute-done.8), channel_id=1, source_target_pairs={{2,0},{3,1},{10,8},{11,9},{18,16},{19,17},{26,24},{27,25},{34,32},... | collective-permute-start | bytes 1769480 | tf_op jit(solution)/shard_map/ppermute | solution.py:33
  125.0 15.1 %collective-permute-start.11 = (bf16[144,2048]{1,0:T(8,128)(2,1)S(1)}, bf16[144,2048]{1,0:T(8,128)(2,1)S(1)}, u32[]{:S(2)}, u32[]{:S(2)}) collective-permute-start(bf16[144,2048]{1,0:T(8,128)(2,1)S(1)} %collective-permute-done.10), channel_id=1, source_target_pairs={{4,6},{5,7},{12,14},{13,15},{20,22},{21,23},{28,30},{29,31},{36,38... | collective-permute-start | bytes 1769480 | tf_op jit(solution)/shard_map/ppermute | solution.py:33
  130.2 26.0 %collective-permute-start.18 = (bf16[144,2048]{1,0:T(8,128)(2,1)S(1)}, bf16[144,2048]{1,0:T(8,128)(2,1)S(1)}, u32[]{:S(2)}, u32[]{:S(2)}) collective-permute-start(bf16[144,2048]{1,0:T(8,128)(2,1)S(1)} %collective-permute-done.14), channel_id=1, source_target_pairs={{2,0},{3,1},{10,8},{11,9},{18,16},{19,17},{26,24},{27,25},{34,32},... | collective-permute-start | bytes 1769480 | tf_op jit(solution)/shard_map/ppermute | solution.py:33
  134.4 21.7 %collective-permute-start.19 = (bf16[144,2048]{1,0:T(8,128)(2,1)S(1)}, bf16[144,2048]{1,0:T(8,128)(2,1)S(1)}, u32[]{:S(2)}, u32[]{:S(2)}) collective-permute-start(bf16[144,2048]{1,0:T(8,128)(2,1)S(1)} %collective-permute-done.15), channel_id=1, source_target_pairs={{4,6},{5,7},{12,14},{13,15},{20,22},{21,23},{28,30},{29,31},{36,38... | collective-permute-start | bytes 1769480 | tf_op jit(solution)/shard_map/ppermute | solution.py:33
  140.2 46.8 %copy-start.5 = (bf16[144,2048]{1,0:T(8,128)(2,1)}, bf16[144,2048]{1,0:T(8,128)(2,1)S(1)}, u32[]{:S(2)}) copy-start(bf16[144,2048]{1,0:T(8,128)(2,1)S(1)} %select_select_fusion.1) | copy-start | bytes 1769476
  142.7 19.9 %collective-permute-start.17 = (bf16[160,2048]{1,0:T(8,128)(2,1)S(1)}, bf16[160,2048]{1,0:T(8,128)(2,1)S(1)}, u32[]{:S(2)}, u32[]{:S(2)}) collective-permute-start(bf16[160,2048]{1,0:T(8,128)(2,1)S(1)} %get-tuple-element.66), channel_id=1, source_target_pairs={{6,4},{4,2},{7,5},{5,3},{14,12},{12,10},{15,13},{13,11},{22,20},{2... | collective-permute-start | bytes 1966088 | tf_op jit(solution)/shard_map/ppermute | solution.py:33
  144.0 33.0 %collective-permute-start.16 = (bf16[160,2048]{1,0:T(8,128)(2,1)S(1)}, bf16[160,2048]{1,0:T(8,128)(2,1)S(1)}, u32[]{:S(2)}, u32[]{:S(2)}) collective-permute-start(bf16[160,2048]{1,0:T(8,128)(2,1)S(1)} %get-tuple-element.66), channel_id=1, source_target_pairs={{0,2},{2,4},{1,3},{3,5},{8,10},{10,12},{9,11},{11,13},{16,18},{18,... | collective-permute-start | bytes 1966088 | tf_op jit(solution)/shard_map/ppermute | solution.py:33
  158.7 38.9 %collective-permute-start.22 = (bf16[160,2048]{1,0:T(8,128)(2,1)S(1)}, bf16[160,2048]{1,0:T(8,128)(2,1)S(1)}, u32[]{:S(2)}, u32[]{:S(2)}) collective-permute-start(bf16[160,2048]{1,0:T(8,128)(2,1)S(1)} %get-tuple-element.69), channel_id=1, source_target_pairs={{0,6},{6,0},{1,7},{7,1},{8,14},{14,8},{9,15},{15,9},{16,22},{22,16... | collective-permute-start | bytes 1966088 | tf_op jit(solution)/shard_map/ppermute | solution.py:33
  177.5 20.2 %collective-permute-start.21 = (bf16[160,2048]{1,0:T(8,128)(2,1)S(1)}, bf16[160,2048]{1,0:T(8,128)(2,1)S(1)}, u32[]{:S(2)}, u32[]{:S(2)}) collective-permute-start(bf16[160,2048]{1,0:T(8,128)(2,1)S(1)} %get-tuple-element.71), channel_id=1, source_target_pairs={{6,4},{4,2},{2,0},{7,5},{5,3},{3,1},{14,12},{12,10},{10,8},{15,13}... | collective-permute-start | bytes 1966088 | tf_op jit(solution)/shard_map/ppermute | solution.py:33
  179.6 18.1 %collective-permute-start.20 = (bf16[160,2048]{1,0:T(8,128)(2,1)S(1)}, bf16[160,2048]{1,0:T(8,128)(2,1)S(1)}, u32[]{:S(2)}, u32[]{:S(2)}) collective-permute-start(bf16[160,2048]{1,0:T(8,128)(2,1)S(1)} %get-tuple-element.70), channel_id=1, source_target_pairs={{0,2},{2,4},{4,6},{1,3},{3,5},{5,7},{8,10},{10,12},{12,14},{9,11},... | collective-permute-start | bytes 1966088 | tf_op jit(solution)/shard_map/ppermute | solution.py:33
  185.1 12.6 %collective-permute-start.23 = (bf16[128,2048]{1,0:T(8,128)(2,1)S(1)}, bf16[128,2048]{1,0:T(8,128)(2,1)S(1)}, u32[]{:S(2)}, u32[]{:S(2)}) collective-permute-start(bf16[128,2048]{1,0:T(8,128)(2,1)S(1)} %convolution_convert_fusion.3), channel_id=1, source_target_pairs={{0,1},{1,0},{2,3},{3,2},{4,5},{5,4},{6,7},{7,6},{8,9},{9,8},{10,11... | collective-permute-start | bytes 1572872 | tf_op jit(solution)/shard_map/ppermute | solution.py:37
  199.0 41.3 %all-to-all-start.1 = ((bf16[4,40,2048]{2,1,0:T(8,128)(2,1)}), bf16[4,40,2048]{2,1,0:T(8,128)(2,1)}, u32[]{:S(2)}, u32[]{:S(2)}) async-start(bf16[4,40,2048]{2,1,0:T(8,128)(2,1)} %bitcast.39), calls=%async_computation.1 | async-start | bytes 1310720 | tf_op jit(solution)/shard_map/all_to_all | solution.py:193
  208.6 26.0 %collective-permute-start.24 = (bf16[2048,256]{1,0:T(8,128)(2,1)}, bf16[2048,256]{1,0:T(8,128)(2,1)S(1)}, u32[]{:S(2)}, u32[]{:S(2)}) collective-permute-start(bf16[2048,256]{1,0:T(8,128)(2,1)} %convolution_convert_fusion), channel_id=1, source_target_pairs={{0,1},{1,0},{2,3},{3,2},{4,5},{5,4},{6,7},{7,6},{8,9},{9,8},{10,11... | collective-permute-start | bytes 3145736 | tf_op jit(solution)/shard_map/ppermute | solution.py:37
  215.1 26.9 %copy-start.7 = (bf16[128,2048]{1,0:T(8,128)(2,1)S(1)}, bf16[128,2048]{1,0:T(8,128)(2,1)}, u32[]{:S(2)}) copy-start(bf16[128,2048]{1,0:T(8,128)(2,1)} %copy-done.6) | copy-start | bytes 1572868
  (10 other events, 93.4 us)

commit v7 on v5

--- a/solution.py
+++ b/solution.py
@@ -172,11 +172,11 @@
 
     add = lambda *terms: sum(a.astype(F32) for a in terms).astype(BF)
     d0, d1, d3_early, d2 = (d[3] for d in done)
-    near = line(d1, (0, 1), (3, 2))
     r2, l2 = line(d2, (0, 1), (1, 2)), line(d2, (3, 2), (2, 1))
     to_r1 = add(where(zo == 1, d3_early, d1), r2)
     to_l1 = add(where(zo == 2, d3_early, d1), l2)
-    r1, l1 = line(to_r1, (1, 2), (2, 3)), line(to_l1, (2, 1), (1, 0))
+    r1 = line(to_r1, (0, 1), (1, 2), (2, 3))
+    l1 = line(to_l1, (3, 2), (2, 1), (1, 0))
     g3 = g3(to_r1, to_l1, gu3)
     done[2] = expert(gu3, g3)
     far = line(done[2][3], (0, 3), (3, 0))
@@ -189,12 +189,13 @@
     other_down = dot(hid_all[:, hidden:], g_all, 0, 0).astype(BF)
 
     other_down = across(other_down)
-    dx = add(d0, near, r1, l1, after(far, other_gu, other_down))
+    dx = add(d0, r1, l1, after(far, other_gu, other_down))
     dx = dx.reshape(EXPERTS, pitch, width)
     far, up1, down1 = (block(dx[k], -k) for k in (2, 1, 3))
     back = jnp.concatenate([dx[0], up1, far, down1], axis=0)
     other_gu = across(other_gu)
-    grad_gu = (dot(x_all, cat(own), 0, 0) + other_gu.astype(F32)).astype(BF)
+    own_gu = lax.optimization_barrier(dot(x_all, cat(own), 0, 0))
+    grad_gu = (own_gu + other_gu.astype(F32)).astype(BF)
     grad_down = dot(hid_all[:, :hidden], g_all, 0, 0) + other_down.astype(F32)
     grad_down = grad_down.astype(BF)
     back, grad_gu, grad_down = lax.optimization_barrier((back, grad_gu, grad_down))

time: 241 us -> 237 us (0.983)
  waiting for transfers between devices: 97 us -> 93.4 us
    ppermute x1, waiting for transfers between devices: 0.01 us -> 4.33 us  [per_device(): lax.ppermute(upstream, SECTION, [(i, (i - 1) % sections) for i in range(s...]
    all_to_all x2, waiting for transfers between devices: 47.8 us -> 43.6 us  [to_blocks(): units = lax.all_to_all(dispatch(a), 'zb', 0, 0, tiled=True)]
    ppermute x4, starting transfers between devices: 17.5 us -> 14.7 us  [across(): return lax.ppermute(a, 'yh', [(0, 1), (1, 0)])]
    ppermute x3, waiting for transfers between devices: 18.2 us -> 15.6 us  [block(): lax.ppermute(a, 'zb', [(i, (i + k) % EXPERTS) for i in range(EXPERTS)])]
    ppermute x10 -> x9, starting transfers between devices: 16.6 us -> 18.2 us  [line(): return lax.ppermute(a, 'zo', pairs)]
    ppermute x10 -> x9, waiting for transfers between devices: 6.94 us -> 6.07 us  [line(): return lax.ppermute(a, 'zo', pairs)]
  transfers between devices with their start and end apart: 28 -> 27, of which waited for: 12 -> 12; matrix products, arithmetic and copies ran while one was open for 9% -> 10% of each run, Pallas kernels for 4% -> 4%
where the time goes in v7:
time: 237 us; the launch traced here: 234 us
  starting transfers between devices  100 us (42%)
  waiting for transfers between devices  93.4 us (39%)
  matrix products  12.5 us (5%)
  local copies, waits for them, and re-layouts  9.72 us (4%)
  Pallas kernels  9.48 us (4%)
  other arithmetic  7.11 us (3%)
    all_to_all x2, waiting for transfers between devices, to_blocks(): units = lax.all_to_all(dispatch(a), 'zb', 0, 0, tiled=True)  43.6 us
    ppermute x3, starting transfers between devices, block(): lax.ppermute(a, 'zb', [(i, (i + k) % EXPERTS) for i in range(EXPERTS)])  21 us
    all_to_all x2, starting transfers between devices, to_blocks(): units = lax.all_to_all(dispatch(a), 'zb', 0, 0, tiled=True)  18.6 us
    ppermute x9, starting transfers between devices, line(): return lax.ppermute(a, 'zo', pairs)  18.2 us
    ppermute x4, waiting for transfers between devices, down(): lax.ppermute(a, ('zb', 'zo'), [((i + 1) % RING, i) for i in range(RING)])  16.7 us
    ppermute x3, waiting for transfers between devices, block(): lax.ppermute(a, 'zb', [(i, (i + k) % EXPERTS) for i in range(EXPERTS)])  15.6 us
    ppermute x4, starting transfers between devices, across(): return lax.ppermute(a, 'yh', [(0, 1), (1, 0)])  14.7 us
    ppermute x4, starting transfers between devices, down(): lax.ppermute(a, ('zb', 'zo'), [((i + 1) % RING, i) for i in range(RING)])  13.7 us
  transfers between devices with their start and end apart: 27, of which 12 were waited for; matrix products, arithmetic and copies ran while one was open for 10% of the time, Pallas kernels for 4%

profile of v7, /device:TPU:6, one launch (start us, length us, event | category | flops | bytes accessed | tf_op | source)
XLA Modules:
  0.0 233.9 jit_solution(10209085445071421838)
XLA Ops:
  3.6 15.1 %all-to-all-start = ((bf16[4,36,2048]{2,1,0:T(8,128)(2,1)}), bf16[4,36,2048]{2,1,0:T(8,128)(2,1)S(1)}, u32[]{:S(2)}, u32[]{:S(2)}) async-start(bf16[4,36,2048]{2,1,0:T(8,128)(2,1)} %reshape.163), calls=%async_computation | async-start | bytes 1310720 | tf_op jit(solution)/shard_map/all_to_all | solution.py:152
  18.6 5.1 %collective-permute-start.1 = (bf16[2048,256]{1,0:T(8,128)(2,1)}, bf16[2048,256]{1,0:T(8,128)(2,1)}, u32[]{:S(2)}, u32[]{:S(2)}) collective-permute-start(bf16[2048,256]{1,0:T(8,128)(2,1)} %bitcast.3), channel_id=1, source_target_pairs={{0,1},{1,0},{2,3},{3,2},{4,5},{5,4},{6,7},{7,6},{8,9},{9,8},{10,11... | collective-permute-start | bytes 3145736 | tf_op jit(solution)/shard_map/ppermute | solution.py:37
  25.7 2.2 collective-permute-start.4
  28.0 4.3 %collective-permute-done = bf16[128,2048]{1,0:T(8,128)(2,1)S(1)} collective-permute-done((bf16[128,2048]{1,0:T(8,128)(2,1)S(1)}, bf16[128,2048]{1,0:T(8,128)(2,1)S(1)}, u32[]{:S(2)}, u32[]{:S(2)}) %collective-permute-start) | collective-permute-done | bytes 524320 | tf_op jit(solution)/shard_map/ppermute | solution.py:112
  33.7 22.8 %all-to-all-done = bf16[4,36,2048]{2,1,0:T(8,128)(2,1)S(1)} async-done(((bf16[4,36,2048]{2,1,0:T(8,128)(2,1)}), bf16[4,36,2048]{2,1,0:T(8,128)(2,1)S(1)}, u32[]{:S(2)}, u32[]{:S(2)}) %all-to-all-start) | async-done | bytes 589856 | tf_op jit(solution)/shard_map/all_to_all | solution.py:152
  56.5 3.5 %all-to-all-start.1 = ((bf16[4,36,2048]{2,1,0:T(8,128)(2,1)}), bf16[4,36,2048]{2,1,0:T(8,128)(2,1)S(1)}, u32[]{:S(2)}, u32[]{:S(2)}) async-start(bf16[4,36,2048]{2,1,0:T(8,128)(2,1)} %reshape.165), calls=%async_computation.1 | async-start | bytes 1310720 | tf_op jit(solution)/shard_map/all_to_all | solution.py:152
  60.1 2.2 fusion.40
  63.9 6.6 %collective-permute-start.3 = (bf16[144,2048]{1,0:T(8,128)(2,1)}, bf16[144,2048]{1,0:T(8,128)(2,1)}, u32[]{:S(2)}, u32[]{:S(2)}) collective-permute-start(bf16[144,2048]{1,0:T(8,128)(2,1)} %reshape.164), channel_id=1, source_target_pairs={{2,0},{4,2},{6,4},{8,6},{10,8},{12,10},{14,12},{16,14},{18,16},{20... | collective-permute-start | bytes 1769480 | tf_op jit(solution)/shard_map/ppermute | solution.py:29
  70.5 1.9 collective-permute-start.2
  73.9 20.8 %all-to-all-done.1 = bf16[4,36,2048]{2,1,0:T(8,128)(2,1)S(1)} async-done(((bf16[4,36,2048]{2,1,0:T(8,128)(2,1)}), bf16[4,36,2048]{2,1,0:T(8,128)(2,1)S(1)}, u32[]{:S(2)}, u32[]{:S(2)}) %all-to-all-start.1) | async-done | bytes 589856 | tf_op jit(solution)/shard_map/all_to_all | solution.py:152
  99.3 3.9 %collective-permute-start.10 = (bf16[144,2048]{1,0:T(8,128)(2,1)S(1)}, bf16[144,2048]{1,0:T(8,128)(2,1)S(1)}, u32[]{:S(2)}, u32[]{:S(2)}) collective-permute-start(bf16[144,2048]{1,0:T(8,128)(2,1)S(1)} %reshape.166.g_ref), channel_id=1, source_target_pairs={{0,2},{2,4},{4,6},{6,8},{8,10},{10,12},{12,14},{14,16},{16,18},{18... | collective-permute-start | bytes 1769480 | tf_op jit(solution)/shard_map/ppermute | solution.py:25
  105.9 3.1 %collective-permute-start.5 = (bf16[144,2048]{1,0:T(8,128)(2,1)}, bf16[144,2048]{1,0:T(8,128)(2,1)S(1)}, u32[]{:S(2)}, u32[]{:S(2)}) collective-permute-start(bf16[144,2048]{1,0:T(8,128)(2,1)} %collective-permute-done.3), channel_id=1, source_target_pairs={{2,0},{4,2},{6,4},{8,6},{10,8},{12,10},{14,12},{16,14},{18,16},{20... | collective-permute-start | bytes 1769480 | tf_op jit(solution)/shard_map/ppermute | solution.py:29
  109.0 2.7 %collective-permute-start.7 = (bf16[144,2048]{1,0:T(8,128)(2,1)}, bf16[144,2048]{1,0:T(8,128)(2,1)S(1)}, u32[]{:S(2)}, u32[]{:S(2)}) collective-permute-start(bf16[144,2048]{1,0:T(8,128)(2,1)} %collective-permute-done.2), channel_id=1, source_target_pairs={{0,2},{2,4},{4,6},{6,8},{8,10},{10,12},{12,14},{14,16},{16,18},{18... | collective-permute-start | bytes 1769480 | tf_op jit(solution)/shard_map/ppermute | solution.py:25
  113.3 2.2 collective-permute-done.9
  115.5 2.1 collective-permute-start.11
  117.7 3.7 %collective-permute-start.12 = (bf16[144,2048]{1,0:T(8,128)(2,1)S(1)}, bf16[144,2048]{1,0:T(8,128)(2,1)S(1)}, u32[]{:S(2)}, u32[]{:S(2)}) collective-permute-start(bf16[144,2048]{1,0:T(8,128)(2,1)S(1)} %collective-permute-done.10), channel_id=1, source_target_pairs={{0,2},{2,4},{4,6},{6,8},{8,10},{10,12},{12,14},{14,16},{16,18},{18... | collective-permute-start | bytes 1769480 | tf_op jit(solution)/shard_map/ppermute | solution.py:25
  121.5 6.7 %collective-permute-done.5 = bf16[144,2048]{1,0:T(8,128)(2,1)S(1)} collective-permute-done((bf16[144,2048]{1,0:T(8,128)(2,1)}, bf16[144,2048]{1,0:T(8,128)(2,1)S(1)}, u32[]{:S(2)}, u32[]{:S(2)}) %collective-permute-start.5) | collective-permute-done | bytes 589856 | tf_op jit(solution)/shard_map/ppermute | solution.py:29
  133.0 7.8 %collective-permute-done.11 = bf16[144,2048]{1,0:T(8,128)(2,1)S(1)} collective-permute-done((bf16[144,2048]{1,0:T(8,128)(2,1)S(1)}, bf16[144,2048]{1,0:T(8,128)(2,1)S(1)}, u32[]{:S(2)}, u32[]{:S(2)}) %collective-permute-start.11) | collective-permute-done | bytes 589856 | tf_op jit(solution)/shard_map/ppermute | solution.py:29
  143.5 2.1 collective-permute-start.13
  146.9 6.1 %collective-permute-done.6 = bf16[144,2048]{1,0:T(8,128)(2,1)S(1)} collective-permute-done((bf16[144,2048]{1,0:T(8,128)(2,1)S(1)}, bf16[144,2048]{1,0:T(8,128)(2,1)S(1)}, u32[]{:S(2)}, u32[]{:S(2)}) %collective-permute-start.6) | collective-permute-done | bytes 589856 | tf_op jit(solution)/shard_map/ppermute | solution.py:33
  162.0 4.6 %collective-permute-start.14 = (bf16[160,2048]{1,0:T(8,128)(2,1)S(1)}, bf16[160,2048]{1,0:T(8,128)(2,1)S(1)}, u32[]{:S(2)}, u32[]{:S(2)}) collective-permute-start(bf16[160,2048]{1,0:T(8,128)(2,1)S(1)} %get-tuple-element.81), channel_id=1, source_target_pairs={{0,2},{2,4},{4,6},{1,3},{3,5},{5,7},{8,10},{10,12},{12,14},{9,11},... | collective-permute-start | bytes 1966088 | tf_op jit(solution)/shard_map/ppermute | solution.py:33
  168.6 5.4 %collective-permute-start.19 = (bf16[160,2048]{1,0:T(8,128)(2,1)S(1)}, bf16[160,2048]{1,0:T(8,128)(2,1)S(1)}, u32[]{:S(2)}, u32[]{:S(2)}) collective-permute-start(bf16[160,2048]{1,0:T(8,128)(2,1)S(1)} %get-tuple-element.61), channel_id=1, source_target_pairs={{0,6},{6,0},{1,7},{7,1},{8,14},{14,8},{9,15},{15,9},{16,22},{22,16... | collective-permute-start | bytes 1966088 | tf_op jit(solution)/shard_map/ppermute | solution.py:33
  174.6 5.1 %collective-permute-start.20 = (bf16[128,2048]{1,0:T(8,128)(2,1)S(1)}, bf16[128,2048]{1,0:T(8,128)(2,1)S(1)}, u32[]{:S(2)}, u32[]{:S(2)}) collective-permute-start(bf16[128,2048]{1,0:T(8,128)(2,1)S(1)} %convolution_convert_fusion.3), channel_id=1, source_target_pairs={{0,1},{1,0},{2,3},{3,2},{4,5},{5,4},{6,7},{7,6},{8,9},{9,8},{10,11... | collective-permute-start | bytes 1572872 | tf_op jit(solution)/shard_map/ppermute | solution.py:37
  179.6 2.1 fusion.6
  181.8 2.1 convolution_convert_fusion
  183.9 2.3 collective-permute-start.24
  186.2 5.8 %collective-permute-done.20 = bf16[128,2048]{1,0:T(8,128)(2,1)S(1)} collective-permute-done((bf16[128,2048]{1,0:T(8,128)(2,1)S(1)}, bf16[128,2048]{1,0:T(8,128)(2,1)S(1)}, u32[]{:S(2)}, u32[]{:S(2)}) %collective-permute-start.20) | collective-permute-done | bytes 524320 | tf_op jit(solution)/shard_map/ppermute | solution.py:37
  192.5 10.5 %collective-permute-start.23 = (bf16[40,2048]{1,0:T(8,128)(2,1)S(1)}, bf16[40,2048]{1,0:T(8,128)(2,1)S(1)}, u32[]{:S(2)}, u32[]{:S(2)}) collective-permute-start(bf16[40,2048]{1,0:T(8,128)(2,1)S(1)} %get-tuple-element.91), channel_id=1, source_target_pairs={{0,8},{8,16},{16,24},{24,0},{1,9},{9,17},{17,25},{25,1},{2,10},{10... | collective-permute-start | bytes 491528 | tf_op jit(solution)/shard_map/ppermute | solution.py:133
  203.0 4.7 %collective-permute-start.22 = (bf16[40,2048]{1,0:T(8,128)(2,1)S(1)}, bf16[40,2048]{1,0:T(8,128)(2,1)S(1)}, u32[]{:S(2)}, u32[]{:S(2)}) collective-permute-start(bf16[40,2048]{1,0:T(8,128)(2,1)S(1)} %get-tuple-element.92), channel_id=1, source_target_pairs={{0,16},{8,24},{16,0},{24,8},{1,17},{9,25},{17,1},{25,9},{2,18},{10... | collective-permute-start | bytes 491528 | tf_op jit(solution)/shard_map/ppermute | solution.py:133
  207.7 5.9 %collective-permute-start.21 = (bf16[40,2048]{1,0:T(8,128)(2,1)S(1)}, bf16[40,2048]{1,0:T(8,128)(2,1)S(1)}, u32[]{:S(2)}, u32[]{:S(2)}) collective-permute-start(bf16[40,2048]{1,0:T(8,128)(2,1)S(1)} %get-tuple-element.93), channel_id=1, source_target_pairs={{0,24},{8,0},{16,8},{24,16},{1,25},{9,1},{17,9},{25,17},{2,26},{10... | collective-permute-start | bytes 491528 | tf_op jit(solution)/shard_map/ppermute | solution.py:133
  214.9 3.3 %collective-permute-done.23 = bf16[40,2048]{1,0:T(8,128)(2,1)S(1)} collective-permute-done((bf16[40,2048]{1,0:T(8,128)(2,1)S(1)}, bf16[40,2048]{1,0:T(8,128)(2,1)S(1)}, u32[]{:S(2)}, u32[]{:S(2)}) %collective-permute-start.23) | collective-permute-done | bytes 163872 | tf_op jit(solution)/shard_map/ppermute | solution.py:133
  218.2 12.1 %collective-permute-done.22 = bf16[40,2048]{1,0:T(8,128)(2,1)S(1)} collective-permute-done((bf16[40,2048]{1,0:T(8,128)(2,1)S(1)}, bf16[40,2048]{1,0:T(8,128)(2,1)S(1)}, u32[]{:S(2)}, u32[]{:S(2)}) %collective-permute-start.22) | collective-permute-done | bytes 163872 | tf_op jit(solution)/shard_map/ppermute | solution.py:133
  (93 shorter events, 43.9 us)
Async XLA Ops:
  0.6 27.4 %copy-start.5 = (s32[128,1]{0,1:T(1,128)S(1)}, s32[128,1]{0,1:T(1,128)}, u32[]{:S(2)}) copy-start(s32[128,1]{0,1:T(1,128)} %param.8) | copy-start | bytes 1540
  0.7 23.1 %copy-start.6 = (bf16[128,2048]{1,0:T(8,128)(2,1)S(1)}, bf16[128,2048]{1,0:T(8,128)(2,1)}, u32[]{:S(2)}) copy-start(bf16[128,2048]{1,0:T(8,128)(2,1)} %param.7) | copy-start | bytes 1572868
  0.7 27.3 %copy-start.7 = (bf16[128,1]{0,1:T(2,128)(2,1)S(1)}, bf16[128,1]{0,1:T(2,128)(2,1)}, u32[]{:S(2)}) copy-start(bf16[128,1]{0,1:T(2,128)(2,1)} %param.9) | copy-start | bytes 772
  3.6 52.9 %all-to-all-start = ((bf16[4,36,2048]{2,1,0:T(8,128)(2,1)}), bf16[4,36,2048]{2,1,0:T(8,128)(2,1)S(1)}, u32[]{:S(2)}, u32[]{:S(2)}) async-start(bf16[4,36,2048]{2,1,0:T(8,128)(2,1)} %reshape.163), calls=%async_computation | async-start | bytes 1310720 | tf_op jit(solution)/shard_map/all_to_all | solution.py:152
  18.6 45.3 %collective-permute-start.1 = (bf16[2048,256]{1,0:T(8,128)(2,1)}, bf16[2048,256]{1,0:T(8,128)(2,1)}, u32[]{:S(2)}, u32[]{:S(2)}) collective-permute-start(bf16[2048,256]{1,0:T(8,128)(2,1)} %bitcast.3), channel_id=1, source_target_pairs={{0,1},{1,0},{2,3},{3,2},{4,5},{5,4},{6,7},{7,6},{8,9},{9,8},{10,11... | collective-permute-start | bytes 3145736 | tf_op jit(solution)/shard_map/ppermute | solution.py:37
  23.8 8.6 %collective-permute-start = (bf16[128,2048]{1,0:T(8,128)(2,1)S(1)}, bf16[128,2048]{1,0:T(8,128)(2,1)S(1)}, u32[]{:S(2)}, u32[]{:S(2)}) collective-permute-start(bf16[128,2048]{1,0:T(8,128)(2,1)S(1)} %copy-done.6), channel_id=1, source_target_pairs={{0,480},{32,0},{64,32},{96,64},{128,96},{160,128},{192,160},{224,1... | collective-permute-start | bytes 1572872 | tf_op jit(solution)/shard_map/ppermute | solution.py:112
  25.7 71.7 %collective-permute-start.4 = (bf16[128,2048]{1,0:T(8,128)(2,1)}, bf16[128,2048]{1,0:T(8,128)(2,1)}, u32[]{:S(2)}, u32[]{:S(2)}) collective-permute-start(bf16[128,2048]{1,0:T(8,128)(2,1)} %bitcast.5), channel_id=1, source_target_pairs={{0,1},{1,0},{2,3},{3,2},{4,5},{5,4},{6,7},{7,6},{8,9},{9,8},{10,11... | collective-permute-start | bytes 1572872 | tf_op jit(solution)/shard_map/ppermute | solution.py:37
  32.4 27.8 %copy-start.1 = (bf16[128,2048]{1,0:T(8,128)(2,1)}, bf16[128,2048]{1,0:T(8,128)(2,1)S(1)}, u32[]{:S(2)}) copy-start(bf16[128,2048]{1,0:T(8,128)(2,1)S(1)} %collective-permute-done) | copy-start | bytes 1572868
  56.5 38.2 %all-to-all-start.1 = ((bf16[4,36,2048]{2,1,0:T(8,128)(2,1)}), bf16[4,36,2048]{2,1,0:T(8,128)(2,1)S(1)}, u32[]{:S(2)}, u32[]{:S(2)}) async-start(bf16[4,36,2048]{2,1,0:T(8,128)(2,1)} %reshape.165), calls=%async_computation.1 | async-start | bytes 1310720 | tf_op jit(solution)/shard_map/all_to_all | solution.py:152
  63.9 9.8 %copy-start.4 = (bf16[2048,128]{1,0:T(8,128)(2,1)S(1)}, bf16[2048,128]{1,0:T(8,128)(2,1)}, u32[]{:S(2)}) copy-start(bf16[2048,128]{1,0:T(8,128)(2,1)} %get-tuple-element.87) | copy-start | bytes 1572868
  63.9 40.6 %collective-permute-start.3 = (bf16[144,2048]{1,0:T(8,128)(2,1)}, bf16[144,2048]{1,0:T(8,128)(2,1)}, u32[]{:S(2)}, u32[]{:S(2)}) collective-permute-start(bf16[144,2048]{1,0:T(8,128)(2,1)} %reshape.164), channel_id=1, source_target_pairs={{2,0},{4,2},{6,4},{8,6},{10,8},{12,10},{14,12},{16,14},{18,16},{20... | collective-permute-start | bytes 1769480 | tf_op jit(solution)/shard_map/ppermute | solution.py:29
  70.5 34.1 %collective-permute-start.2 = (bf16[144,2048]{1,0:T(8,128)(2,1)}, bf16[144,2048]{1,0:T(8,128)(2,1)}, u32[]{:S(2)}, u32[]{:S(2)}) collective-permute-start(bf16[144,2048]{1,0:T(8,128)(2,1)} %reshape.164), channel_id=1, source_target_pairs={{0,2},{2,4},{4,6},{6,8},{8,10},{10,12},{12,14},{14,16},{16,18},{18... | collective-permute-start | bytes 1769480 | tf_op jit(solution)/shard_map/ppermute | solution.py:25
  97.4 18.2 %collective-permute-start.9 = (bf16[144,2048]{1,0:T(8,128)(2,1)S(1)}, bf16[144,2048]{1,0:T(8,128)(2,1)S(1)}, u32[]{:S(2)}, u32[]{:S(2)}) collective-permute-start(bf16[144,2048]{1,0:T(8,128)(2,1)S(1)} %reshape.166.g_ref), channel_id=1, source_target_pairs={{2,0},{4,2},{6,4},{8,6},{10,8},{12,10},{14,12},{16,14},{18,16},{20... | collective-permute-start | bytes 1769480 | tf_op jit(solution)/shard_map/ppermute | solution.py:29
  99.3 18.4 %collective-permute-start.10 = (bf16[144,2048]{1,0:T(8,128)(2,1)S(1)}, bf16[144,2048]{1,0:T(8,128)(2,1)S(1)}, u32[]{:S(2)}, u32[]{:S(2)}) collective-permute-start(bf16[144,2048]{1,0:T(8,128)(2,1)S(1)} %reshape.166.g_ref), channel_id=1, source_target_pairs={{0,2},{2,4},{4,6},{6,8},{8,10},{10,12},{12,14},{14,16},{16,18},{18... | collective-permute-start | bytes 1769480 | tf_op jit(solution)/shard_map/ppermute | solution.py:25
  105.9 22.3 %collective-permute-start.5 = (bf16[144,2048]{1,0:T(8,128)(2,1)}, bf16[144,2048]{1,0:T(8,128)(2,1)S(1)}, u32[]{:S(2)}, u32[]{:S(2)}) collective-permute-start(bf16[144,2048]{1,0:T(8,128)(2,1)} %collective-permute-done.3), channel_id=1, source_target_pairs={{2,0},{4,2},{6,4},{8,6},{10,8},{12,10},{14,12},{16,14},{18,16},{20... | collective-permute-start | bytes 1769480 | tf_op jit(solution)/shard_map/ppermute | solution.py:29
  109.0 20.5 %collective-permute-start.7 = (bf16[144,2048]{1,0:T(8,128)(2,1)}, bf16[144,2048]{1,0:T(8,128)(2,1)S(1)}, u32[]{:S(2)}, u32[]{:S(2)}) collective-permute-start(bf16[144,2048]{1,0:T(8,128)(2,1)} %collective-permute-done.2), channel_id=1, source_target_pairs={{0,2},{2,4},{4,6},{6,8},{8,10},{10,12},{12,14},{14,16},{16,18},{18... | collective-permute-start | bytes 1769480 | tf_op jit(solution)/shard_map/ppermute | solution.py:25
  115.5 25.3 %collective-permute-start.11 = (bf16[144,2048]{1,0:T(8,128)(2,1)S(1)}, bf16[144,2048]{1,0:T(8,128)(2,1)S(1)}, u32[]{:S(2)}, u32[]{:S(2)}) collective-permute-start(bf16[144,2048]{1,0:T(8,128)(2,1)S(1)} %collective-permute-done.9), channel_id=1, source_target_pairs={{2,0},{4,2},{6,4},{8,6},{10,8},{12,10},{14,12},{16,14},{18,16},{20... | collective-permute-start | bytes 1769480 | tf_op jit(solution)/shard_map/ppermute | solution.py:29
  117.7 23.2 %collective-permute-start.12 = (bf16[144,2048]{1,0:T(8,128)(2,1)S(1)}, bf16[144,2048]{1,0:T(8,128)(2,1)S(1)}, u32[]{:S(2)}, u32[]{:S(2)}) collective-permute-start(bf16[144,2048]{1,0:T(8,128)(2,1)S(1)} %collective-permute-done.10), channel_id=1, source_target_pairs={{0,2},{2,4},{4,6},{6,8},{8,10},{10,12},{12,14},{14,16},{16,18},{18... | collective-permute-start | bytes 1769480 | tf_op jit(solution)/shard_map/ppermute | solution.py:25
  130.1 22.9 %collective-permute-start.6 = (bf16[144,2048]{1,0:T(8,128)(2,1)S(1)}, bf16[144,2048]{1,0:T(8,128)(2,1)S(1)}, u32[]{:S(2)}, u32[]{:S(2)}) collective-permute-start(bf16[144,2048]{1,0:T(8,128)(2,1)S(1)} %collective-permute-done.5), channel_id=1, source_target_pairs={{2,0},{3,1},{10,8},{11,9},{18,16},{19,17},{26,24},{27,25},{34,32},... | collective-permute-start | bytes 1769480 | tf_op jit(solution)/shard_map/ppermute | solution.py:33
  131.4 22.3 %collective-permute-start.8 = (bf16[144,2048]{1,0:T(8,128)(2,1)S(1)}, bf16[144,2048]{1,0:T(8,128)(2,1)S(1)}, u32[]{:S(2)}, u32[]{:S(2)}) collective-permute-start(bf16[144,2048]{1,0:T(8,128)(2,1)S(1)} %collective-permute-done.7), channel_id=1, source_target_pairs={{4,6},{5,7},{12,14},{13,15},{20,22},{21,23},{28,30},{29,31},{36,38... | collective-permute-start | bytes 1769480 | tf_op jit(solution)/shard_map/ppermute | solution.py:33
  142.8 17.2 %collective-permute-start.15 = (bf16[160,2048]{1,0:T(8,128)(2,1)S(1)}, bf16[160,2048]{1,0:T(8,128)(2,1)S(1)}, u32[]{:S(2)}, u32[]{:S(2)}) collective-permute-start(bf16[160,2048]{1,0:T(8,128)(2,1)S(1)} %get-tuple-element.58), channel_id=1, source_target_pairs={{6,4},{4,2},{7,5},{5,3},{14,12},{12,10},{15,13},{13,11},{22,20},{2... | collective-permute-start | bytes 1966088 | tf_op jit(solution)/shard_map/ppermute | solution.py:33
  143.5 16.5 %collective-permute-start.13 = (bf16[160,2048]{1,0:T(8,128)(2,1)S(1)}, bf16[160,2048]{1,0:T(8,128)(2,1)S(1)}, u32[]{:S(2)}, u32[]{:S(2)}) collective-permute-start(bf16[160,2048]{1,0:T(8,128)(2,1)S(1)} %get-tuple-element.58), channel_id=1, source_target_pairs={{0,2},{2,4},{1,3},{3,5},{8,10},{10,12},{9,11},{11,13},{16,18},{18,... | collective-permute-start | bytes 1966088 | tf_op jit(solution)/shard_map/ppermute | solution.py:33
  145.6 21.0 %collective-permute-start.17 = (bf16[144,2048]{1,0:T(8,128)(2,1)S(1)}, bf16[144,2048]{1,0:T(8,128)(2,1)S(1)}, u32[]{:S(2)}, u32[]{:S(2)}) collective-permute-start(bf16[144,2048]{1,0:T(8,128)(2,1)S(1)} %collective-permute-done.11), channel_id=1, source_target_pairs={{2,0},{3,1},{10,8},{11,9},{18,16},{19,17},{26,24},{27,25},{34,32},... | collective-permute-start | bytes 1769480 | tf_op jit(solution)/shard_map/ppermute | solution.py:33
  152.9 13.6 %collective-permute-start.18 = (bf16[144,2048]{1,0:T(8,128)(2,1)S(1)}, bf16[144,2048]{1,0:T(8,128)(2,1)S(1)}, u32[]{:S(2)}, u32[]{:S(2)}) collective-permute-start(bf16[144,2048]{1,0:T(8,128)(2,1)S(1)} %collective-permute-done.12), channel_id=1, source_target_pairs={{4,6},{5,7},{12,14},{13,15},{20,22},{21,23},{28,30},{29,31},{36,38... | collective-permute-start | bytes 1769480 | tf_op jit(solution)/shard_map/ppermute | solution.py:33
  160.5 31.5 %collective-permute-start.16 = (bf16[160,2048]{1,0:T(8,128)(2,1)S(1)}, bf16[160,2048]{1,0:T(8,128)(2,1)S(1)}, u32[]{:S(2)}, u32[]{:S(2)}) collective-permute-start(bf16[160,2048]{1,0:T(8,128)(2,1)S(1)} %get-tuple-element.80), channel_id=1, source_target_pairs={{6,4},{4,2},{2,0},{7,5},{5,3},{3,1},{14,12},{12,10},{10,8},{15,13}... | collective-permute-start | bytes 1966088 | tf_op jit(solution)/shard_map/ppermute | solution.py:33
  162.0 30.0 %collective-permute-start.14 = (bf16[160,2048]{1,0:T(8,128)(2,1)S(1)}, bf16[160,2048]{1,0:T(8,128)(2,1)S(1)}, u32[]{:S(2)}, u32[]{:S(2)}) collective-permute-start(bf16[160,2048]{1,0:T(8,128)(2,1)S(1)} %get-tuple-element.81), channel_id=1, source_target_pairs={{0,2},{2,4},{4,6},{1,3},{3,5},{5,7},{8,10},{10,12},{12,14},{9,11},... | collective-permute-start | bytes 1966088 | tf_op jit(solution)/shard_map/ppermute | solution.py:33
  168.6 23.4 %collective-permute-start.19 = (bf16[160,2048]{1,0:T(8,128)(2,1)S(1)}, bf16[160,2048]{1,0:T(8,128)(2,1)S(1)}, u32[]{:S(2)}, u32[]{:S(2)}) collective-permute-start(bf16[160,2048]{1,0:T(8,128)(2,1)S(1)} %get-tuple-element.61), channel_id=1, source_target_pairs={{0,6},{6,0},{1,7},{7,1},{8,14},{14,8},{9,15},{15,9},{16,22},{22,16... | collective-permute-start | bytes 1966088 | tf_op jit(solution)/shard_map/ppermute | solution.py:33
  174.6 17.4 %collective-permute-start.20 = (bf16[128,2048]{1,0:T(8,128)(2,1)S(1)}, bf16[128,2048]{1,0:T(8,128)(2,1)S(1)}, u32[]{:S(2)}, u32[]{:S(2)}) collective-permute-start(bf16[128,2048]{1,0:T(8,128)(2,1)S(1)} %convolution_convert_fusion.3), channel_id=1, source_target_pairs={{0,1},{1,0},{2,3},{3,2},{4,5},{5,4},{6,7},{7,6},{8,9},{9,8},{10,11... | collective-permute-start | bytes 1572872 | tf_op jit(solution)/shard_map/ppermute | solution.py:37
  183.9 46.7 %collective-permute-start.24 = (bf16[2048,256]{1,0:T(8,128)(2,1)S(1)}, bf16[2048,256]{1,0:T(8,128)(2,1)S(1)}, u32[]{:S(2)}, u32[]{:S(2)}) collective-permute-start(bf16[2048,256]{1,0:T(8,128)(2,1)S(1)} %convolution_convert_fusion), channel_id=1, source_target_pairs={{0,1},{1,0},{2,3},{3,2},{4,5},{5,4},{6,7},{7,6},{8,9},{9,8},{10,11... | collective-permute-start | bytes 3145736 | tf_op jit(solution)/shard_map/ppermute | solution.py:37
  192.5 25.7 %collective-permute-start.23 = (bf16[40,2048]{1,0:T(8,128)(2,1)S(1)}, bf16[40,2048]{1,0:T(8,128)(2,1)S(1)}, u32[]{:S(2)}, u32[]{:S(2)}) collective-permute-start(bf16[40,2048]{1,0:T(8,128)(2,1)S(1)} %get-tuple-element.91), channel_id=1, source_target_pairs={{0,8},{8,16},{16,24},{24,0},{1,9},{9,17},{17,25},{25,1},{2,10},{10... | collective-permute-start | bytes 491528 | tf_op jit(solution)/shard_map/ppermute | solution.py:133
  203.0 27.3 %collective-permute-start.22 = (bf16[40,2048]{1,0:T(8,128)(2,1)S(1)}, bf16[40,2048]{1,0:T(8,128)(2,1)S(1)}, u32[]{:S(2)}, u32[]{:S(2)}) collective-permute-start(bf16[40,2048]{1,0:T(8,128)(2,1)S(1)} %get-tuple-element.92), channel_id=1, source_target_pairs={{0,16},{8,24},{16,0},{24,8},{1,17},{9,25},{17,1},{25,9},{2,18},{10... | collective-permute-start | bytes 491528 | tf_op jit(solution)/shard_map/ppermute | solution.py:133
  207.7 22.9 %collective-permute-start.21 = (bf16[40,2048]{1,0:T(8,128)(2,1)S(1)}, bf16[40,2048]{1,0:T(8,128)(2,1)S(1)}, u32[]{:S(2)}, u32[]{:S(2)}) collective-permute-start(bf16[40,2048]{1,0:T(8,128)(2,1)S(1)} %get-tuple-element.93), channel_id=1, source_target_pairs={{0,24},{8,0},{16,8},{24,16},{1,25},{9,1},{17,9},{25,17},{2,26},{10... | collective-permute-start | bytes 491528 | tf_op jit(solution)/shard_map/ppermute | solution.py:133
  (3 other events, 13.6 us)

commit v8 on v7

--- a/solution.py
+++ b/solution.py
@@ -168,10 +168,10 @@
     gus.append(forward(after(xs[3], gs[1])))
     gu3 = forward(x3)
     early = (x3, x3, x3, gs[3])
-    done = [expert(gu, after(g, e)) for gu, g, e in zip(gus, gs, early)]
+    done = [None] + [expert(*a) for a in zip(gus[1:], map(after, gs[1:], early[1:]))]
 
     add = lambda *terms: sum(a.astype(F32) for a in terms).astype(BF)
-    d0, d1, d3_early, d2 = (d[3] for d in done)
+    d1, d3_early, d2 = (d[3] for d in done[1:])
     r2, l2 = line(d2, (0, 1), (1, 2)), line(d2, (3, 2), (2, 1))
     to_r1 = add(where(zo == 1, d3_early, d1), r2)
     to_l1 = add(where(zo == 2, d3_early, d1), l2)
@@ -180,6 +180,8 @@
     g3 = g3(to_r1, to_l1, gu3)
     done[2] = expert(gu3, g3)
     far = line(done[2][3], (0, 3), (3, 0))
+    done[0] = expert(gus[0], after(gs[0], to_r1, to_l1))
+    d0 = done[0][3]
     own, other, hids, _ = zip(*(done[k] for k in (0, 1, 3, 2)))
 
     cat = lambda arrays: jnp.concatenate(arrays, axis=0)
@@ -188,13 +190,12 @@
     other_gu = dot(x_all, cat(other), 0, 0).astype(BF)
     other_down = dot(hid_all[:, hidden:], g_all, 0, 0).astype(BF)
 
-    other_down = across(other_down)
     dx = add(d0, r1, l1, after(far, other_gu, other_down))
     dx = dx.reshape(EXPERTS, pitch, width)
     far, up1, down1 = (block(dx[k], -k) for k in (2, 1, 3))
     back = jnp.concatenate([dx[0], up1, far, down1], axis=0)
-    other_gu = across(other_gu)
-    own_gu = lax.optimization_barrier(dot(x_all, cat(own), 0, 0))
+    other_gu, other_down = across(other_gu), across(other_down)
+    own_gu = lax.optimization_barrier(dot(after(x_all, dx), cat(own), 0, 0))
     grad_gu = (own_gu + other_gu.astype(F32)).astype(BF)
     grad_down = dot(hid_all[:, :hidden], g_all, 0, 0) + other_down.astype(F32)
     grad_down = grad_down.astype(BF)

time: 237 us -> 235 us (level)
  starting transfers between devices: 100 us -> 112 us
  waiting for transfers between devices: 93.4 us -> 82 us
    ppermute x3, waiting for transfers between devices: 15.6 us -> 3.63 us  [block(): lax.ppermute(a, 'zb', [(i, (i + k) % EXPERTS) for i in range(EXPERTS)])]
    ppermute x3, starting transfers between devices: 21 us -> 31.8 us  [block(): lax.ppermute(a, 'zb', [(i, (i + k) % EXPERTS) for i in range(EXPERTS)])]
    ppermute x9, waiting for transfers between devices: 6.07 us -> 12 us  [line(): return lax.ppermute(a, 'zo', pairs)]
    ppermute x4, waiting for transfers between devices: 5.78 us -> 0.01 us  [across(): return lax.ppermute(a, 'yh', [(0, 1), (1, 0)])]
  transfers between devices with their start and end apart: 27 -> 27, of which waited for: 12 -> 11; matrix products, arithmetic and copies ran while one was open for 10% -> 10% of each run, Pallas kernels for 4% -> 4%
where the time goes in v8:
time: 235 us; the launch traced here: 233 us
  starting transfers between devices  112 us (48%)
  waiting for transfers between devices  82 us (35%)
  matrix products  10.4 us (4%)
  local copies, waits for them, and re-layouts  9.72 us (4%)
  Pallas kernels  9.48 us (4%)
  other arithmetic  8.42 us (4%)
    all_to_all x2, waiting for transfers between devices, to_blocks(): units = lax.all_to_all(dispatch(a), 'zb', 0, 0, tiled=True)  44 us
    ppermute x3, starting transfers between devices, block(): lax.ppermute(a, 'zb', [(i, (i + k) % EXPERTS) for i in range(EXPERTS)])  31.8 us
    ppermute x9, starting transfers between devices, line(): return lax.ppermute(a, 'zo', pairs)  19.2 us
    all_to_all x2, starting transfers between devices, to_blocks(): units = lax.all_to_all(dispatch(a), 'zb', 0, 0, tiled=True)  18.6 us
    ppermute x4, waiting for transfers between devices, down(): lax.ppermute(a, ('zb', 'zo'), [((i + 1) % RING, i) for i in range(RING)])  17.2 us
    ppermute x4, starting transfers between devices, down(): lax.ppermute(a, ('zb', 'zo'), [((i + 1) % RING, i) for i in range(RING)])  15 us
    ppermute x4, starting transfers between devices, across(): return lax.ppermute(a, 'yh', [(0, 1), (1, 0)])  14.7 us
    ppermute x9, waiting for transfers between devices, line(): return lax.ppermute(a, 'zo', pairs)  12 us
  transfers between devices with their start and end apart: 27, of which 11 were waited for; matrix products, arithmetic and copies ran while one was open for 10% of the time, Pallas kernels for 4%

profile of v8, /device:TPU:6, one launch (start us, length us, event | category | flops | bytes accessed | tf_op | source)
XLA Modules:
  0.0 233.5 jit_solution(13858606635892910491)
XLA Ops:
  3.6 15.1 %all-to-all-start = ((bf16[4,36,2048]{2,1,0:T(8,128)(2,1)}), bf16[4,36,2048]{2,1,0:T(8,128)(2,1)S(1)}, u32[]{:S(2)}, u32[]{:S(2)}) async-start(bf16[4,36,2048]{2,1,0:T(8,128)(2,1)} %reshape.163), calls=%async_computation | async-start | bytes 1310720 | tf_op jit(solution)/shard_map/all_to_all | solution.py:152
  18.6 5.1 %collective-permute-start.1 = (bf16[2048,256]{1,0:T(8,128)(2,1)}, bf16[2048,256]{1,0:T(8,128)(2,1)}, u32[]{:S(2)}, u32[]{:S(2)}) collective-permute-start(bf16[2048,256]{1,0:T(8,128)(2,1)} %bitcast.3), channel_id=1, source_target_pairs={{0,1},{1,0},{2,3},{3,2},{4,5},{5,4},{6,7},{7,6},{8,9},{9,8},{10,11... | collective-permute-start | bytes 3145736 | tf_op jit(solution)/shard_map/ppermute | solution.py:37
  23.8 1.9 collective-permute-start
  25.7 2.2 collective-permute-start.4
  28.0 4.3 %collective-permute-done = bf16[128,2048]{1,0:T(8,128)(2,1)S(1)} collective-permute-done((bf16[128,2048]{1,0:T(8,128)(2,1)S(1)}, bf16[128,2048]{1,0:T(8,128)(2,1)S(1)}, u32[]{:S(2)}, u32[]{:S(2)}) %collective-permute-start) | collective-permute-done | bytes 524320 | tf_op jit(solution)/shard_map/ppermute | solution.py:112
  33.7 22.8 %all-to-all-done = bf16[4,36,2048]{2,1,0:T(8,128)(2,1)S(1)} async-done(((bf16[4,36,2048]{2,1,0:T(8,128)(2,1)}), bf16[4,36,2048]{2,1,0:T(8,128)(2,1)S(1)}, u32[]{:S(2)}, u32[]{:S(2)}) %all-to-all-start) | async-done | bytes 589856 | tf_op jit(solution)/shard_map/all_to_all | solution.py:152
  56.5 3.5 %all-to-all-start.1 = ((bf16[4,36,2048]{2,1,0:T(8,128)(2,1)}), bf16[4,36,2048]{2,1,0:T(8,128)(2,1)S(1)}, u32[]{:S(2)}, u32[]{:S(2)}) async-start(bf16[4,36,2048]{2,1,0:T(8,128)(2,1)} %reshape.165), calls=%async_computation.1 | async-start | bytes 1310720 | tf_op jit(solution)/shard_map/all_to_all | solution.py:152
  60.1 2.2 fusion.40
  63.9 2.2 collective-permute-start.2
  66.1 6.3 %collective-permute-start.3 = (bf16[144,2048]{1,0:T(8,128)(2,1)}, bf16[144,2048]{1,0:T(8,128)(2,1)}, u32[]{:S(2)}, u32[]{:S(2)}) collective-permute-start(bf16[144,2048]{1,0:T(8,128)(2,1)} %reshape.164), channel_id=1, source_target_pairs={{2,0},{4,2},{6,4},{8,6},{10,8},{12,10},{14,12},{16,14},{18,16},{20... | collective-permute-start | bytes 1769480 | tf_op jit(solution)/shard_map/ppermute | solution.py:29
  73.9 21.2 %all-to-all-done.1 = bf16[4,36,2048]{2,1,0:T(8,128)(2,1)S(1)} async-done(((bf16[4,36,2048]{2,1,0:T(8,128)(2,1)}), bf16[4,36,2048]{2,1,0:T(8,128)(2,1)S(1)}, u32[]{:S(2)}, u32[]{:S(2)}) %all-to-all-start.1) | async-done | bytes 589856 | tf_op jit(solution)/shard_map/all_to_all | solution.py:152
  97.8 2.4 %collective-permute-start.7 = (bf16[144,2048]{1,0:T(8,128)(2,1)S(1)}, bf16[144,2048]{1,0:T(8,128)(2,1)S(1)}, u32[]{:S(2)}, u32[]{:S(2)}) collective-permute-start(bf16[144,2048]{1,0:T(8,128)(2,1)S(1)} %reshape.166.g_ref), channel_id=1, source_target_pairs={{2,0},{4,2},{6,4},{8,6},{10,8},{12,10},{14,12},{16,14},{18,16},{20... | collective-permute-start | bytes 1769480 | tf_op jit(solution)/shard_map/ppermute | solution.py:29
  100.2 3.5 %collective-permute-start.8 = (bf16[144,2048]{1,0:T(8,128)(2,1)S(1)}, bf16[144,2048]{1,0:T(8,128)(2,1)S(1)}, u32[]{:S(2)}, u32[]{:S(2)}) collective-permute-start(bf16[144,2048]{1,0:T(8,128)(2,1)S(1)} %reshape.166.g_ref), channel_id=1, source_target_pairs={{0,2},{2,4},{4,6},{6,8},{8,10},{10,12},{12,14},{14,16},{16,18},{18... | collective-permute-start | bytes 1769480 | tf_op jit(solution)/shard_map/ppermute | solution.py:25
  106.3 3.6 %collective-permute-start.5 = (bf16[144,2048]{1,0:T(8,128)(2,1)}, bf16[144,2048]{1,0:T(8,128)(2,1)S(1)}, u32[]{:S(2)}, u32[]{:S(2)}) collective-permute-start(bf16[144,2048]{1,0:T(8,128)(2,1)} %collective-permute-done.3), channel_id=1, source_target_pairs={{2,0},{4,2},{6,4},{8,6},{10,8},{12,10},{14,12},{16,14},{18,16},{20... | collective-permute-start | bytes 1769480 | tf_op jit(solution)/shard_map/ppermute | solution.py:29
  109.9 2.3 collective-permute-start.6
  113.7 2.2 collective-permute-done.7
  116.0 2.8 %collective-permute-start.11 = (bf16[144,2048]{1,0:T(8,128)(2,1)S(1)}, bf16[144,2048]{1,0:T(8,128)(2,1)S(1)}, u32[]{:S(2)}, u32[]{:S(2)}) collective-permute-start(bf16[144,2048]{1,0:T(8,128)(2,1)S(1)} %collective-permute-done.7), channel_id=1, source_target_pairs={{2,0},{4,2},{6,4},{8,6},{10,8},{12,10},{14,12},{16,14},{18,16},{20... | collective-permute-start | bytes 1769480 | tf_op jit(solution)/shard_map/ppermute | solution.py:29
  118.8 3.0 %collective-permute-start.12 = (bf16[144,2048]{1,0:T(8,128)(2,1)S(1)}, bf16[144,2048]{1,0:T(8,128)(2,1)S(1)}, u32[]{:S(2)}, u32[]{:S(2)}) collective-permute-start(bf16[144,2048]{1,0:T(8,128)(2,1)S(1)} %collective-permute-done.8), channel_id=1, source_target_pairs={{0,2},{2,4},{4,6},{6,8},{8,10},{10,12},{12,14},{14,16},{16,18},{18... | collective-permute-start | bytes 1769480 | tf_op jit(solution)/shard_map/ppermute | solution.py:25
  121.9 6.7 %collective-permute-done.5 = bf16[144,2048]{1,0:T(8,128)(2,1)S(1)} collective-permute-done((bf16[144,2048]{1,0:T(8,128)(2,1)}, bf16[144,2048]{1,0:T(8,128)(2,1)S(1)}, u32[]{:S(2)}, u32[]{:S(2)}) %collective-permute-start.5) | collective-permute-done | bytes 589856 | tf_op jit(solution)/shard_map/ppermute | solution.py:29
  133.0 8.2 %collective-permute-done.11 = bf16[144,2048]{1,0:T(8,128)(2,1)S(1)} collective-permute-done((bf16[144,2048]{1,0:T(8,128)(2,1)S(1)}, bf16[144,2048]{1,0:T(8,128)(2,1)S(1)}, u32[]{:S(2)}, u32[]{:S(2)}) %collective-permute-start.11) | collective-permute-done | bytes 589856 | tf_op jit(solution)/shard_map/ppermute | solution.py:29
  147.4 5.4 %collective-permute-done.9 = bf16[144,2048]{1,0:T(8,128)(2,1)S(1)} collective-permute-done((bf16[144,2048]{1,0:T(8,128)(2,1)S(1)}, bf16[144,2048]{1,0:T(8,128)(2,1)S(1)}, u32[]{:S(2)}, u32[]{:S(2)}) %collective-permute-start.9) | collective-permute-done | bytes 589856 | tf_op jit(solution)/shard_map/ppermute | solution.py:33
  154.2 1.9 shard_map.94
  159.0 4.0 %collective-permute-start.15 = (bf16[160,2048]{1,0:T(8,128)(2,1)S(1)}, bf16[160,2048]{1,0:T(8,128)(2,1)S(1)}, u32[]{:S(2)}, u32[]{:S(2)}) collective-permute-start(bf16[160,2048]{1,0:T(8,128)(2,1)S(1)} %get-tuple-element.81), channel_id=1, source_target_pairs={{0,2},{2,4},{4,6},{1,3},{3,5},{5,7},{8,10},{10,12},{12,14},{9,11},... | collective-permute-start | bytes 1966088 | tf_op jit(solution)/shard_map/ppermute | solution.py:33
  166.5 1.9 shard_map.97
  169.1 5.1 %collective-permute-start.24 = (bf16[128,2048]{1,0:T(8,128)(2,1)S(1)}, bf16[128,2048]{1,0:T(8,128)(2,1)S(1)}, u32[]{:S(2)}, u32[]{:S(2)}) collective-permute-start(bf16[128,2048]{1,0:T(8,128)(2,1)S(1)} %convolution_convert_fusion.3), channel_id=1, source_target_pairs={{0,1},{1,0},{2,3},{3,2},{4,5},{5,4},{6,7},{7,6},{8,9},{9,8},{10,11... | collective-permute-start | bytes 1572872 | tf_op jit(solution)/shard_map/ppermute | solution.py:37
  174.2 7.5 %collective-permute-start.19 = (bf16[160,2048]{1,0:T(8,128)(2,1)S(1)}, bf16[160,2048]{1,0:T(8,128)(2,1)S(1)}, u32[]{:S(2)}, u32[]{:S(2)}) collective-permute-start(bf16[160,2048]{1,0:T(8,128)(2,1)S(1)} %get-tuple-element.61), channel_id=1, source_target_pairs={{0,6},{6,0},{1,7},{7,1},{8,14},{14,8},{9,15},{15,9},{16,22},{22,16... | collective-permute-start | bytes 1966088 | tf_op jit(solution)/shard_map/ppermute | solution.py:33
  183.9 2.3 collective-permute-start.23
  186.1 6.5 %collective-permute-done.19 = bf16[160,2048]{1,0:T(8,128)(2,1)S(1)} collective-permute-done((bf16[160,2048]{1,0:T(8,128)(2,1)S(1)}, bf16[160,2048]{1,0:T(8,128)(2,1)S(1)}, u32[]{:S(2)}, u32[]{:S(2)}) %collective-permute-start.19) | collective-permute-done | bytes 655392 | tf_op jit(solution)/shard_map/ppermute | solution.py:33
  193.2 8.3 %collective-permute-start.20 = (bf16[40,2048]{1,0:T(8,128)(2,1)S(1)}, bf16[40,2048]{1,0:T(8,128)(2,1)S(1)}, u32[]{:S(2)}, u32[]{:S(2)}) collective-permute-start(bf16[40,2048]{1,0:T(8,128)(2,1)S(1)} %get-tuple-element.93), channel_id=1, source_target_pairs={{0,24},{8,0},{16,8},{24,16},{1,25},{9,1},{17,9},{25,17},{2,26},{10... | collective-permute-start | bytes 491528 | tf_op jit(solution)/shard_map/ppermute | solution.py:133
  201.5 15.7 %collective-permute-start.21 = (bf16[40,2048]{1,0:T(8,128)(2,1)S(1)}, bf16[40,2048]{1,0:T(8,128)(2,1)S(1)}, u32[]{:S(2)}, u32[]{:S(2)}) collective-permute-start(bf16[40,2048]{1,0:T(8,128)(2,1)S(1)} %get-tuple-element.92), channel_id=1, source_target_pairs={{0,16},{8,24},{16,0},{24,8},{1,17},{9,25},{17,1},{25,9},{2,18},{10... | collective-permute-start | bytes 491528 | tf_op jit(solution)/shard_map/ppermute | solution.py:133
  217.2 7.8 %collective-permute-start.22 = (bf16[40,2048]{1,0:T(8,128)(2,1)S(1)}, bf16[40,2048]{1,0:T(8,128)(2,1)S(1)}, u32[]{:S(2)}, u32[]{:S(2)}) collective-permute-start(bf16[40,2048]{1,0:T(8,128)(2,1)S(1)} %get-tuple-element.91), channel_id=1, source_target_pairs={{0,8},{8,16},{16,24},{24,0},{1,9},{9,17},{17,25},{25,1},{2,10},{10... | collective-permute-start | bytes 491528 | tf_op jit(solution)/shard_map/ppermute | solution.py:133
  226.5 2.6 %collective-permute-done.21 = bf16[40,2048]{1,0:T(8,128)(2,1)S(1)} collective-permute-done((bf16[40,2048]{1,0:T(8,128)(2,1)S(1)}, bf16[40,2048]{1,0:T(8,128)(2,1)S(1)}, u32[]{:S(2)}, u32[]{:S(2)}) %collective-permute-start.21) | collective-permute-done | bytes 163872 | tf_op jit(solution)/shard_map/ppermute | solution.py:133
  (94 shorter events, 41.6 us)
Async XLA Ops:
  0.6 27.4 %copy-start.5 = (s32[128,1]{0,1:T(1,128)S(1)}, s32[128,1]{0,1:T(1,128)}, u32[]{:S(2)}) copy-start(s32[128,1]{0,1:T(1,128)} %param.8) | copy-start | bytes 1540
  0.7 23.1 %copy-start.6 = (bf16[128,2048]{1,0:T(8,128)(2,1)S(1)}, bf16[128,2048]{1,0:T(8,128)(2,1)}, u32[]{:S(2)}) copy-start(bf16[128,2048]{1,0:T(8,128)(2,1)} %param.7) | copy-start | bytes 1572868
  0.7 27.3 %copy-start.7 = (bf16[128,1]{0,1:T(2,128)(2,1)S(1)}, bf16[128,1]{0,1:T(2,128)(2,1)}, u32[]{:S(2)}) copy-start(bf16[128,1]{0,1:T(2,128)(2,1)} %param.9) | copy-start | bytes 772
  3.6 52.9 %all-to-all-start = ((bf16[4,36,2048]{2,1,0:T(8,128)(2,1)}), bf16[4,36,2048]{2,1,0:T(8,128)(2,1)S(1)}, u32[]{:S(2)}, u32[]{:S(2)}) async-start(bf16[4,36,2048]{2,1,0:T(8,128)(2,1)} %reshape.163), calls=%async_computation | async-start | bytes 1310720 | tf_op jit(solution)/shard_map/all_to_all | solution.py:152
  18.6 45.3 %collective-permute-start.1 = (bf16[2048,256]{1,0:T(8,128)(2,1)}, bf16[2048,256]{1,0:T(8,128)(2,1)}, u32[]{:S(2)}, u32[]{:S(2)}) collective-permute-start(bf16[2048,256]{1,0:T(8,128)(2,1)} %bitcast.3), channel_id=1, source_target_pairs={{0,1},{1,0},{2,3},{3,2},{4,5},{5,4},{6,7},{7,6},{8,9},{9,8},{10,11... | collective-permute-start | bytes 3145736 | tf_op jit(solution)/shard_map/ppermute | solution.py:37
  23.8 8.6 %collective-permute-start = (bf16[128,2048]{1,0:T(8,128)(2,1)S(1)}, bf16[128,2048]{1,0:T(8,128)(2,1)S(1)}, u32[]{:S(2)}, u32[]{:S(2)}) collective-permute-start(bf16[128,2048]{1,0:T(8,128)(2,1)S(1)} %copy-done.6), channel_id=1, source_target_pairs={{0,480},{32,0},{64,32},{96,64},{128,96},{160,128},{192,160},{224,1... | collective-permute-start | bytes 1572872 | tf_op jit(solution)/shard_map/ppermute | solution.py:112
  25.7 72.1 %collective-permute-start.4 = (bf16[128,2048]{1,0:T(8,128)(2,1)}, bf16[128,2048]{1,0:T(8,128)(2,1)}, u32[]{:S(2)}, u32[]{:S(2)}) collective-permute-start(bf16[128,2048]{1,0:T(8,128)(2,1)} %bitcast.5), channel_id=1, source_target_pairs={{0,1},{1,0},{2,3},{3,2},{4,5},{5,4},{6,7},{7,6},{8,9},{9,8},{10,11... | collective-permute-start | bytes 1572872 | tf_op jit(solution)/shard_map/ppermute | solution.py:37
  32.4 27.8 %copy-start.1 = (bf16[128,2048]{1,0:T(8,128)(2,1)}, bf16[128,2048]{1,0:T(8,128)(2,1)S(1)}, u32[]{:S(2)}) copy-start(bf16[128,2048]{1,0:T(8,128)(2,1)S(1)} %collective-permute-done) | copy-start | bytes 1572868
  56.5 38.6 %all-to-all-start.1 = ((bf16[4,36,2048]{2,1,0:T(8,128)(2,1)}), bf16[4,36,2048]{2,1,0:T(8,128)(2,1)S(1)}, u32[]{:S(2)}, u32[]{:S(2)}) async-start(bf16[4,36,2048]{2,1,0:T(8,128)(2,1)} %reshape.165), calls=%async_computation.1 | async-start | bytes 1310720 | tf_op jit(solution)/shard_map/all_to_all | solution.py:152
  63.9 9.8 %copy-start.4 = (bf16[2048,128]{1,0:T(8,128)(2,1)S(1)}, bf16[2048,128]{1,0:T(8,128)(2,1)}, u32[]{:S(2)}) copy-start(bf16[2048,128]{1,0:T(8,128)(2,1)} %get-tuple-element.87) | copy-start | bytes 1572868
  63.9 41.0 %collective-permute-start.2 = (bf16[144,2048]{1,0:T(8,128)(2,1)}, bf16[144,2048]{1,0:T(8,128)(2,1)}, u32[]{:S(2)}, u32[]{:S(2)}) collective-permute-start(bf16[144,2048]{1,0:T(8,128)(2,1)} %reshape.164), channel_id=1, source_target_pairs={{0,2},{2,4},{4,6},{6,8},{8,10},{10,12},{12,14},{14,16},{16,18},{18... | collective-permute-start | bytes 1769480 | tf_op jit(solution)/shard_map/ppermute | solution.py:25
  66.1 38.9 %collective-permute-start.3 = (bf16[144,2048]{1,0:T(8,128)(2,1)}, bf16[144,2048]{1,0:T(8,128)(2,1)}, u32[]{:S(2)}, u32[]{:S(2)}) collective-permute-start(bf16[144,2048]{1,0:T(8,128)(2,1)} %reshape.164), channel_id=1, source_target_pairs={{2,0},{4,2},{6,4},{8,6},{10,8},{12,10},{14,12},{16,14},{18,16},{20... | collective-permute-start | bytes 1769480 | tf_op jit(solution)/shard_map/ppermute | solution.py:29
  97.8 18.2 %collective-permute-start.7 = (bf16[144,2048]{1,0:T(8,128)(2,1)S(1)}, bf16[144,2048]{1,0:T(8,128)(2,1)S(1)}, u32[]{:S(2)}, u32[]{:S(2)}) collective-permute-start(bf16[144,2048]{1,0:T(8,128)(2,1)S(1)} %reshape.166.g_ref), channel_id=1, source_target_pairs={{2,0},{4,2},{6,4},{8,6},{10,8},{12,10},{14,12},{16,14},{18,16},{20... | collective-permute-start | bytes 1769480 | tf_op jit(solution)/shard_map/ppermute | solution.py:29
  100.2 18.6 %collective-permute-start.8 = (bf16[144,2048]{1,0:T(8,128)(2,1)S(1)}, bf16[144,2048]{1,0:T(8,128)(2,1)S(1)}, u32[]{:S(2)}, u32[]{:S(2)}) collective-permute-start(bf16[144,2048]{1,0:T(8,128)(2,1)S(1)} %reshape.166.g_ref), channel_id=1, source_target_pairs={{0,2},{2,4},{4,6},{6,8},{8,10},{10,12},{12,14},{14,16},{16,18},{18... | collective-permute-start | bytes 1769480 | tf_op jit(solution)/shard_map/ppermute | solution.py:25
  106.3 22.3 %collective-permute-start.5 = (bf16[144,2048]{1,0:T(8,128)(2,1)}, bf16[144,2048]{1,0:T(8,128)(2,1)S(1)}, u32[]{:S(2)}, u32[]{:S(2)}) collective-permute-start(bf16[144,2048]{1,0:T(8,128)(2,1)} %collective-permute-done.3), channel_id=1, source_target_pairs={{2,0},{4,2},{6,4},{8,6},{10,8},{12,10},{14,12},{16,14},{18,16},{20... | collective-permute-start | bytes 1769480 | tf_op jit(solution)/shard_map/ppermute | solution.py:29
  109.9 19.6 %collective-permute-start.6 = (bf16[144,2048]{1,0:T(8,128)(2,1)}, bf16[144,2048]{1,0:T(8,128)(2,1)S(1)}, u32[]{:S(2)}, u32[]{:S(2)}) collective-permute-start(bf16[144,2048]{1,0:T(8,128)(2,1)} %collective-permute-done.2), channel_id=1, source_target_pairs={{0,2},{2,4},{4,6},{6,8},{8,10},{10,12},{12,14},{14,16},{16,18},{18... | collective-permute-start | bytes 1769480 | tf_op jit(solution)/shard_map/ppermute | solution.py:25
  116.0 25.3 %collective-permute-start.11 = (bf16[144,2048]{1,0:T(8,128)(2,1)S(1)}, bf16[144,2048]{1,0:T(8,128)(2,1)S(1)}, u32[]{:S(2)}, u32[]{:S(2)}) collective-permute-start(bf16[144,2048]{1,0:T(8,128)(2,1)S(1)} %collective-permute-done.7), channel_id=1, source_target_pairs={{2,0},{4,2},{6,4},{8,6},{10,8},{12,10},{14,12},{16,14},{18,16},{20... | collective-permute-start | bytes 1769480 | tf_op jit(solution)/shard_map/ppermute | solution.py:29
  118.8 22.5 %collective-permute-start.12 = (bf16[144,2048]{1,0:T(8,128)(2,1)S(1)}, bf16[144,2048]{1,0:T(8,128)(2,1)S(1)}, u32[]{:S(2)}, u32[]{:S(2)}) collective-permute-start(bf16[144,2048]{1,0:T(8,128)(2,1)S(1)} %collective-permute-done.8), channel_id=1, source_target_pairs={{0,2},{2,4},{4,6},{6,8},{8,10},{10,12},{12,14},{14,16},{16,18},{18... | collective-permute-start | bytes 1769480 | tf_op jit(solution)/shard_map/ppermute | solution.py:25
  130.0 16.1 %collective-permute-start.10 = (bf16[144,2048]{1,0:T(8,128)(2,1)S(1)}, bf16[144,2048]{1,0:T(8,128)(2,1)S(1)}, u32[]{:S(2)}, u32[]{:S(2)}) collective-permute-start(bf16[144,2048]{1,0:T(8,128)(2,1)S(1)} %collective-permute-done.6), channel_id=1, source_target_pairs={{4,6},{5,7},{12,14},{13,15},{20,22},{21,23},{28,30},{29,31},{36,38... | collective-permute-start | bytes 1769480 | tf_op jit(solution)/shard_map/ppermute | solution.py:33
  130.7 22.1 %collective-permute-start.9 = (bf16[144,2048]{1,0:T(8,128)(2,1)S(1)}, bf16[144,2048]{1,0:T(8,128)(2,1)S(1)}, u32[]{:S(2)}, u32[]{:S(2)}) collective-permute-start(bf16[144,2048]{1,0:T(8,128)(2,1)S(1)} %collective-permute-done.5), channel_id=1, source_target_pairs={{2,0},{3,1},{10,8},{11,9},{18,16},{19,17},{26,24},{27,25},{34,32},... | collective-permute-start | bytes 1769480 | tf_op jit(solution)/shard_map/ppermute | solution.py:33
  143.2 15.3 %collective-permute-start.13 = (bf16[160,2048]{1,0:T(8,128)(2,1)S(1)}, bf16[160,2048]{1,0:T(8,128)(2,1)S(1)}, u32[]{:S(2)}, u32[]{:S(2)}) collective-permute-start(bf16[160,2048]{1,0:T(8,128)(2,1)S(1)} %get-tuple-element.56), channel_id=1, source_target_pairs={{0,2},{2,4},{1,3},{3,5},{8,10},{10,12},{9,11},{11,13},{16,18},{18,... | collective-permute-start | bytes 1966088 | tf_op jit(solution)/shard_map/ppermute | solution.py:33
  144.7 13.8 %collective-permute-start.14 = (bf16[160,2048]{1,0:T(8,128)(2,1)S(1)}, bf16[160,2048]{1,0:T(8,128)(2,1)S(1)}, u32[]{:S(2)}, u32[]{:S(2)}) collective-permute-start(bf16[160,2048]{1,0:T(8,128)(2,1)S(1)} %get-tuple-element.56), channel_id=1, source_target_pairs={{6,4},{4,2},{7,5},{5,3},{14,12},{12,10},{15,13},{13,11},{22,20},{2... | collective-permute-start | bytes 1966088 | tf_op jit(solution)/shard_map/ppermute | solution.py:33
  145.4 19.1 %collective-permute-start.18 = (bf16[144,2048]{1,0:T(8,128)(2,1)S(1)}, bf16[144,2048]{1,0:T(8,128)(2,1)S(1)}, u32[]{:S(2)}, u32[]{:S(2)}) collective-permute-start(bf16[144,2048]{1,0:T(8,128)(2,1)S(1)} %collective-permute-done.12), channel_id=1, source_target_pairs={{4,6},{5,7},{12,14},{13,15},{20,22},{21,23},{28,30},{29,31},{36,38... | collective-permute-start | bytes 1769480 | tf_op jit(solution)/shard_map/ppermute | solution.py:33
  146.1 20.3 %collective-permute-start.17 = (bf16[144,2048]{1,0:T(8,128)(2,1)S(1)}, bf16[144,2048]{1,0:T(8,128)(2,1)S(1)}, u32[]{:S(2)}, u32[]{:S(2)}) collective-permute-start(bf16[144,2048]{1,0:T(8,128)(2,1)S(1)} %collective-permute-done.11), channel_id=1, source_target_pairs={{2,0},{3,1},{10,8},{11,9},{18,16},{19,17},{26,24},{27,25},{34,32},... | collective-permute-start | bytes 1769480 | tf_op jit(solution)/shard_map/ppermute | solution.py:33
  159.0 33.7 %collective-permute-start.15 = (bf16[160,2048]{1,0:T(8,128)(2,1)S(1)}, bf16[160,2048]{1,0:T(8,128)(2,1)S(1)}, u32[]{:S(2)}, u32[]{:S(2)}) collective-permute-start(bf16[160,2048]{1,0:T(8,128)(2,1)S(1)} %get-tuple-element.81), channel_id=1, source_target_pairs={{0,2},{2,4},{4,6},{1,3},{3,5},{5,7},{8,10},{10,12},{12,14},{9,11},... | collective-permute-start | bytes 1966088 | tf_op jit(solution)/shard_map/ppermute | solution.py:33
  163.0 29.7 %collective-permute-start.16 = (bf16[160,2048]{1,0:T(8,128)(2,1)S(1)}, bf16[160,2048]{1,0:T(8,128)(2,1)S(1)}, u32[]{:S(2)}, u32[]{:S(2)}) collective-permute-start(bf16[160,2048]{1,0:T(8,128)(2,1)S(1)} %get-tuple-element.80), channel_id=1, source_target_pairs={{6,4},{4,2},{2,0},{7,5},{5,3},{3,1},{14,12},{12,10},{10,8},{15,13}... | collective-permute-start | bytes 1966088 | tf_op jit(solution)/shard_map/ppermute | solution.py:33
  169.1 56.0 %collective-permute-start.24 = (bf16[128,2048]{1,0:T(8,128)(2,1)S(1)}, bf16[128,2048]{1,0:T(8,128)(2,1)S(1)}, u32[]{:S(2)}, u32[]{:S(2)}) collective-permute-start(bf16[128,2048]{1,0:T(8,128)(2,1)S(1)} %convolution_convert_fusion.3), channel_id=1, source_target_pairs={{0,1},{1,0},{2,3},{3,2},{4,5},{5,4},{6,7},{7,6},{8,9},{9,8},{10,11... | collective-permute-start | bytes 1572872 | tf_op jit(solution)/shard_map/ppermute | solution.py:37
  174.2 18.5 %collective-permute-start.19 = (bf16[160,2048]{1,0:T(8,128)(2,1)S(1)}, bf16[160,2048]{1,0:T(8,128)(2,1)S(1)}, u32[]{:S(2)}, u32[]{:S(2)}) collective-permute-start(bf16[160,2048]{1,0:T(8,128)(2,1)S(1)} %get-tuple-element.61), channel_id=1, source_target_pairs={{0,6},{6,0},{1,7},{7,1},{8,14},{14,8},{9,15},{15,9},{16,22},{22,16... | collective-permute-start | bytes 1966088 | tf_op jit(solution)/shard_map/ppermute | solution.py:33
  183.9 46.3 %collective-permute-start.23 = (bf16[2048,256]{1,0:T(8,128)(2,1)S(1)}, bf16[2048,256]{1,0:T(8,128)(2,1)S(1)}, u32[]{:S(2)}, u32[]{:S(2)}) collective-permute-start(bf16[2048,256]{1,0:T(8,128)(2,1)S(1)} %convolution_convert_fusion), channel_id=1, source_target_pairs={{0,1},{1,0},{2,3},{3,2},{4,5},{5,4},{6,7},{7,6},{8,9},{9,8},{10,11... | collective-permute-start | bytes 3145736 | tf_op jit(solution)/shard_map/ppermute | solution.py:37
  193.2 33.3 %collective-permute-start.20 = (bf16[40,2048]{1,0:T(8,128)(2,1)S(1)}, bf16[40,2048]{1,0:T(8,128)(2,1)S(1)}, u32[]{:S(2)}, u32[]{:S(2)}) collective-permute-start(bf16[40,2048]{1,0:T(8,128)(2,1)S(1)} %get-tuple-element.93), channel_id=1, source_target_pairs={{0,24},{8,0},{16,8},{24,16},{1,25},{9,1},{17,9},{25,17},{2,26},{10... | collective-permute-start | bytes 491528 | tf_op jit(solution)/shard_map/ppermute | solution.py:133
  201.5 27.5 %collective-permute-start.21 = (bf16[40,2048]{1,0:T(8,128)(2,1)S(1)}, bf16[40,2048]{1,0:T(8,128)(2,1)S(1)}, u32[]{:S(2)}, u32[]{:S(2)}) collective-permute-start(bf16[40,2048]{1,0:T(8,128)(2,1)S(1)} %get-tuple-element.92), channel_id=1, source_target_pairs={{0,16},{8,24},{16,0},{24,8},{1,17},{9,25},{17,1},{25,9},{2,18},{10... | collective-permute-start | bytes 491528 | tf_op jit(solution)/shard_map/ppermute | solution.py:133
  217.2 12.9 %collective-permute-start.22 = (bf16[40,2048]{1,0:T(8,128)(2,1)S(1)}, bf16[40,2048]{1,0:T(8,128)(2,1)S(1)}, u32[]{:S(2)}, u32[]{:S(2)}) collective-permute-start(bf16[40,2048]{1,0:T(8,128)(2,1)S(1)} %get-tuple-element.91), channel_id=1, source_target_pairs={{0,8},{8,16},{16,24},{24,0},{1,9},{9,17},{17,25},{25,1},{2,10},{10... | collective-permute-start | bytes 491528 | tf_op jit(solution)/shard_map/ppermute | solution.py:133
  (3 other events, 13.6 us)
